TPU v7x, 32 devices: a whole 2x2x4 slice. The times are simulated.
32 devices in a mesh: section: 2 (over x), dp: 16 (over z, y, core).
Axes of the slice: x: 2, y: 2, z: 4, core: 2. Of those that a mesh axis runs over, the one named last changes fastest.
Arguments:
- entering: bfloat16 [2, 2, 6144, 1280], P('section', None, 'dp'), may hold values from -6 to 6
- deal: int32 [2, 6144], P(None, 'dp'), may hold values from 0 to 6143, as said below
- seq_lens: int32 [2, 16, 3], P(None, 'dp'), may hold values from 1 to 256, 384 in all within a row
- mats: float32 [2, 7680, 1280], P('section', 'dp')
- gains: float32 [2, 2560], P('section', 'dp'), may hold values from 0.1 to 1.9
- biases: float32 [2, 2560], P('section', 'dp'), may hold values from -3 to 3
Outputs:
- results: bfloat16 [2, 2, 6144, 1280], P('section', None, 'dp')
- mats_grad: float32 [2, 7680, 1280], P('section', 'dp')
- gains_grad: float32 [2, 2560], P('section', 'dp')
- biases_grad: float32 [2, 2560], P('section', 'dp')
Inputs may be any that keep to these rules, and one draw needn't show every extreme that they name: `deal`: for each micro-batch a permutation of the rows; the dealt rows of each block of 384 take exactly 24 = 24 rows from each block of 384 arrival rows. `seq_lens`: each device's 3 lengths of a micro-batch sum to 384.
All inputs are finite; a program needn't handle non-finite values.
Results may differ from a plain program's by a relative error of at most 0.018.
Values may be sent and summed in bfloat16 or wider, within the bound.
A program may use at most 384 MiB of HBM per device.

v0:
```python
import jax
import jax.numpy as jnp
from jax import lax
from jax.sharding import PartitionSpec as P

HEADS = 16


EPS = 1e-06
NEG = -1000000000.0


def shifted(value, axis, steps):
    count = lax.axis_size(axis)
    initial, last = (max(0, -steps), min(count, count - steps))
    return lax.ppermute(value, axis, [(source, source + steps) for source in range(initial, last)])


def normed(value, gain):
    return value * lax.rsqrt(jnp.mean(value * value, axis=-1, keepdims=True) + EPS) * gain


def mul_plain(left, right):
    return jnp.dot(left, right, preferred_element_type=jnp.float32)


def mul_first_t(left, right):
    return lax.dot_general(
        left, right, (((0,), (0,)), ((), ())), preferred_element_type=jnp.float32
    )


def mul_second_t(left, right):
    return lax.dot_general(
        left, right, (((1,), (1,)), ((), ())), preferred_element_type=jnp.float32
    )


def unpack(gathered, model_width):
    full_mats, full_gains, full_biases = gathered
    section_mats = full_mats[0].reshape(6, model_width, model_width)
    gain_vals = full_gains[0].astype(jnp.float32).reshape(2, model_width)
    bias_vals = full_biases[0].astype(jnp.float32).reshape(2, model_width)
    return tuple((section_mats[index] for index in range(6))) + (
        gain_vals[0],
        gain_vals[1],
        bias_vals[0],
        bias_vals[1],
    )


def owner_split(d_mats, d_gains, d_biases, peer_count, model_width):
    return (
        d_mats.reshape(peer_count, 6 * model_width // peer_count, model_width),
        d_gains.reshape(peer_count, 2 * model_width // peer_count),
        d_biases.reshape(peer_count, 2 * model_width // peer_count),
    )


def owner_total(received):
    got_mats, got_gains, got_biases = received
    return (
        jnp.sum(got_mats, axis=0)[None],
        jnp.sum(got_gains, axis=0)[None],
        jnp.sum(got_biases, axis=0)[None],
    )


def forward_parts(inputs, segment, weights):
    w_query, w_key, w_value, w_mix, w_inner, w_outer, gain_one, gain_two, bias_inner, bias_outer = (
        weights
    )
    row_count, model_width = inputs.shape
    depth = model_width // HEADS
    scale = depth ** (-0.5)
    first = normed(inputs, gain_one).astype(jnp.bfloat16)
    query = mul_plain(first, w_query).astype(jnp.bfloat16)
    keys = mul_plain(first, w_key).astype(jnp.bfloat16)
    values = mul_plain(first, w_value).astype(jnp.bfloat16)
    query_h = query.reshape(row_count, HEADS, depth)
    keys_h = keys.reshape(row_count, HEADS, depth)
    values_h = values.reshape(row_count, HEADS, depth)
    scores = jnp.einsum("qhd,khd->hqk", query_h, keys_h, preferred_element_type=jnp.float32) * scale
    positions = jnp.arange(row_count, dtype=jnp.int32)
    allowed = (segment[:, None] == segment[None, :]) & (positions[None, :] <= positions[:, None])
    scores = jnp.where(allowed[None], scores, NEG)
    top_score = jnp.max(scores, axis=-1, keepdims=True)
    expd = jnp.exp(scores - top_score)
    soft = expd / jnp.sum(expd, axis=-1, keepdims=True)
    probs = soft.astype(jnp.bfloat16)
    attended = jnp.einsum("hqk,khd->qhd", probs, values_h, preferred_element_type=jnp.float32)
    attended = attended.reshape(row_count, model_width).astype(jnp.bfloat16)
    middle = inputs + mul_plain(attended, w_mix)
    second = normed(middle, gain_two).astype(jnp.bfloat16)
    inner = mul_plain(second, w_inner) + bias_inner
    active = jax.nn.gelu(inner, approximate=True).astype(jnp.bfloat16)
    output = middle + (mul_plain(active, w_outer) + bias_outer)
    saved = (first, query_h, keys_h, values_h, soft, probs, attended, middle, second, inner, active)
    return (output, saved)


def layer_backward(inputs, segment, weights, cotangent):
    w_query, w_key, w_value, w_mix, w_inner, w_outer, gain_one, gain_two, bias_inner, bias_outer = (
        weights
    )
    row_count, model_width = inputs.shape
    depth = model_width // HEADS
    scale = depth ** (-0.5)
    output, saved = forward_parts(inputs, segment, weights)
    first, query_h, keys_h, values_h, soft, probs, attended, middle, second, inner, active = saved
    grad_outer = cotangent.astype(jnp.bfloat16)
    d_bias_outer = jnp.sum(grad_outer.astype(jnp.float32), axis=0)
    d_w_outer = mul_first_t(active, grad_outer)
    d_active = mul_second_t(grad_outer, w_outer)
    gelu_value, gelu_back = jax.vjp(lambda pre_act: jax.nn.gelu(pre_act, approximate=True), inner)
    d_inner = gelu_back(d_active)[0].astype(jnp.bfloat16)
    d_bias_inner = jnp.sum(d_inner.astype(jnp.float32), axis=0)
    d_w_inner = mul_first_t(second, d_inner)
    d_second = mul_second_t(d_inner, w_inner)
    norm_value, norm_back = jax.vjp(normed, middle, gain_two)
    d_middle_norm, d_gain_two = norm_back(d_second)
    d_middle = cotangent + d_middle_norm
    d_branch = d_middle.astype(jnp.bfloat16)
    d_w_mix = mul_first_t(attended, d_branch)
    d_attended = mul_second_t(d_branch, w_mix).astype(jnp.bfloat16).reshape(row_count, HEADS, depth)
    d_probs = jnp.einsum("qhd,khd->hqk", d_attended, values_h, preferred_element_type=jnp.float32)
    d_values = jnp.einsum("hqk,qhd->khd", probs, d_attended, preferred_element_type=jnp.float32)
    d_values = d_values.reshape(row_count, model_width).astype(jnp.bfloat16)
    d_scores = (soft * (d_probs - jnp.sum(d_probs * soft, axis=-1, keepdims=True))).astype(
        jnp.bfloat16
    )
    d_query = (
        jnp.einsum("hqk,khd->qhd", d_scores, keys_h, preferred_element_type=jnp.float32) * scale
    )
    d_query = d_query.reshape(row_count, model_width).astype(jnp.bfloat16)
    d_keys = (
        jnp.einsum("hqk,qhd->khd", d_scores, query_h, preferred_element_type=jnp.float32) * scale
    )
    d_keys = d_keys.reshape(row_count, model_width).astype(jnp.bfloat16)
    d_w_query = mul_first_t(first, d_query)
    d_w_key = mul_first_t(first, d_keys)
    d_w_value = mul_first_t(first, d_values)
    d_first = (
        mul_second_t(d_query, w_query)
        + mul_second_t(d_keys, w_key)
        + mul_second_t(d_values, w_value)
    )
    first_value, first_back = jax.vjp(normed, inputs, gain_one)
    d_inputs_norm, d_gain_one = first_back(d_first)
    d_inputs = d_middle + d_inputs_norm
    d_mats = jnp.stack([d_w_query, d_w_key, d_w_value, d_w_mix, d_w_inner, d_w_outer])
    d_gains = jnp.stack([d_gain_one, d_gain_two])
    d_biases = jnp.stack([d_bias_inner, d_bias_outer])
    return (d_inputs, d_mats, d_gains, d_biases)


def local(entering, deal, seq_lens, mats, gains, biases):
    section_index = lax.axis_index("section")
    section_count = lax.axis_size("section")
    peer_count = lax.axis_size("dp")
    arrival = entering[0]
    batch_count, row_count, model_width = arrival.shape
    per_peer = row_count // peer_count
    positions = jnp.arange(row_count, dtype=jnp.int32)
    seg_ends = jnp.cumsum(seq_lens[:, 0, :], axis=-1)
    segments = jnp.sum(
        (positions[None, :, None] >= seg_ends[:, None, :]).astype(jnp.int32), axis=-1
    )
    scatter_ints = jax.vmap(
        lambda index_row, value_row: jnp.zeros((row_count,), jnp.int32).at[index_row].set(value_row)
    )
    source_dev = deal // row_count
    source_row = deal % row_count
    matches = (
        source_dev[:, :, None] == jnp.arange(peer_count, dtype=jnp.int32)[None, None, :]
    ).astype(jnp.int32)
    ranking = jnp.sum(jnp.cumsum(matches, axis=1) * matches, axis=-1) - 1
    slot_index = source_dev * per_peer + ranking
    request = scatter_ints(slot_index, source_row).reshape(batch_count, peer_count, per_peer)
    slot_owner = scatter_ints(slot_index, jnp.broadcast_to(positions, slot_index.shape))
    wanted = lax.all_to_all(request, "dp", split_axis=1, concat_axis=1, tiled=True).reshape(
        batch_count, row_count
    )
    outgoing = jnp.take_along_axis(arrival, wanted[:, :, None], axis=1)
    outgoing = outgoing.reshape(batch_count, peer_count, per_peer, model_width)
    arrived = lax.all_to_all(outgoing, "dp", split_axis=1, concat_axis=1, tiled=True).reshape(
        batch_count, row_count, model_width
    )
    dealt_rows = jnp.take_along_axis(arrived, slot_index[:, :, None], axis=1)
    weights_fwd = unpack(
        (
            lax.all_gather(mats.astype(jnp.bfloat16), "dp", axis=1, tiled=True),
            lax.all_gather(gains.astype(jnp.bfloat16), "dp", axis=1, tiled=True),
            lax.all_gather(biases.astype(jnp.bfloat16), "dp", axis=1, tiled=True),
        ),
        model_width,
    )
    tick_count = batch_count + section_count - 1
    zero_rows = jnp.zeros((row_count, model_width), jnp.bfloat16)
    received = zero_rows
    saved_inputs = []
    final_out = []
    for tick in range(tick_count):
        fresh = dealt_rows[tick] if tick < batch_count else zero_rows
        batch_now = jnp.clip(tick - section_index, 0, batch_count - 1)
        layer_in = jnp.where(section_index == 0, fresh, received)
        layer_out = forward_parts(layer_in.astype(jnp.float32), segments[batch_now], weights_fwd)[0]
        saved_inputs.append(layer_in)
        final_out.append(layer_out.astype(jnp.bfloat16))
        if tick + 1 < tick_count:
            received = shifted(final_out[-1], "section", 1)
    weights_bwd = unpack(
        (
            lax.all_gather(mats.astype(jnp.bfloat16), "dp", axis=1, tiled=True),
            lax.all_gather(gains.astype(jnp.bfloat16), "dp", axis=1, tiled=True),
            lax.all_gather(biases.astype(jnp.bfloat16), "dp", axis=1, tiled=True),
        ),
        model_width,
    )
    saved_stack = jnp.stack(saved_inputs)
    incoming = zero_rows
    input_grads = []
    total_mats = jnp.zeros((6, model_width, model_width), jnp.float32)
    total_gains = jnp.zeros((2, model_width), jnp.float32)
    total_biases = jnp.zeros((2, model_width), jnp.float32)
    for tick in range(tick_count):
        fresh = dealt_rows[tick] if tick < batch_count else zero_rows
        cot_now = jnp.where(section_index == section_count - 1, fresh, incoming).astype(jnp.float32)
        fwd_tick = jnp.clip(tick - section_count + 1 + 2 * section_index, 0, tick_count - 1)
        batch_now = jnp.clip(tick - (section_count - 1 - section_index), 0, batch_count - 1)
        layer_in = saved_stack[fwd_tick].astype(jnp.float32)
        d_inputs, d_mats, d_gains, d_biases = layer_backward(
            layer_in, segments[batch_now], weights_bwd, cot_now
        )
        d_low = d_inputs.astype(jnp.bfloat16)
        input_grads.append(d_low)
        if tick + 1 < tick_count:
            incoming = shifted(d_low, "section", -1)
        total_mats = total_mats + d_mats
        total_gains = total_gains + d_gains
        total_biases = total_biases + d_biases
    split_mats, split_gains, split_biases = owner_split(
        total_mats, total_gains, total_biases, peer_count, model_width
    )
    shard_mats, shard_gains, shard_biases = owner_total(
        (
            lax.all_to_all(
                split_mats.astype(jnp.bfloat16), "dp", split_axis=0, concat_axis=0, tiled=True
            ).astype(split_mats.dtype),
            lax.all_to_all(
                split_gains.astype(jnp.bfloat16), "dp", split_axis=0, concat_axis=0, tiled=True
            ).astype(split_gains.dtype),
            lax.all_to_all(
                split_biases.astype(jnp.bfloat16), "dp", split_axis=0, concat_axis=0, tiled=True
            ).astype(split_biases.dtype),
        )
    )
    result_dealt = jnp.stack(
        [
            jnp.where(
                section_index == section_count - 1,
                final_out[batch + section_count - 1],
                input_grads[batch + section_count - 1],
            )
            for batch in range(batch_count)
        ]
    )
    going_back = jnp.take_along_axis(result_dealt, slot_owner[:, :, None], axis=1)
    going_back = going_back.reshape(batch_count, peer_count, per_peer, model_width)
    returned = lax.all_to_all(going_back, "dp", split_axis=1, concat_axis=1, tiled=True).reshape(
        batch_count, row_count, model_width
    )
    inverse = scatter_ints(wanted, jnp.broadcast_to(positions, wanted.shape))
    arrival_rows = jnp.take_along_axis(returned, inverse[:, :, None], axis=1)
    return (arrival_rows[None], shard_mats, shard_gains, shard_biases)


def solution(mesh):
    in_specs = (
        P("section", None, "dp", None),
        P(None, "dp"),
        P(None, "dp", None),
        P("section", "dp", None),
        P("section", "dp"),
        P("section", "dp"),
    )
    out_specs = (
        P("section", None, "dp", None),
        P("section", "dp", None),
        P("section", "dp"),
        P("section", "dp"),
    )
    return jax.shard_map(local, mesh=mesh, in_specs=in_specs, out_specs=out_specs, check_vma=False)
```

profile of v0, /device:TPU:17, one launch (start us, length us, event | category | flops | bytes accessed | tf_op | source)
XLA Modules:
  0.0 1310.1 jit_solution(2446857867919564608)
XLA Ops:
  12.4 36.3 %scatter_fusion = s32[2,384]{1,0:T(2,128)S(1)} fusion(s32[2,384]{1,0:T(2,128)S(1)} %broadcast.626.clone, s32[768]{0:T(1024)S(1)} %reshape.1071, s32[768]{0:T(1024)S(1)} %reshape.1073), kind=kCustom, calls=%fused_computation.4 | custom fusion | bytes 15360 | tf_op jit(solution)/shard_map/vmap()/scatter | solution.py:170
  48.8 10.5 all_to_all.32
  60.0 11.1 gather_fusion
  74.4 7.0 all-to-all-start.1
  83.2 100.6 %all-reduce.2 = (bf16[2560]{0:T(1024)(128)(2,1)S(1)}, bf16[2560]{0:T(1024)(128)(2,1)S(1)}) all-reduce(bf16[2560]{0:T(1024)(128)(2,1)S(1)} %dynamic-update-slice, bf16[2560]{0:T(1024)(128)(2,1)S(1)} %dynamic-update-slice.1), channel_id=1, replica_groups=mesh['section'=2,'dp'=16] {'dp'}, use_global_device_ids=true, to_apply=%add | all-reduce | flops 5120 | bytes 20480
  186.2 11.1 gather_fusion.1
  219.9 8.4 fusion.340
  238.0 8.0 fusion.54
  249.2 18.1 %collective-permute-done = bf16[384,1280]{1,0:T(8,128)(2,1)S(1)} collective-permute-done((bf16[384,1280]{1,0:T(8,128)(2,1)}, bf16[384,1280]{1,0:T(8,128)(2,1)S(1)}, u32[]{:S(2)}, u32[]{:S(2)}) %collective-permute-start) | collective-permute-done | bytes 983072 | tf_op jit(solution)/shard_map/ppermute | solution.py:16
  286.8 8.4 fusion.341
  304.6 8.1 fusion.55
  316.8 36.3 %scatter_fusion.1 = s32[2,384]{1,0:T(2,128)S(1)} fusion(s32[2,384]{1,0:T(2,128)S(1)} %broadcast.626.clone.1, s32[768]{0:T(1024)S(1)} %reshape.1071, s32[768]{0:T(1024)S(1)} %reshape.1079), kind=kCustom, calls=%fused_computation.5 | custom fusion | bytes 15360 | tf_op jit(solution)/shard_map/vmap()/scatter | solution.py:170
  374.0 5.9 fusion.342
  404.0 9.4 multiply_reduce_fusion.2
  413.4 10.3 multiply_convert_fusion.2
  429.6 5.9 fusion.163
  435.5 5.4 fusion.23
  467.1 8.1 fusion.343
  480.2 5.4 multiply_reduce_fusion.10
  506.1 6.3 fusion.22
  512.4 6.0 fusion.21
  527.8 8.3 fusion.345
  536.1 5.1 fusion.178
  541.3 6.0 multiply_reduce_fusion.8
  568.5 9.3 multiply_reduce_fusion.1
  577.8 10.3 multiply_convert_fusion.1
  594.0 5.9 fusion.169
  599.9 5.4 fusion.17
  632.4 6.3 fusion.16
  638.7 6.0 fusion.15
  654.0 5.8 fusion.344
  664.8 5.7 multiply_reduce_fusion.7
  691.1 9.5 multiply_reduce_fusion
  700.6 10.3 multiply_convert_fusion
  716.7 5.6 fusion.175
  722.4 5.4 fusion.11
  755.7 17.8 %all-to-all-start.4 = ((bf16[16,1,160]{2,1,0:T(2,128)(2,1)}), bf16[16,1,160]{2,1,0:T(2,128)(2,1)S(1)}, u32[]{:S(2)}, u32[]{:S(2)}) async-start(bf16[16,1,160]{2,1,0:T(2,128)(2,1)} %convert_element_type.666), calls=%async_computation.4 | async-start | bytes 32768 | tf_op jit(solution)/shard_map/all_to_all | solution.py:250
  773.6 9.6 fusion.185
  784.5 11.1 gather_fusion.2
  798.2 6.1 all-to-all-start.5
  804.3 6.6 fusion.6
  812.2 6.0 all-to-all-start.2
  818.3 43.0 %add_convert_fusion = bf16[6,1280,1280]{2,1,0:T(8,128)(2,1)} fusion(f32[6,1280,1280]{2,1,0:T(8,128)} %fusion.6, f32[6,1280,1280]{2,1,0:T(8,128)} %fusion.18, f32[6,1280,1280]{2,1,0:T(8,128)} %fusion.12), kind=kLoop, calls=%fused_computation.14 | loop fusion | flops 29491200 | bytes 137625600 | tf_op jit(solution)/shard_map/convert_element_type | solution.py:248
  863.9 5.5 all-to-all-start.3
  869.4 36.3 %scatter_fusion.2 = s32[2,384]{1,0:T(2,128)S(1)} fusion(s32[2,384]{1,0:T(2,128)S(1)} %broadcast.626.clone.2, s32[768]{0:T(1024)S(1)} %reshape.1083, s32[768]{0:T(1024)S(1)} %copy-done.58), kind=kCustom, calls=%fused_computation.6 | custom fusion | bytes 15360 | tf_op jit(solution)/shard_map/vmap()/scatter | solution.py:170
  908.7 11.1 gather_fusion.3
  922.8 370.5 %all-to-all-done.3 = bf16[16,480,1280]{2,1,0:T(8,128)(2,1)} async-done(((bf16[16,480,1280]{2,1,0:T(8,128)(2,1)}), bf16[16,480,1280]{2,1,0:T(8,128)(2,1)}, u32[]{:S(2)}, u32[]{:S(2)}) %all-to-all-start.3) | async-done | bytes 19660832 | tf_op jit(solution)/shard_map/all_to_all | solution.py:247
  1293.3 9.7 convert_reduce_fusion
  (429 shorter events, 329.0 us)
Async XLA Ops:
  7.2 52.9 %copy-start = (bf16[1,2,384,1280]{3,2,1,0:T(8,128)(2,1)S(1)}, bf16[1,2,384,1280]{3,2,1,0:T(8,128)(2,1)}, u32[]{:S(2)}) copy-start(bf16[1,2,384,1280]{3,2,1,0:T(8,128)(2,1)} %param.8) | copy-start | bytes 5898244
  7.2 192.3 %all-gather.2.cloned.1.call-start = ((), (), s32[]{:S(2)}) async-start(), calls=%async_computation.6 | async-start | bytes 20889600 | tf_op jit(solution)/shard_map/all_gather | solution.py:192
  74.4 109.4 %copy-start.69 = (s32[2,1,3]{2,1,0:T(1,128)S(1)}, s32[2,1,3]{2,1,0:T(1,128)}, u32[]{:S(2)}) copy-start(s32[2,1,3]{2,1,0:T(1,128)} %param.10) | copy-start | bytes 76
  74.4 110.2 %all-to-all-start.1 = ((bf16[2,16,24,1280]{3,2,0,1:T(8,128)(2,1)}), bf16[2,16,24,1280]{3,2,0,1:T(8,128)(2,1)}, u32[]{:S(2)}, u32[]{:S(2)}) async-start(bf16[2,16,24,1280]{3,2,0,1:T(8,128)(2,1)} %copy.194), calls=%async_computation.1 | async-start | bytes 3932160 | tf_op jit(solution)/shard_map/all_to_all | solution.py:186
  184.3 120.3 %copy-start.64 = (f32[1280]{0:T(1024)}, f32[1280]{0:T(1024)S(1)}, u32[]{:S(2)}) copy-start(f32[1280]{0:T(1024)S(1)} %get-tuple-element.22) | copy-start | bytes 15364
  199.1 68.2 %copy-start.10 = (bf16[2,384,1280]{2,1,0:T(8,128)(2,1)}, bf16[2,384,1280]{2,1,0:T(8,128)(2,1)S(1)}, u32[]{:S(2)}) copy-start(bf16[2,384,1280]{2,1,0:T(8,128)(2,1)S(1)} %broadcast_select_fusion.1) | copy-start | bytes 5898244
  246.0 21.2 %collective-permute-start = (bf16[384,1280]{1,0:T(8,128)(2,1)}, bf16[384,1280]{1,0:T(8,128)(2,1)S(1)}, u32[]{:S(2)}, u32[]{:S(2)}) collective-permute-start(bf16[384,1280]{1,0:T(8,128)(2,1)} %fusion.54), channel_id=1, source_target_pairs={{0,16},{1,17},{2,18},{3,19},{4,20},{5,21},{6,22},{7,23},{8,24},{9,... | collective-permute-start | bytes 2949128 | tf_op jit(solution)/shard_map/ppermute | solution.py:16
  312.7 42.7 %collective-permute-start.1 = (bf16[384,1280]{1,0:T(8,128)(2,1)}, bf16[384,1280]{1,0:T(8,128)(2,1)S(1)}, u32[]{:S(2)}, u32[]{:S(2)}) collective-permute-start(bf16[384,1280]{1,0:T(8,128)(2,1)} %fusion.55), channel_id=1, source_target_pairs={{0,16},{1,17},{2,18},{3,19},{4,20},{5,21},{6,22},{7,23},{8,24},{9,... | collective-permute-start | bytes 2949128 | tf_op jit(solution)/shard_map/ppermute | solution.py:16
  316.7 36.3 %copy-start.57 = (s32[768]{0:T(1024)}, s32[768]{0:T(1024)S(1)}, u32[]{:S(2)}) copy-start(s32[768]{0:T(1024)S(1)} %reshape.1079) | copy-start | bytes 9220
  363.0 17.0 %copy-start.48 = (bf16[384,1280]{0,1:T(8,128)(2,1)}, bf16[384,1280]{0,1:T(8,128)(2,1)S(1)}, u32[]{:S(2)}) copy-start(bf16[384,1280]{0,1:T(8,128)(2,1)S(1)} %copy.205) | copy-start | bytes 2949124
  379.9 9.9 slice-start
  379.9 9.9 slice-start.1
  380.0 9.9 slice-start.2
  380.0 10.2 slice-start.3
  429.5 14.9 %copy-start.32 = (bf16[16,80,384]{2,1,0:T(8,128)(2,1)}, bf16[16,80,384]{2,1,0:T(8,128)(2,1)S(1)}, u32[]{:S(2)}) copy-start(bf16[16,80,384]{2,1,0:T(8,128)(2,1)S(1)} %multiply_convert_fusion.13) | copy-start | bytes 2949124
  429.5 11.3 slice-start.5
  429.5 11.3 slice-start.6
  429.5 11.3 slice-start.7
  429.5 12.4 slice-start.8
  435.4 10.5 copy-start.52
  449.6 107.0 %collective-permute-start.2 = (bf16[384,1280]{1,0:T(8,128)(2,1)}, bf16[384,1280]{1,0:T(8,128)(2,1)}, u32[]{:S(2)}, u32[]{:S(2)}) collective-permute-start(bf16[384,1280]{1,0:T(8,128)(2,1)} %fusion.144), channel_id=1, source_target_pairs={{16,0},{17,1},{18,2},{19,3},{20,4},{21,5},{22,6},{23,7},{24,8},{25... | collective-permute-start | bytes 2949128 | tf_op jit(solution)/shard_map/ppermute | solution.py:16
  536.1 19.0 %slice-start.10 = ((s8[19660800]{0:T(1024)(128)(4,1)}), s8[4194304]{0:T(1024)(128)(4,1)S(1)}, s32[]{:S(2)}) async-start(s8[19660800]{0:T(1024)(128)(4,1)} %bitcast.625), calls=%async_computation.17 | async-start | bytes 8388608
  536.1 19.0 %slice-start.11 = ((s8[19660800]{0:T(1024)(128)(4,1)}), s8[4194304]{0:T(1024)(128)(4,1)S(1)}, s32[]{:S(2)}) async-start(s8[19660800]{0:T(1024)(128)(4,1)} %bitcast.625), calls=%async_computation.18 | async-start | bytes 8388608
  536.1 19.0 %slice-start.12 = ((s8[19660800]{0:T(1024)(128)(4,1)}), s8[4194304]{0:T(1024)(128)(4,1)S(1)}, s32[]{:S(2)}) async-start(s8[19660800]{0:T(1024)(128)(4,1)} %bitcast.625), calls=%async_computation.19 | async-start | bytes 8388608
  541.3 13.8 %slice-start.13 = ((s8[19660800]{0:T(1024)(128)(4,1)}), s8[4194304]{0:T(1024)(128)(4,1)S(1)}, s32[]{:S(2)}) async-start(s8[19660800]{0:T(1024)(128)(4,1)} %bitcast.625), calls=%async_computation.20 | async-start | bytes 8388608
  593.9 14.9 %copy-start.33 = (bf16[16,80,384]{2,1,0:T(8,128)(2,1)}, bf16[16,80,384]{2,1,0:T(8,128)(2,1)S(1)}, u32[]{:S(2)}) copy-start(bf16[16,80,384]{2,1,0:T(8,128)(2,1)S(1)} %multiply_convert_fusion.10) | copy-start | bytes 2949124
  593.9 11.3 slice-start.15
  593.9 11.3 slice-start.16
  594.0 11.3 slice-start.17
  594.0 12.4 slice-start.18
  599.8 10.5 copy-start.54
  615.0 61.9 %collective-permute-start.3 = (bf16[384,1280]{1,0:T(8,128)(2,1)}, bf16[384,1280]{1,0:T(8,128)(2,1)}, u32[]{:S(2)}, u32[]{:S(2)}) collective-permute-start(bf16[384,1280]{1,0:T(8,128)(2,1)} %get-tuple-element.34), channel_id=1, source_target_pairs={{16,0},{17,1},{18,2},{19,3},{20,4},{21,5},{22,6},{23,7},{24,8},{25... | collective-permute-start | bytes 2949128 | tf_op jit(solution)/shard_map/ppermute | solution.py:16
  659.9 15.4 %slice-start.20 = ((s8[19660800]{0:T(1024)(128)(4,1)}), s8[2883584]{0:T(1024)(128)(4,1)S(1)}, s32[]{:S(2)}) async-start(s8[19660800]{0:T(1024)(128)(4,1)} %bitcast.629), calls=%async_computation.27 | async-start | bytes 5767168
  659.9 15.4 %slice-start.21 = ((s8[19660800]{0:T(1024)(128)(4,1)}), s8[4194304]{0:T(1024)(128)(4,1)S(1)}, s32[]{:S(2)}) async-start(s8[19660800]{0:T(1024)(128)(4,1)} %bitcast.629), calls=%async_computation.28 | async-start | bytes 8388608
  659.9 15.4 %slice-start.22 = ((s8[19660800]{0:T(1024)(128)(4,1)}), s8[4194304]{0:T(1024)(128)(4,1)S(1)}, s32[]{:S(2)}) async-start(s8[19660800]{0:T(1024)(128)(4,1)} %bitcast.629), calls=%async_computation.29 | async-start | bytes 8388608
  664.7 10.5 slice-start.23
  716.7 11.1 slice-start.25
  716.7 11.1 slice-start.26
  716.7 11.1 slice-start.27
  716.7 11.0 slice-start.28
  750.2 23.4 %copy-start.65 = (f32[1280]{0:T(1024)S(1)}, f32[1280]{0:T(1024)}, u32[]{:S(2)}) copy-start(f32[1280]{0:T(1024)} %copy-done.64) | copy-start | bytes 15364
  750.2 23.4 %copy-start.68 = (f32[384]{0:T(512)S(1)}, f32[384]{0:T(512)}, u32[]{:S(2)}) copy-start(f32[384]{0:T(512)} %add_rsqrt_fusion) | copy-start | bytes 4612
  755.7 42.5 %all-to-all-start.4 = ((bf16[16,1,160]{2,1,0:T(2,128)(2,1)}), bf16[16,1,160]{2,1,0:T(2,128)(2,1)S(1)}, u32[]{:S(2)}, u32[]{:S(2)}) async-start(bf16[16,1,160]{2,1,0:T(2,128)(2,1)} %convert_element_type.666), calls=%async_computation.4 | async-start | bytes 32768 | tf_op jit(solution)/shard_map/all_to_all | solution.py:250
  784.5 11.1 copy-start.66
  798.2 14.0 %all-to-all-start.5 = ((bf16[16,1,160]{2,1,0:T(2,128)(2,1)}), bf16[16,1,160]{2,1,0:T(2,128)(2,1)S(1)}, u32[]{:S(2)}, u32[]{:S(2)}) async-start(bf16[16,1,160]{2,1,0:T(2,128)(2,1)} %convert_element_type.667), calls=%async_computation.5 | async-start | bytes 32768 | tf_op jit(solution)/shard_map/all_to_all | solution.py:253
  812.2 50.3 %all-to-all-start.2 = ((bf16[2,16,24,1280]{3,2,0,1:T(8,128)(2,1)}), bf16[2,16,24,1280]{3,2,0,1:T(8,128)(2,1)S(1)}, u32[]{:S(2)}, u32[]{:S(2)}) async-start(bf16[2,16,24,1280]{3,2,0,1:T(8,128)(2,1)} %copy.233), calls=%async_computation.2 | async-start | bytes 3932160 | tf_op jit(solution)/shard_map/all_to_all | solution.py:270
  863.9 429.4 %all-to-all-start.3 = ((bf16[16,480,1280]{2,1,0:T(8,128)(2,1)}), bf16[16,480,1280]{2,1,0:T(8,128)(2,1)}, u32[]{:S(2)}, u32[]{:S(2)}) async-start(bf16[16,480,1280]{2,1,0:T(8,128)(2,1)} %bitcast.552), calls=%async_computation.3 | async-start | bytes 39321600 | tf_op jit(solution)/shard_map/all_to_all | solution.py:247
  1293.3 9.7 copy-start.1
  (70 other events, 324.3 us)
Sparse Core Ops, SparseCore 0:
  10.4 145.6 all-gather.1
where the time goes:
time: 1320 us; the launch traced here: 1310 us
  matrix products  404 us (31%)
  waiting for transfers between devices  390 us (30%)
  local copies, waits for them, and re-layouts  220 us (17%)
  other arithmetic  115 us (9%)
  blocking collectives  111 us (8%)
  starting transfers between devices  52.2 us (4%)
  between operations  16.7 us (1%)
    all_to_all x1, waiting for transfers between devices, local(): lax.all_to_all(split_mats.astype(jnp.bfloat16), 'dp', split_axis=0, conca...  370 us
    dot_general x30, matrix products, mul_plain(): return jnp.dot(left, right, preferred_element_type=jnp.float32)  135 us
    scatter x5, local copies, waits for them, and re-layouts, local(): jnp.zeros((row_count,), jnp.int32).at[index_row].set(value_row)  109 us
    unnamed x1, blocking collectives  101 us
    dot_general x18, matrix products, mul_first_t(): lax.dot_general(left, right, (((0,), (0,)), ((), ())), preferred_element_...  94.5 us
    sub x6, matrix products, forward_parts(): expd = jnp.exp(scores - top_score)  44.9 us
    convert_element_type x1, other arithmetic, local(): split_mats.astype(jnp.bfloat16)  43 us
    dot_general x18, matrix products, mul_second_t(): lax.dot_general(left, right, (((1,), (1,)), ((), ())), preferred_element_...  38.8 us
  transfers between devices with their start and end apart: 10, of which 3 were waited for; matrix products, arithmetic and copies ran while one was open for 31% of the time, Pallas kernels for 0%

commit v1 on v0

v1 whole, which is shorter than its diff:
```python
import functools

import jax
import jax.numpy as jnp
from jax import lax
from jax.experimental import pallas as pl
from jax.experimental.pallas import tpu as pltpu
from jax.sharding import PartitionSpec as P

HEADS = 16
EPS = 1e-06
NEG = -1000000000.0
BOTH = ("section", "dp")
MESH = pl.DeviceIdType.MESH
PARTS = ((0, 112, "zxy"), (112, 112, "zyx"), (224, 128, "xzy"), (352, 128, "yzx"))


def coords():
    s=lax.axis_index("section"); d=lax.axis_index("dp")
    return s,d,d//4,(d//2)%2,d%2

def items():
    out=[]
    for bx in (0,1):
        for by in (0,1):
            for dz in (0,-1,1,-2,2,-3,3):
                out.append((bx,by,dz))
    return out
def hops(it): return it[0]+it[1]+abs(it[2])
def arrival(order,it):
    diff={"x":it[0]!=0,"y":it[1]!=0,"z":it[2]!=0}
    last=None
    for k,dim in enumerate(order):
        if diff[dim]: last=k
    return last

def neighbours(s,d,z,y,c,zn):
    return [(None,(1-s,d)),(None,(s,(z*2+1-y)*2+c)),(None,(s,(z*2+y)*2+1-c)),(z>0,(s,d-4)),(z<zn-1,(s,d+4))]

def ag_kernel(parts,zn,x_ref,w_ref,ssem,rsem,cs,cr,lsem):
    s,d,z,y,c=coords()
    bar=pltpu.get_barrier_semaphore()
    for cond,dev in neighbours(s,d,z,y,c,zn):
        def sig(dev=dev): pl.semaphore_signal(bar,inc=1,device_id=dev,device_id_type=MESH)
        sig() if cond is None else pl.when(cond)(sig)
    inner=jnp.logical_and(z>0,z<zn-1)
    pl.when(inner)(lambda: pl.semaphore_wait(bar,5))
    pl.when(jnp.logical_not(inner))(lambda: pl.semaphore_wait(bar,4))
    lc=pltpu.make_async_copy(x_ref,w_ref.at[s,d],lsem)
    lc.start()
    KIND={"x":0,"y":1,"l":2,"r":3}
    def where(it):
        s2=1-s if it[0] else s
        y2=1-y if it[1] else y
        z2=z+it[2]
        return s2,z2,y2
    def dsc(p,it,kind):
        r0,rn,order=parts[p]
        s2,z2,y2=where(it)
        idx=s2*(2*zn)+z2*2+y2
        own=it==(0,0,0)
        src=x_ref.at[pl.ds(r0,rn)] if own else w_ref.at[s2,(z2*2+y2)*2+c,pl.ds(r0,rn)]
        dst=w_ref.at[s2,(z2*2+y2)*2+c,pl.ds(r0,rn)]
        if kind=="core":
            dev=(s,(z*2+y)*2+1-c)
            return pltpu.make_async_remote_copy(src,dst,cs.at[p,idx],cr.at[p,idx],device_id=dev,device_id_type=MESH)
        dev={"x":(1-s,d),"y":(s,(z*2+1-y)*2+c),"l":(s,d-4),"r":(s,d+4)}[kind]
        return pltpu.make_async_remote_copy(src,dst,ssem.at[KIND[kind],p,idx],rsem.at[p,idx],device_id=dev,device_id_type=MESH)
    def cdsc(p,it):
        r0,rn,order=parts[p]
        s2,z2,y2=where(it)
        idx=s2*(2*zn)+z2*2+y2
        dst=w_ref.at[s2,(z2*2+y2)*2+1-c,pl.ds(r0,rn)]
        return pltpu.make_async_remote_copy(dst,dst,cs.at[p,idx],cr.at[p,idx],device_id=(s,(z*2+y)*2+1-c),device_id_type=MESH)
    def conds(it,kind):
        cs_=[]
        if it[2]<0: cs_.append(z+it[2]>=0)
        if it[2]>0: cs_.append(z+it[2]<=zn-1)
        if kind=="l": cs_.append(z>0)
        if kind=="r": cs_.append(z<zn-1)
        return cs_
    def guarded(cl,fn):
        if not cl: fn(); return
        e=cl[0]
        for q in cl[1:]: e=jnp.logical_and(e,q)
        pl.when(e)(fn)
    def sends(p,it):
        order=parts[p][2]
        a=arrival(order,it)
        ks=[]
        if a is not None and order[a]=="z": ks.append("l" if it[2]>0 else "r")
        for dim in order[(a+1) if a is not None else 0:]:
            ks += ["r","l"] if dim=="z" else [dim]
        ks.append("core")
        return ks
    evs=[]
    for p in range(len(parts)):
        for it in items(): evs.append((hops(it),p,it))
    evs.sort(key=lambda e:e[0])
    todo=[]
    for h,p,it in evs:
        if abs(it[2])>zn-1: continue
        def ev(p=p,it=it):
            if it!=(0,0,0): dsc(p,it,"x").wait_recv()
            for k in sends(p,it):
                guarded([q for q in conds((0,0,0),k)], lambda k=k: dsc(p,it,k).start())
        guarded(conds(it,None),ev)
        todo.append((p,it))
    for p,it in todo:
        def fin(p=p,it=it):
            cdsc(p,it).wait_recv()
            for k in sends(p,it):
                guarded(conds((0,0,0),k), lambda k=k: dsc(p,it,k).wait_send())
        guarded(conds(it,None),fin)
    lc.wait()

def ag(x,parts,zn,cid=0):
    n=len(parts)
    return pl.pallas_call(functools.partial(ag_kernel,parts,zn),
        out_shape=jax.ShapeDtypeStruct((2,4*zn,480,1280),jnp.bfloat16),
        in_specs=[pl.BlockSpec(memory_space=pl.ANY)],out_specs=pl.BlockSpec(memory_space=pl.ANY),
        scratch_shapes=[pltpu.SemaphoreType.DMA((4,n,4*zn)),pltpu.SemaphoreType.DMA((n,4*zn)),
          pltpu.SemaphoreType.DMA((n,4*zn)),pltpu.SemaphoreType.DMA((n,4*zn)),pltpu.SemaphoreType.DMA],
        compiler_params=pltpu.CompilerParams(collective_id=cid,has_side_effects=True))(x)


def rs_kernel(parts,zn,g_ref,o_ref,land,buf,obuf,*rest):
    nP=len(parts)
    lks=rest[:nP]
    ssem,rsem,cs,cr,lsem,osem=rest[nP:]
    s,d,z,y,c=coords()
    bar=pltpu.get_barrier_semaphore()
    for cond,dev in neighbours(s,d,z,y,c,zn):
        def sig(dev=dev): pl.semaphore_signal(bar,inc=1,device_id=dev,device_id_type=MESH)
        sig() if cond is None else pl.when(cond)(sig)
    inner=jnp.logical_and(z>0,z<zn-1)
    pl.when(inner)(lambda: pl.semaphore_wait(bar,5))
    pl.when(jnp.logical_not(inner))(lambda: pl.semaphore_wait(bar,4))
    sib=(s,(z*2+y)*2+1-c)
    def where(it):
        s2=1-s if it[0] else s
        y2=1-y if it[1] else y
        return s2,z+it[2],y2
    def conds(it):
        cl=[]
        if it[2]<0: cl.append(z+it[2]>=0)
        if it[2]>0: cl.append(z+it[2]<=zn-1)
        return cl
    def guarded(cl,fn):
        if not cl: fn(); return
        e=cl[0]
        for q in cl[1:]: e=jnp.logical_and(e,q)
        pl.when(e)(fn)
    def slot_base(order):
        sizes={"x":2,"y":2,"z":zn}
        base={};cur=0
        for k,dim in enumerate(order):
            n=1
            for q in order[k+1:]: n*=sizes[q]
            if dim=="z": n*=2*zn
            base[dim]=cur; cur+=n
        return base,cur
    def slot(p,dim,side,dest):
        order=parts[p][2][::-1]
        base,_=slot_base(order)
        k=order.index(dim)
        v={"x":dest[0],"z":dest[1],"y":dest[2]}
        idx=0
        for q in order[k+1:]:
            idx=idx*(zn if q=="z" else 2)+v[q]
        if dim=="z": idx=(idx*zn+dest[1])*2+side
        return base[dim]+idx
    evs=[]
    for p in range(nP):
        for it in items():
            if abs(it[2])<=zn-1: evs.append((-hops(it),p,it))
    evs.sort(key=lambda e:e[0])
    seq=[(p,it) for _,p,it in evs]
    def core_dsc(p,it,mine):
        r0,rn,_=parts[p]
        s2,z2,y2=where(it)
        idx=(s2*zn+z2)*2+y2
        cc=c if mine else 1-c
        return pltpu.make_async_remote_copy(g_ref.at[s2,(z2*2+y2)*2+cc,pl.ds(r0,rn)],land.at[idx,pl.ds(r0,rn)],cs.at[p,idx],cr.at[p,idx],device_id=sib,device_id_type=MESH)
    for p,it in seq:
        guarded(conds(it),lambda p=p,it=it: core_dsc(p,it,False).start())
    def load(i):
        p,it=seq[i]
        r0,rn,_=parts[p]
        s2,z2,y2=where(it)
        return pltpu.make_async_copy(g_ref.at[s2,(z2*2+y2)*2+c,pl.ds(r0,rn)],buf.at[i%NB,pl.ds(0,rn)],lsem.at[i%NB])
    NB=buf.shape[0]
    for i in range(min(NB-1,len(seq))):
        guarded(conds(seq[i][1]),lambda i=i: load(i).start())
    def contribs(p,it):
        order=parts[p][2][::-1]
        diff={"x":it[0],"y":it[1],"z":it[2]}
        out=[];nxt=None
        for dim in order:
            if dim=="z":
                if it[2]==0: out+=[("z",0,z>0),("z",1,z<zn-1)]
                elif it[2]>0: out.append(("z",0,z>0))
                else: out.append(("z",1,z<zn-1))
                if it[2]!=0: nxt="r" if it[2]>0 else "l"; break
            else:
                if diff[dim]: nxt=dim; break
                out.append((dim,0,None))
        return out,nxt
    semoff=[0]
    for p in range(nP): semoff.append(semoff[-1]+slot_base(parts[p][2][::-1])[1])
    def out_dsc(p,it,nxt):
        r0,rn,_=parts[p]
        dest=where(it)
        s2,z2,y2=dest
        idx=(s2*zn+z2)*2+y2
        dim="z" if nxt in "lr" else nxt
        side=1 if nxt=="l" else 0
        sl=slot(p,dim,side,dest)
        dev={"x":(1-s,d),"y":(s,(z*2+1-y)*2+c),"l":(s,d-4),"r":(s,d+4)}[nxt]
        return pltpu.make_async_remote_copy(land.at[idx,pl.ds(r0,rn)],lks[p].at[sl],ssem.at[p,idx],rsem.at[semoff[p]+sl],device_id=dev,device_id_type=MESH)
    for i,(p,it) in enumerate(seq):
        r0,rn,_=parts[p]
        if i+NB-1<len(seq):
            guarded(conds(seq[i+NB-1][1]),lambda i=i: load(i+NB-1).start())
        def ev(i=i,p=p,it=it,r0=r0,rn=rn):
            dest=where(it)
            s2,z2,y2=dest
            idx=(s2*zn+z2)*2+y2
            con,nxt=contribs(p,it)
            lk=lks[p]
            load(i).wait()
            core_dsc(p,it,True).wait_recv()
            plain=[x for x in con if x[2] is None]
            cond=[x for x in con if x[2] is not None]
            def rdsc(dim,side):
                sl=slot(p,dim,side,dest)
                return pltpu.make_async_remote_copy(lk.at[sl],lk.at[sl],ssem.at[p,idx],rsem.at[semoff[p]+sl],device_id=sib,device_id_type=MESH),sl
            for dim,side,_ in plain: rdsc(dim,side)[0].wait_recv()
            for dim,side,cnd in cond:
                pl.when(cnd)(lambda dim=dim,side=side: rdsc(dim,side)[0].wait_recv())
            if not cond: variants=[(None,plain)]
            elif len(cond)==1:
                variants=[(cond[0][2],plain+cond),(jnp.logical_not(cond[0][2]),plain)]
            else:
                a,b=cond
                variants=[(jnp.logical_and(a[2],b[2]),plain+cond),(jnp.logical_and(a[2],jnp.logical_not(b[2])),plain+[a]),
                          (jnp.logical_and(jnp.logical_not(a[2]),b[2]),plain+[b])]
            def total(lst):
                slots=[slot(p,dim,side,dest) for dim,side,_ in lst]
                CH=16
                def body(k,_):
                    ro=pl.multiple_of(k*CH,CH)
                    acc=buf[i%NB,pl.ds(ro,CH),:].astype(jnp.float32)+land[idx,pl.ds(r0+ro,CH),:].astype(jnp.float32)
                    for sl in slots: acc=acc+lk[sl,pl.ds(ro,CH),:].astype(jnp.float32)
                    if nxt is None: obuf[pl.ds(r0+ro,CH),:]=acc
                    else: land[idx,pl.ds(r0+ro,CH),:]=acc.astype(jnp.bfloat16)
                    return 0
                lax.fori_loop(0,rn//CH,body,0)
            for cnd,lst in variants:
                if cnd is None: total(lst)
                else: pl.when(cnd)(lambda lst=lst: total(lst))
            if nxt is not None: out_dsc(p,it,nxt).start()
            else: pltpu.make_async_copy(obuf.at[pl.ds(r0,rn)],o_ref.at[pl.ds(r0,rn)],osem.at[p]).start()
        guarded(conds(it),ev)
    for p,it in seq:
        def fin(p=p,it=it):
            core_dsc(p,it,False).wait_send()
            nxt=contribs(p,it)[1]
            if nxt is not None: out_dsc(p,it,nxt).wait_send()
        guarded(conds(it),fin)
    for p,(r0,rn,_) in enumerate(parts):
        pltpu.make_async_copy(obuf.at[pl.ds(r0,rn)],o_ref.at[pl.ds(r0,rn)],osem.at[p]).wait()

def slot_count(order,zn):
    sizes={"x":2,"y":2,"z":zn};cur=0
    for k,dim in enumerate(order):
        n=1
        for q in order[k+1:]: n*=sizes[q]
        if dim=="z": n*=2*zn
        cur+=n
    return cur
def rs(g,parts,zn,cid=1,nb=4):
    n=len(parts)
    cnt=[slot_count(p[2][::-1],zn) for p in parts]
    mx=max(p[1] for p in parts)
    return pl.pallas_call(functools.partial(rs_kernel,parts,zn),
        out_shape=jax.ShapeDtypeStruct((480,1280),jnp.float32),
        in_specs=[pl.BlockSpec(memory_space=pl.ANY)],out_specs=pl.BlockSpec(memory_space=pl.ANY),
        scratch_shapes=[pltpu.VMEM((4*zn,480,1280),jnp.bfloat16),pltpu.VMEM((nb,mx,1280),jnp.bfloat16),pltpu.VMEM((480,1280),jnp.float32)]
          +[pltpu.VMEM((cnt[p],parts[p][1],1280),jnp.bfloat16) for p in range(n)]
          +[pltpu.SemaphoreType.DMA((n,4*zn)),pltpu.SemaphoreType.DMA((sum(cnt),)),
          pltpu.SemaphoreType.DMA((n,4*zn)),pltpu.SemaphoreType.DMA((n,4*zn)),pltpu.SemaphoreType.DMA((nb,)),pltpu.SemaphoreType.DMA((n,))],
        compiler_params=pltpu.CompilerParams(collective_id=cid,has_side_effects=True,vmem_limit_bytes=62*2**20))(g)


def normed(value, gain):
    return value * lax.rsqrt(jnp.mean(value * value, axis=-1, keepdims=True) + EPS) * gain


def mul_plain(left, right):
    return jnp.dot(left, right, preferred_element_type=jnp.float32)


def mul_first_t(left, right):
    return lax.dot_general(
        left, right, (((0,), (0,)), ((), ())), preferred_element_type=jnp.float32
    )


def mul_second_t(left, right):
    return lax.dot_general(
        left, right, (((1,), (1,)), ((), ())), preferred_element_type=jnp.float32
    )


def forward_parts(inputs, segment, weights):
    w_query, w_key, w_value, w_mix, w_inner, w_outer, gain_one, gain_two, bias_inner, bias_outer = (
        weights
    )
    row_count, model_width = inputs.shape
    depth = model_width // HEADS
    scale = depth ** (-0.5)
    first = normed(inputs, gain_one).astype(jnp.bfloat16)
    query = mul_plain(first, w_query).astype(jnp.bfloat16)
    keys = mul_plain(first, w_key).astype(jnp.bfloat16)
    values = mul_plain(first, w_value).astype(jnp.bfloat16)
    query_h = query.reshape(row_count, HEADS, depth)
    keys_h = keys.reshape(row_count, HEADS, depth)
    values_h = values.reshape(row_count, HEADS, depth)
    scores = jnp.einsum("qhd,khd->hqk", query_h, keys_h, preferred_element_type=jnp.float32) * scale
    positions = jnp.arange(row_count, dtype=jnp.int32)
    allowed = (segment[:, None] == segment[None, :]) & (positions[None, :] <= positions[:, None])
    scores = jnp.where(allowed[None], scores, NEG)
    top_score = jnp.max(scores, axis=-1, keepdims=True)
    expd = jnp.exp(scores - top_score)
    soft = expd / jnp.sum(expd, axis=-1, keepdims=True)
    probs = soft.astype(jnp.bfloat16)
    attended = jnp.einsum("hqk,khd->qhd", probs, values_h, preferred_element_type=jnp.float32)
    attended = attended.reshape(row_count, model_width).astype(jnp.bfloat16)
    middle = inputs + mul_plain(attended, w_mix)
    second = normed(middle, gain_two).astype(jnp.bfloat16)
    inner = mul_plain(second, w_inner) + bias_inner
    active = jax.nn.gelu(inner, approximate=True).astype(jnp.bfloat16)
    output = middle + (mul_plain(active, w_outer) + bias_outer)
    saved = (first, query_h, keys_h, values_h, soft, probs, attended, middle, second, inner, active)
    return (output, saved)


def layer_backward(inputs, saved, weights, cotangent):
    w_query, w_key, w_value, w_mix, w_inner, w_outer, gain_one, gain_two, bias_inner, bias_outer = (
        weights
    )
    row_count, model_width = inputs.shape
    depth = model_width // HEADS
    scale = depth ** (-0.5)
    first, query_h, keys_h, values_h, soft, probs, attended, middle, second, inner, active = saved
    grad_outer = cotangent.astype(jnp.bfloat16)
    d_bias_outer = jnp.sum(grad_outer.astype(jnp.float32), axis=0)
    d_w_outer = mul_first_t(active, grad_outer)
    d_active = mul_second_t(grad_outer, w_outer)
    gelu_value, gelu_back = jax.vjp(lambda pre_act: jax.nn.gelu(pre_act, approximate=True), inner)
    d_inner = gelu_back(d_active)[0].astype(jnp.bfloat16)
    d_bias_inner = jnp.sum(d_inner.astype(jnp.float32), axis=0)
    d_w_inner = mul_first_t(second, d_inner)
    d_second = mul_second_t(d_inner, w_inner)
    norm_value, norm_back = jax.vjp(normed, middle, gain_two)
    d_middle_norm, d_gain_two = norm_back(d_second)
    d_middle = cotangent + d_middle_norm
    d_branch = d_middle.astype(jnp.bfloat16)
    d_w_mix = mul_first_t(attended, d_branch)
    d_attended = mul_second_t(d_branch, w_mix).astype(jnp.bfloat16).reshape(row_count, HEADS, depth)
    d_probs = jnp.einsum("qhd,khd->hqk", d_attended, values_h, preferred_element_type=jnp.float32)
    d_values = jnp.einsum("hqk,qhd->khd", probs, d_attended, preferred_element_type=jnp.float32)
    d_values = d_values.reshape(row_count, model_width).astype(jnp.bfloat16)
    d_scores = (soft * (d_probs - jnp.sum(d_probs * soft, axis=-1, keepdims=True))).astype(
        jnp.bfloat16
    )
    d_query = (
        jnp.einsum("hqk,khd->qhd", d_scores, keys_h, preferred_element_type=jnp.float32) * scale
    )
    d_query = d_query.reshape(row_count, model_width).astype(jnp.bfloat16)
    d_keys = (
        jnp.einsum("hqk,qhd->khd", d_scores, query_h, preferred_element_type=jnp.float32) * scale
    )
    d_keys = d_keys.reshape(row_count, model_width).astype(jnp.bfloat16)
    d_w_query = mul_first_t(first, d_query)
    d_w_key = mul_first_t(first, d_keys)
    d_w_value = mul_first_t(first, d_values)
    d_first = (
        mul_second_t(d_query, w_query)
        + mul_second_t(d_keys, w_key)
        + mul_second_t(d_values, w_value)
    )
    first_value, first_back = jax.vjp(normed, inputs, gain_one)
    d_inputs_norm, d_gain_one = first_back(d_first)
    d_inputs = d_middle + d_inputs_norm
    d_mats = jnp.stack([w.astype(jnp.bfloat16) for w in (d_w_query, d_w_key, d_w_value, d_w_mix, d_w_inner, d_w_outer)])
    d_gains = jnp.stack([d_gain_one, d_gain_two])
    d_biases = jnp.stack([d_bias_inner, d_bias_outer])
    return (d_inputs, d_mats, d_gains, d_biases)


def one_hot(rank):
    rows = rank.shape[0]
    return (rank[None, :] == jnp.arange(rows, dtype=jnp.int32)[:, None]).astype(jnp.bfloat16)


def rank_of(key):
    return jnp.sum((key[None, :] < key[:, None]).astype(jnp.int32), axis=1)


def gather_weights(own, peers):
    if peers == 16:
        return ag(own, PARTS, peers // 4)
    rows, width = own.shape
    return lax.all_gather(own, BOTH, axis=0, tiled=True).reshape(2, peers, rows, width)


def scatter_grads(terms, peers):
    if peers == 16:
        return rs(terms, PARTS, peers // 4)
    sections, _, rows, width = terms.shape
    terms = terms.reshape(sections * peers * rows, width)
    return lax.psum_scatter(terms, BOTH, scatter_dimension=0, tiled=True).astype(jnp.float32)


def local(entering, deal, seq_lens, mats, gains, biases):
    section = lax.axis_index("section")
    own_dp = lax.axis_index("dp")
    peers = lax.axis_size("dp")
    arrival = entering[0]
    batches, rows, width = arrival.shape
    per_peer = rows // peers
    all_deal = lax.all_gather(deal, "dp", axis=1, tiled=True)
    small = jnp.concatenate([gains[0], biases[0]]).astype(jnp.bfloat16).astype(jnp.float32)
    small = lax.all_gather(small, BOTH, axis=0).reshape(2, peers, 2, -1)
    small = jnp.swapaxes(small, 1, 2).reshape(2, 2, 2, width)
    all_mats = gather_weights(mats[0].astype(jnp.bfloat16), peers)
    all_mats = all_mats.reshape(2, 6, width, width)
    own_rows = own_dp * rows + jnp.arange(rows, dtype=jnp.int32)
    block_ids = jnp.arange(all_deal.shape[1], dtype=jnp.int32) // rows
    sends = []
    returns = []
    for batch in range(batches):
        hit = all_deal[batch][None, :] == own_rows[:, None]
        target = jnp.sum(jnp.where(hit, block_ids[None, :], 0), axis=1)
        key = target * rows + jnp.arange(rows, dtype=jnp.int32)
        pick = one_hot(rank_of(key))
        returns.append(pick)
        sends.append(mul_plain(pick, arrival[batch]).astype(jnp.bfloat16))
    outgoing = jnp.stack(sends).reshape(2 * peers, per_peer, width)
    arrived = lax.all_to_all(outgoing, BOTH, split_axis=0, concat_axis=0, tiled=True)
    arrived = arrived.reshape(2, rows, width)
    own_deal = jnp.where(section == 0, deal[0], deal[1])
    place = one_hot(rank_of(own_deal))
    tokens = mul_first_t(place, arrived[0])
    cotangent = mul_first_t(place, arrived[1])
    lens = jnp.where(section == 0, seq_lens[0, 0], seq_lens[1, 0])
    ends = jnp.cumsum(lens)
    positions = jnp.arange(rows, dtype=jnp.int32)
    segment = jnp.sum((positions[:, None] >= ends[None, :]).astype(jnp.int32), axis=1)
    state = tokens
    kept = []
    weights = []
    for layer in range(2):
        if layer:
            state = state.astype(jnp.bfloat16).astype(jnp.float32)
        mats_l = tuple(all_mats[layer, index] for index in range(6))
        weights.append(mats_l + (small[layer, 0, 0], small[layer, 0, 1], small[layer, 1, 0], small[layer, 1, 1]))
        out, saved = forward_parts(state, segment, weights[layer])
        kept.append((state, saved))
        state = out
    final = state.astype(jnp.bfloat16)
    grads = [None, None]
    down = cotangent
    for layer in (1, 0):
        down, d_mats, d_gains, d_biases = layer_backward(kept[layer][0], kept[layer][1], weights[layer], down)
        down = down.astype(jnp.bfloat16).astype(jnp.float32)
        grads[layer] = (d_mats, d_gains, d_biases)
    terms = jnp.stack([grads[0][0], grads[1][0]]).reshape(2, peers, -1, width)
    shard_mats = scatter_grads(terms, peers)[None]
    small_grads = jnp.stack([jnp.stack([grads[layer][1], grads[layer][2]]) for layer in range(2)])
    small_grads = lax.psum(small_grads.reshape(2, 2, 2 * width), BOTH)
    per = 2 * width // peers
    mine = lax.dynamic_slice(small_grads, (section, 0, own_dp * per), (1, 2, per))
    back = jnp.stack([mul_plain(place, down.astype(jnp.bfloat16)), mul_plain(place, final)]).astype(jnp.bfloat16)
    back = back.reshape(2 * peers, per_peer, width)
    returned = lax.all_to_all(back, BOTH, split_axis=0, concat_axis=0, tiled=True).reshape(2, rows, width)
    results = jnp.stack([mul_first_t(returns[batch], returned[batch]) for batch in range(batches)])
    return (results.astype(jnp.bfloat16)[None], shard_mats, mine[:, 0], mine[:, 1])


def solution(mesh):
    in_specs = (
        P("section", None, "dp", None),
        P(None, "dp"),
        P(None, "dp", None),
        P("section", "dp", None),
        P("section", "dp"),
        P("section", "dp"),
    )
    out_specs = (
        P("section", None, "dp", None),
        P("section", "dp", None),
        P("section", "dp"),
        P("section", "dp"),
    )
    return jax.shard_map(local, mesh=mesh, in_specs=in_specs, out_specs=out_specs, check_vma=False)
```

time: 1320 us -> 754 us (0.57)
  the two profiles are of different devices: /device:TPU:17 before, /device:TPU:0 now
where the time goes in v1:
time: 754 us; the launch traced here: 748 us
  Pallas kernels  294 us (39%)
  matrix products  218 us (29%)
  blocking collectives  137 us (18%)
  other arithmetic  60.4 us (8%)
  local copies, waits for them, and re-layouts  29.7 us (4%)
    pallas_call x1, Pallas kernels, rs(): pl.pallas_call(functools.partial(rs_kernel, parts, zn), out_shape=jax.Sha...  147 us
    pallas_call x1, Pallas kernels, ag(): pl.pallas_call(functools.partial(ag_kernel, parts, zn), out_shape=jax.Sha...  147 us
    all_gather x1, blocking collectives, local(): small = lax.all_gather(small, BOTH, axis=0).reshape(2, peers, 2, -1)  72.6 us
    dot_general x15, matrix products, mul_plain(): return jnp.dot(left, right, preferred_element_type=jnp.float32)  57.7 us
    dot_general x12, matrix products, mul_second_t(): lax.dot_general(left, right, (((1,), (1,)), ((), ())), preferred_element_...  50.9 us
    dot_general x16, matrix products, mul_first_t(): lax.dot_general(left, right, (((0,), (0,)), ((), ())), preferred_element_...  49 us
    psum x1, blocking collectives, local(): small_grads = lax.psum(small_grads.reshape(2, 2, 2 * width), BOTH)  40.3 us
    another operation x1, other arithmetic, local(): terms = jnp.stack([grads[0][0], grads[1][0]]).reshape(2, peers, -1, width)  26.7 us
  transfers between devices with their start and end apart: 2, of which 0 were waited for; matrix products, arithmetic and copies ran while one was open for 9% of the time, Pallas kernels for 39%

profile of v1, /device:TPU:0, one launch (start us, length us, event | category | flops | bytes accessed | tf_op | source)
XLA Modules:
  0.0 747.9 jit_solution(15103957611458076217)
XLA Ops:
  0.7 23.6 %all_gather.7 = s32[2,6144]{1,0:T(2,128)S(1)} all-gather(s32[2,384]{1,0:T(2,128)} %param.7), channel_id=1, replica_groups=mesh['section'=2,'dp'=16] {'dp'}, dimensions={1}, use_global_device_ids=true | all-gather | bytes 52224 | tf_op jit(solution)/shard_map/all_gather | solution.py:434
  34.7 72.6 %all-gather = f32[32,1,320]{2,1,0:T(1,128)S(1)} all-gather(f32[1,1,320]{2,1,0:T(1,128)S(1)} %fusion.146), channel_id=1, replica_groups=mesh['section'=2,'dp'=16] {'section','dp'}, dimensions={0}, use_global_device_ids=true | all-gather | bytes 42240 | tf_op jit(solution)/shard_map/all_gather | solution.py:436
  110.5 146.8 %shard_map.93 = bf16[2,16,480,1280]{3,2,1,0:T(8,128)(2,1)} custom-call(bf16[480,1280]{1,0:T(8,128)(2,1)} %convert_bitcast_fusion.x_ref), custom_call_target="tpu_custom_call" | custom-call | tf_op jit(solution)/shard_map/pallas_call | solution.py:119
  260.6 5.1 fusion.55
  265.8 4.4 fusion.56
  270.1 4.3 fusion.57
  281.3 8.1 %fusion.164 = (f32[16,384]{1,0:T(8,128)S(1)}, f32[16,384,384]{1,2,0:T(8,128)}) fusion(pred[384,384]{0,1:T(8,128)(4,1)S(1)} %fusion.125, bf16[384,16,80]{0,2,1:T(8,128)(2,1)} %bitcast.309, bf16[384,16,80]{0,2,1:T(8,128)(2,1)S(1)} %bitcast.307), kind=kOutput, calls=%fused_computation.280 | convolution fusion | flops 386924928 | bytes 11575296 | tf_op jit(solution)/shard_map/sub | solution.py:335
  289.5 5.0 fusion.99
  294.5 3.9 multiply_reduce_fusion.9
  298.4 4.1 convolution_add_fusion.7
  302.6 4.6 fusion.97
  307.2 4.7 fusion.52
  311.9 4.4 fusion.51
  316.3 4.4 fusion.53
  328.1 8.1 %fusion.165 = (f32[16,384]{1,0:T(8,128)S(1)}, f32[16,384,384]{1,2,0:T(8,128)}) fusion(pred[384,384]{0,1:T(8,128)(4,1)S(1)} %fusion.125, bf16[384,16,80]{0,2,1:T(8,128)(2,1)S(1)} %bitcast.311, bf16[384,16,80]{0,2,1:T(8,128)(2,1)} %bitcast.313), kind=kOutput, calls=%fused_computation.281 | convolution fusion | flops 386924928 | bytes 11575296 | tf_op jit(solution)/shard_map/sub | solution.py:335
  336.2 5.0 fusion.105
  341.3 3.9 multiply_reduce_fusion.8
  345.2 4.1 convolution_add_fusion.5
  349.3 4.9 convert_reduce_fusion.2
  354.2 3.9 multiply_reduce_fusion.2
  360.1 4.4 fusion.50
  366.8 6.9 fusion.108
  373.9 4.8 multiply_reduce_fusion.1
  378.7 10.4 %multiply_convert_fusion.1 = bf16[16,384,384]{1,2,0:T(8,128)(2,1)} fusion(f32[16,384,384]{1,2,0:T(8,128)} %get-tuple-element.48, f32[16,384]{1,0:T(8,128)S(1)} %get-tuple-element.47, f32[16,384,384]{1,2,0:T(8,128)} %get-tuple-element.43, f32[16,384]{1,0:T(8,128)S(1)} %get-tuple-element.42), kind=kLoop, calls=%fused_computation.5 | loop fusion | flops 9437184 | bytes 23642112 | tf_op jit(solution)/shard_map/convert_element_type | solution.py:375
  389.1 4.2 multiply_convert_fusion.5
  394.4 3.8 fusion.45
  401.9 3.9 fusion.77
  407.4 4.3 convert_reduce_fusion.3
  411.7 4.1 multiply_reduce_fusion.3
  417.6 4.4 fusion.54
  424.3 6.9 fusion.102
  431.4 4.5 multiply_reduce_fusion
  435.9 10.4 %multiply_convert_fusion = bf16[16,384,384]{1,2,0:T(8,128)(2,1)} fusion(f32[16,384,384]{1,2,0:T(8,128)} %get-tuple-element.52, f32[16,384]{1,0:T(8,128)S(1)} %get-tuple-element.51, f32[16,384,384]{1,2,0:T(8,128)} %get-tuple-element.37, f32[16,384]{1,0:T(8,128)S(1)} %get-tuple-element.36), kind=kLoop, calls=%fused_computation.3 | loop fusion | flops 9437184 | bytes 23642112 | tf_op jit(solution)/shard_map/convert_element_type | solution.py:375
  446.3 5.2 multiply_convert_fusion.3
  452.4 4.8 fusion.38
  460.8 3.7 fusion.17
  464.6 6.3 fusion.63
  471.1 4.9 convolution_add_fusion.2
  476.0 3.8 multiply_reduce_fusion.4
  482.7 4.4 all-to-all-start.1
  487.0 5.2 fusion.7
  503.2 3.8 fusion.15
  510.7 4.0 fusion.21
  518.3 3.7 fusion.25
  522.0 3.8 fusion.27
  525.8 26.7 %pad_maximum_fusion.g_ref = bf16[2,16,480,1280]{3,2,1,0:T(8,128)(2,1)} fusion(bf16[1,16,480,1280]{3,2,1,0:T(8,128)(2,1)} %bitcast.79, bf16[1,16,480,1280]{3,2,1,0:T(8,128)(2,1)} %bitcast.299), kind=kLoop, calls=%fused_computation.2 | loop fusion | flops 19660800 | bytes 78643200 | tf_op jit(solution)/shard_map/stack | solution.py:480
  552.6 147.1 %shard_map.94 = f32[480,1280]{1,0:T(8,128)} custom-call(bf16[2,16,480,1280]{3,2,1,0:T(8,128)(2,1)} %pad_maximum_fusion.g_ref), custom_call_target="tpu_custom_call" | custom-call | tf_op jit(solution)/shard_map/pallas_call | solution.py:286
  699.7 40.3 %psum.7 = f32[2,2,2560]{2,1,0:T(2,128)S(1)} all-reduce(f32[2,2,2560]{2,1,0:T(2,128)S(1)} %maximum_maximum_fusion), channel_id=1, replica_groups=mesh['section'=2,'dp'=16] {'section','dp'}, use_global_device_ids=true, to_apply=%region_29.30 | all-reduce | flops 10240 | bytes 81920 | tf_op jit(solution)/shard_map/psum | solution.py:483
  (247 shorter events, 79.1 us)
Async XLA Ops:
  0.6 28.8 %copy-start.58 = (bf16[1,2,384,1280]{3,2,1,0:T(8,128)(2,1)S(1)}, bf16[1,2,384,1280]{3,2,1,0:T(8,128)(2,1)}, u32[]{:S(2)}) copy-start(bf16[1,2,384,1280]{3,2,1,0:T(8,128)(2,1)} %param.6) | copy-start | bytes 5898244
  31.6 226.9 %all-to-all-start = ((bf16[32,24,1280]{2,1,0:T(8,128)(2,1)}), bf16[32,24,1280]{2,1,0:T(8,128)(2,1)S(1)}, u32[]{:S(2)}, u32[]{:S(2)}) async-start(bf16[32,24,1280]{2,1,0:T(8,128)(2,1)} %bitcast.305), calls=%async_computation | async-start | bytes 3932160 | tf_op jit(solution)/shard_map/all_to_all | solution.py:452
  110.5 146.8 %copy-start.49 = (s32[2,384]{1,0:T(2,128)S(1)}, s32[2,384]{1,0:T(2,128)}, u32[]{:S(2)}) copy-start(s32[2,384]{1,0:T(2,128)} %param.7) | copy-start | bytes 9220
  260.3 5.4 copy-start.47
  260.3 34.1 %copy-start.2 = (f32[384,1280]{1,0:T(8,128)}, f32[384,1280]{1,0:T(8,128)S(1)}, u32[]{:S(2)}) copy-start(f32[384,1280]{1,0:T(8,128)S(1)} %get-tuple-element.35) | copy-start | bytes 5898244
  260.4 5.4 copy-start.45
  260.6 9.5 %copy-start.33 = (bf16[384,1280]{1,0:T(8,128)(2,1)}, bf16[384,1280]{1,0:T(8,128)(2,1)S(1)}, u32[]{:S(2)}) copy-start(bf16[384,1280]{1,0:T(8,128)(2,1)S(1)} %multiply_convert_fusion.10) | copy-start | bytes 2949124
  276.0 5.3 copy-start.14
  298.4 4.2 copy-start.5
  302.5 4.6 copy-start.65
  307.1 9.1 %copy-start.25 = (bf16[384,1280]{1,0:T(8,128)(2,1)}, bf16[384,1280]{1,0:T(8,128)(2,1)S(1)}, u32[]{:S(2)}) copy-start(bf16[384,1280]{1,0:T(8,128)(2,1)S(1)} %get-tuple-element.41) | copy-start | bytes 2949124
  316.3 4.5 copy-start.22
  323.0 5.0 copy-start.19
  336.2 5.1 copy-start.26
  341.2 3.9 copy-start.59
  345.2 13.0 %copy-start.23 = (f32[384,1280]{1,0:T(8,128)}, f32[384,1280]{1,0:T(8,128)S(1)}, u32[]{:S(2)}) copy-start(f32[384,1280]{1,0:T(8,128)S(1)} %get-tuple-element.45) | copy-start | bytes 5898244
  349.3 4.9 copy-start.68
  364.5 9.2 %slice-start.3 = ((s8[9437184]{0:T(1024)(128)(4,1)}), s8[1048576]{0:T(1024)(128)(4,1)S(1)}, s32[]{:S(2)}) async-start(s8[9437184]{0:T(1024)(128)(4,1)} %bitcast.303), calls=%async_computation.5 | async-start | bytes 2097152
  366.8 6.9 slice-start.4
  366.8 6.9 slice-start.5
  366.8 6.9 copy-start.39
  366.8 7.1 copy-start.40
  378.7 10.5 %copy-start.20 = (bf16[384,1280]{0,1:T(8,128)(2,1)S(1)}, bf16[384,1280]{0,1:T(8,128)(2,1)}, u32[]{:S(2)}) copy-start(bf16[384,1280]{0,1:T(8,128)(2,1)} %copy-done.19) | copy-start | bytes 2949124
  389.1 4.2 copy-start
  389.1 4.2 copy-start.21
  393.4 4.8 copy-start.29
  401.9 4.0 copy-start.9
  406.5 9.3 %copy-start.16 = (bf16[384,1280]{1,0:T(8,128)(2,1)}, bf16[384,1280]{1,0:T(8,128)(2,1)S(1)}, u32[]{:S(2)}) copy-start(bf16[384,1280]{1,0:T(8,128)(2,1)S(1)} %get-tuple-element.23) | copy-start | bytes 2949124
  407.4 4.3 copy-start.6
  411.7 4.1 copy-start.72
  417.6 13.6 %slice-start = ((s8[9437184]{0:T(1024)(128)(4,1)}), s8[1048576]{0:T(1024)(128)(4,1)S(1)}, s32[]{:S(2)}) async-start(s8[9437184]{0:T(1024)(128)(4,1)} %bitcast.301), calls=%async_computation.2 | async-start | bytes 2097152
  424.3 6.9 slice-start.1
  424.3 6.9 slice-start.2
  424.3 6.9 copy-start.38
  424.3 7.1 copy-start.41
  435.9 10.4 %copy-start.18 = (bf16[384,1280]{0,1:T(8,128)(2,1)S(1)}, bf16[384,1280]{0,1:T(8,128)(2,1)}, u32[]{:S(2)}) copy-start(bf16[384,1280]{0,1:T(8,128)(2,1)} %copy.86) | copy-start | bytes 2949124
  446.3 5.2 copy-start.1
  446.3 5.2 copy-start.15
  452.4 4.8 copy-start.34
  471.0 4.9 copy-start.3
  471.0 4.9 copy-start.44
  471.1 4.9 copy-start.46
  471.1 4.9 copy-start.63
  482.7 258.1 %all-to-all-start.1 = ((bf16[32,24,1280]{2,1,0:T(8,128)(2,1)}), bf16[32,24,1280]{2,1,0:T(8,128)(2,1)}, u32[]{:S(2)}, u32[]{:S(2)}) async-start(bf16[32,24,1280]{2,1,0:T(8,128)(2,1)} %bitcast.306), calls=%async_computation.1 | async-start | bytes 3932160 | tf_op jit(solution)/shard_map/all_to_all | solution.py:488
  487.0 5.3 copy-start.35
  487.0 5.3 copy-start.64
  510.7 4.0 copy-start.10
  510.7 4.0 copy-start.60
  (34 other events, 102.6 us)

commit v2 on v1

--- a/solution.py
+++ b/solution.py
@@ -13,6 +13,58 @@
 BOTH = ("section", "dp")
 MESH = pl.DeviceIdType.MESH
 PARTS = ((0, 112, "zxy"), (112, 112, "zyx"), (224, 128, "xzy"), (352, 128, "yzx"))
+
+
+def greet(total, me, peers):
+    barrier = pltpu.get_barrier_semaphore()
+
+    def one(step, carry):
+        other = lax.rem(me + step, total)
+        pl.semaphore_signal(
+            barrier, inc=1, device_id=(other // peers, lax.rem(other, peers)), device_id_type=MESH
+        )
+        return carry
+
+    lax.fori_loop(1, total, one, 0)
+    pl.semaphore_wait(barrier, total - 1)
+
+
+def share_kernel(peers, own_ref, all_ref, local_sem, send_sem, recv_sem):
+    total = 2 * peers
+    me = lax.axis_index("section") * peers + lax.axis_index("dp")
+    greet(total, me, peers)
+    keep = pltpu.make_async_copy(own_ref, all_ref.at[me], local_sem)
+    keep.start()
+
+    def one(step, carry):
+        other = lax.rem(me + step, total)
+        pltpu.make_async_remote_copy(
+            own_ref, all_ref.at[me], send_sem, recv_sem,
+            device_id=(other // peers, lax.rem(other, peers)), device_id_type=MESH,
+        ).start()
+        return carry
+
+    lax.fori_loop(1, total, one, 0)
+    rest = all_ref.at[pl.ds(0, total - 1)]
+    bulk = pltpu.make_async_remote_copy(
+        rest, rest, send_sem, recv_sem, device_id=(0, 0), device_id_type=MESH
+    )
+    bulk.wait_recv()
+    bulk.wait_send()
+    keep.wait()
+
+
+def share(own, peers):
+    vm = pl.BlockSpec(memory_space=pltpu.VMEM)
+    return pl.pallas_call(
+        functools.partial(share_kernel, peers),
+        out_shape=jax.ShapeDtypeStruct((2 * peers,) + own.shape, own.dtype),
+        in_specs=[vm],
+        out_specs=vm,
+        scratch_shapes=[pltpu.SemaphoreType.DMA, pltpu.SemaphoreType.DMA, pltpu.SemaphoreType.DMA],
+        compiler_params=pltpu.CompilerParams(collective_id=2, has_side_effects=True),
+        name="share_small",
+    )(own)
 
 
 def coords():
@@ -124,18 +176,21 @@
         compiler_params=pltpu.CompilerParams(collective_id=cid,has_side_effects=True))(x)
 
 
-def rs_kernel(parts,zn,g_ref,o_ref,land,buf,obuf,*rest):
+def rs_kernel(parts,zn,g_ref,v_ref,o_ref,vo_ref,land,buf,obuf,vland,*rest):
     nP=len(parts)
     lks=rest[:nP]
-    ssem,rsem,cs,cr,lsem,osem=rest[nP:]
+    ssem,rsem,cs,cr,lsem,osem,vsend,vrecv=rest[nP:]
     s,d,z,y,c=coords()
-    bar=pltpu.get_barrier_semaphore()
-    for cond,dev in neighbours(s,d,z,y,c,zn):
-        def sig(dev=dev): pl.semaphore_signal(bar,inc=1,device_id=dev,device_id_type=MESH)
-        sig() if cond is None else pl.when(cond)(sig)
-    inner=jnp.logical_and(z>0,z<zn-1)
-    pl.when(inner)(lambda: pl.semaphore_wait(bar,5))
-    pl.when(jnp.logical_not(inner))(lambda: pl.semaphore_wait(bar,4))
+    peers=4*zn
+    total_dev=2*peers
+    me=s*peers+d
+    greet(total_dev,me,peers)
+    vland[me]=v_ref[me]
+    def small(step,carry):
+        other=lax.rem(me+step,total_dev)
+        pltpu.make_async_remote_copy(v_ref.at[other],vland.at[me],vsend,vrecv,device_id=(other//peers,lax.rem(other,peers)),device_id_type=MESH).start()
+        return carry
+    lax.fori_loop(1,total_dev,small,0)
     sib=(s,(z*2+y)*2+1-c)
     def where(it):
         s2=1-s if it[0] else s
@@ -270,6 +325,12 @@
         guarded(conds(it),fin)
     for p,(r0,rn,_) in enumerate(parts):
         pltpu.make_async_copy(obuf.at[pl.ds(r0,rn)],o_ref.at[pl.ds(r0,rn)],osem.at[p]).wait()
+    rest_of=vland.at[pl.ds(0,total_dev-1)]
+    bulk=pltpu.make_async_remote_copy(rest_of,rest_of,vsend,vrecv,device_id=(0,0),device_id_type=MESH)
+    bulk.wait_recv()
+    bulk.wait_send()
+    vo_ref[...]=jnp.sum(vland[...],axis=0)
+
 
 def slot_count(order,zn):
     sizes={"x":2,"y":2,"z":zn};cur=0
@@ -279,125 +340,333 @@
         if dim=="z": n*=2*zn
         cur+=n
     return cur
-def rs(g,parts,zn,cid=1,nb=4):
+def rs(g,v,parts,zn,cid=1,nb=4):
     n=len(parts)
     cnt=[slot_count(p[2][::-1],zn) for p in parts]
     mx=max(p[1] for p in parts)
     return pl.pallas_call(functools.partial(rs_kernel,parts,zn),
-        out_shape=jax.ShapeDtypeStruct((480,1280),jnp.float32),
-        in_specs=[pl.BlockSpec(memory_space=pl.ANY)],out_specs=pl.BlockSpec(memory_space=pl.ANY),
-        scratch_shapes=[pltpu.VMEM((4*zn,480,1280),jnp.bfloat16),pltpu.VMEM((nb,mx,1280),jnp.bfloat16),pltpu.VMEM((480,1280),jnp.float32)]
+        out_shape=[jax.ShapeDtypeStruct((480,1280),jnp.float32),jax.ShapeDtypeStruct(v.shape[1:],jnp.float32)],
+        in_specs=[pl.BlockSpec(memory_space=pl.ANY),pl.BlockSpec(memory_space=pltpu.VMEM)],
+        out_specs=[pl.BlockSpec(memory_space=pl.ANY),pl.BlockSpec(memory_space=pltpu.VMEM)],
+        scratch_shapes=[pltpu.VMEM((4*zn,480,1280),jnp.bfloat16),pltpu.VMEM((nb,mx,1280),jnp.bfloat16),pltpu.VMEM((480,1280),jnp.float32),pltpu.VMEM(v.shape,jnp.float32)]
           +[pltpu.VMEM((cnt[p],parts[p][1],1280),jnp.bfloat16) for p in range(n)]
           +[pltpu.SemaphoreType.DMA((n,4*zn)),pltpu.SemaphoreType.DMA((sum(cnt),)),
-          pltpu.SemaphoreType.DMA((n,4*zn)),pltpu.SemaphoreType.DMA((n,4*zn)),pltpu.SemaphoreType.DMA((nb,)),pltpu.SemaphoreType.DMA((n,))],
-        compiler_params=pltpu.CompilerParams(collective_id=cid,has_side_effects=True,vmem_limit_bytes=62*2**20))(g)
-
-
-def normed(value, gain):
-    return value * lax.rsqrt(jnp.mean(value * value, axis=-1, keepdims=True) + EPS) * gain
-
-
-def mul_plain(left, right):
+          pltpu.SemaphoreType.DMA((n,4*zn)),pltpu.SemaphoreType.DMA((n,4*zn)),pltpu.SemaphoreType.DMA((nb,)),pltpu.SemaphoreType.DMA((n,)),pltpu.SemaphoreType.DMA,pltpu.SemaphoreType.DMA],
+        compiler_params=pltpu.CompilerParams(collective_id=cid,has_side_effects=True,vmem_limit_bytes=62*2**20))(g,v)
+
+
+WIN = 256
+QB = 128
+GC = 0.7978845608028654
+GA = 0.044715
+VMEM_LIMIT = 62 * 2**20
+
+
+def nn(left, right):
     return jnp.dot(left, right, preferred_element_type=jnp.float32)
 
 
-def mul_first_t(left, right):
+def nt(left, right):
+    return lax.dot_general(
+        left, right, (((1,), (1,)), ((), ())), preferred_element_type=jnp.float32
+    )
+
+
+def tn(left, right):
     return lax.dot_general(
         left, right, (((0,), (0,)), ((), ())), preferred_element_type=jnp.float32
     )
 
 
-def mul_second_t(left, right):
-    return lax.dot_general(
-        left, right, (((1,), (1,)), ((), ())), preferred_element_type=jnp.float32
-    )
-
-
-def forward_parts(inputs, segment, weights):
-    w_query, w_key, w_value, w_mix, w_inner, w_outer, gain_one, gain_two, bias_inner, bias_outer = (
-        weights
-    )
-    row_count, model_width = inputs.shape
-    depth = model_width // HEADS
+def head_window(head, depth, width):
+    start = jnp.minimum((head * depth) // 128, (width - WIN) // 128) * 128
+    start = pl.multiple_of(start, 128)
+    lane = lax.broadcasted_iota(jnp.int32, (1, WIN), 1) + (start - head * depth)
+    return start, (lane >= 0) & (lane < depth)
+
+
+def norm_rows(value, gain):
+    return value * lax.rsqrt(jnp.mean(value * value, axis=-1, keepdims=True) + EPS) * gain
+
+
+def norm_back(value, gain, down):
+    inv = lax.rsqrt(jnp.mean(value * value, axis=-1, keepdims=True) + EPS)
+    unit = value * inv
+    scaled = down * gain
+    lean = jnp.mean(scaled * unit, axis=-1, keepdims=True)
+    return inv * (scaled - unit * lean), jnp.sum(down * unit, axis=0, keepdims=True)
+
+
+def forward_kernel(
+    layer, mats_ref, x_ref, vec_ref, segc_ref, segr_ref,
+    y_ref, qkv_out, prob_out, att_out, mid_out, u_out,
+    held, qkv, prob, att, mid, u, norm, mask, sems, out_sems,
+):
+    rows, width = x_ref.shape
+    depth = width // HEADS
     scale = depth ** (-0.5)
-    first = normed(inputs, gain_one).astype(jnp.bfloat16)
-    query = mul_plain(first, w_query).astype(jnp.bfloat16)
-    keys = mul_plain(first, w_key).astype(jnp.bfloat16)
-    values = mul_plain(first, w_value).astype(jnp.bfloat16)
-    query_h = query.reshape(row_count, HEADS, depth)
-    keys_h = keys.reshape(row_count, HEADS, depth)
-    values_h = values.reshape(row_count, HEADS, depth)
-    scores = jnp.einsum("qhd,khd->hqk", query_h, keys_h, preferred_element_type=jnp.float32) * scale
-    positions = jnp.arange(row_count, dtype=jnp.int32)
-    allowed = (segment[:, None] == segment[None, :]) & (positions[None, :] <= positions[:, None])
-    scores = jnp.where(allowed[None], scores, NEG)
-    top_score = jnp.max(scores, axis=-1, keepdims=True)
-    expd = jnp.exp(scores - top_score)
-    soft = expd / jnp.sum(expd, axis=-1, keepdims=True)
-    probs = soft.astype(jnp.bfloat16)
-    attended = jnp.einsum("hqk,khd->qhd", probs, values_h, preferred_element_type=jnp.float32)
-    attended = attended.reshape(row_count, model_width).astype(jnp.bfloat16)
-    middle = inputs + mul_plain(attended, w_mix)
-    second = normed(middle, gain_two).astype(jnp.bfloat16)
-    inner = mul_plain(second, w_inner) + bias_inner
-    active = jax.nn.gelu(inner, approximate=True).astype(jnp.bfloat16)
-    output = middle + (mul_plain(active, w_outer) + bias_outer)
-    saved = (first, query_h, keys_h, values_h, soft, probs, attended, middle, second, inner, active)
-    return (output, saved)
-
-
-def layer_backward(inputs, saved, weights, cotangent):
-    w_query, w_key, w_value, w_mix, w_inner, w_outer, gain_one, gain_two, bias_inner, bias_outer = (
-        weights
-    )
-    row_count, model_width = inputs.shape
-    depth = model_width // HEADS
+
+    def weight(index):
+        return pltpu.make_async_copy(
+            mats_ref.at[layer, pl.ds(index * width, width)], held.at[index], sems.at[index]
+        )
+
+    keeps = [
+        pltpu.make_async_copy(src, dst, out_sems.at[index])
+        for index, (src, dst) in enumerate(
+            ((qkv, qkv_out), (prob, prob_out), (att, att_out), (mid, mid_out), (u, u_out))
+        )
+    ]
+    for index in range(6):
+        weight(index).start()
+    tiles = [slice(c, c + WIN) for c in range(0, width, WIN)]
+    norm[...] = norm_rows(x_ref[...].astype(jnp.float32), vec_ref[0:1, :]).astype(jnp.bfloat16)
+    qi = lax.broadcasted_iota(jnp.int32, (rows, rows), 0)
+    ki = lax.broadcasted_iota(jnp.int32, (rows, rows), 1)
+    mask[...] = jnp.where((segc_ref[...] == segr_ref[...]) & (ki <= qi), 1.0, 0.0)
+    for index in range(3):
+        weight(index).wait()
+        for cols in tiles:
+            qkv[index, :, cols] = nn(norm[...], held[index, :, cols]).astype(jnp.bfloat16)
+    keeps[0].start()
+    att[...] = jnp.zeros_like(att)
+
+    def one_head(head, carry):
+        start, lanes = head_window(head, depth, width)
+        cols = pl.ds(start, WIN)
+        for block in range(rows // QB):
+            here = slice(block * QB, (block + 1) * QB)
+            upto = slice(0, (block + 1) * QB)
+            query = jnp.where(lanes, qkv[0, here, cols], 0)
+            score = nt(query, qkv[1, upto, cols]) * scale
+            score = jnp.where(mask[here, upto] > 0.5, score, NEG)
+            expd = jnp.exp(score - jnp.max(score, axis=-1, keepdims=True))
+            soft = (expd * (1.0 / jnp.sum(expd, axis=-1, keepdims=True))).astype(jnp.bfloat16)
+            prob[head, here, upto] = soft
+            mixed = nn(soft, qkv[2, upto, cols])
+            att[here, cols] = jnp.where(lanes, mixed.astype(jnp.bfloat16), att[here, cols])
+        return carry
+
+    lax.fori_loop(0, HEADS, one_head, 0)
+    keeps[1].start()
+    keeps[2].start()
+    weight(3).wait()
+    for cols in tiles:
+        mid[:, cols] = x_ref[:, cols].astype(jnp.float32) + nn(att[...], held[3, :, cols])
+    keeps[3].start()
+    norm[...] = norm_rows(mid[...], vec_ref[1:2, :]).astype(jnp.bfloat16)
+    weight(4).wait()
+    for cols in tiles:
+        u[:, cols] = nn(norm[...], held[4, :, cols]) + vec_ref[2:3, cols]
+    keeps[4].start()
+    for cols in tiles:
+        pre = u[:, cols]
+        act = 0.5 * pre * (1.0 + jnp.tanh(GC * (pre + GA * (pre * pre * pre))))
+        norm[:, cols] = act.astype(jnp.bfloat16)
+    weight(5).wait()
+    for cols in tiles:
+        out = mid[:, cols] + (nn(norm[...], held[5, :, cols]) + vec_ref[3:4, cols])
+        y_ref[:, cols] = out.astype(jnp.bfloat16)
+    for keep in keeps:
+        keep.wait()
+
+
+def forward_layer(layer, mats, x, vec, segc, segr):
+    rows, width = x.shape
+    f32, b16 = jnp.float32, jnp.bfloat16
+    vm = pl.BlockSpec(memory_space=pltpu.VMEM)
+    hbm = pl.BlockSpec(memory_space=pl.ANY)
+    kept = [
+        ((3, rows, width), b16), ((HEADS, rows, rows), b16), ((rows, width), b16),
+        ((rows, width), f32), ((rows, width), f32),
+    ]
+    return pl.pallas_call(
+        functools.partial(forward_kernel, layer),
+        out_shape=[jax.ShapeDtypeStruct((rows, width), b16)]
+        + [jax.ShapeDtypeStruct(shape, dtype) for shape, dtype in kept],
+        in_specs=[hbm, vm, vm, vm, vm],
+        out_specs=[vm] + [hbm] * 5,
+        scratch_shapes=[pltpu.VMEM((6, width, width), b16)]
+        + [pltpu.VMEM(shape, dtype) for shape, dtype in kept]
+        + [
+            pltpu.VMEM((rows, width), b16),
+            pltpu.VMEM((rows, rows), f32),
+            pltpu.SemaphoreType.DMA((6,)),
+            pltpu.SemaphoreType.DMA((5,)),
+        ],
+        compiler_params=pltpu.CompilerParams(vmem_limit_bytes=VMEM_LIMIT),
+        name="layer_forward",
+    )(mats, x, vec, segc, segr)
+
+
+def backward_kernel(layer, aliased, *refs):
+    mats_ref, x_ref, vec_ref, dy_ref, qkv_in, prob_in, att_in, mid_in, u_in = refs[:9]
+    rest = refs[10:] if aliased else refs[9:]
+    (
+        grads_ref, dx_ref, dvec_ref,
+        held, qkv, prob, att, mid, u, act, low, wide, dmid, dqkv, dscore, turned, stage,
+        sems, in_sems, out_sems,
+    ) = rest
+    rows, width = x_ref.shape
+    depth = width // HEADS
     scale = depth ** (-0.5)
-    first, query_h, keys_h, values_h, soft, probs, attended, middle, second, inner, active = saved
-    grad_outer = cotangent.astype(jnp.bfloat16)
-    d_bias_outer = jnp.sum(grad_outer.astype(jnp.float32), axis=0)
-    d_w_outer = mul_first_t(active, grad_outer)
-    d_active = mul_second_t(grad_outer, w_outer)
-    gelu_value, gelu_back = jax.vjp(lambda pre_act: jax.nn.gelu(pre_act, approximate=True), inner)
-    d_inner = gelu_back(d_active)[0].astype(jnp.bfloat16)
-    d_bias_inner = jnp.sum(d_inner.astype(jnp.float32), axis=0)
-    d_w_inner = mul_first_t(second, d_inner)
-    d_second = mul_second_t(d_inner, w_inner)
-    norm_value, norm_back = jax.vjp(normed, middle, gain_two)
-    d_middle_norm, d_gain_two = norm_back(d_second)
-    d_middle = cotangent + d_middle_norm
-    d_branch = d_middle.astype(jnp.bfloat16)
-    d_w_mix = mul_first_t(attended, d_branch)
-    d_attended = mul_second_t(d_branch, w_mix).astype(jnp.bfloat16).reshape(row_count, HEADS, depth)
-    d_probs = jnp.einsum("qhd,khd->hqk", d_attended, values_h, preferred_element_type=jnp.float32)
-    d_values = jnp.einsum("hqk,qhd->khd", probs, d_attended, preferred_element_type=jnp.float32)
-    d_values = d_values.reshape(row_count, model_width).astype(jnp.bfloat16)
-    d_scores = (soft * (d_probs - jnp.sum(d_probs * soft, axis=-1, keepdims=True))).astype(
-        jnp.bfloat16
-    )
-    d_query = (
-        jnp.einsum("hqk,khd->qhd", d_scores, keys_h, preferred_element_type=jnp.float32) * scale
-    )
-    d_query = d_query.reshape(row_count, model_width).astype(jnp.bfloat16)
-    d_keys = (
-        jnp.einsum("hqk,qhd->khd", d_scores, query_h, preferred_element_type=jnp.float32) * scale
-    )
-    d_keys = d_keys.reshape(row_count, model_width).astype(jnp.bfloat16)
-    d_w_query = mul_first_t(first, d_query)
-    d_w_key = mul_first_t(first, d_keys)
-    d_w_value = mul_first_t(first, d_values)
-    d_first = (
-        mul_second_t(d_query, w_query)
-        + mul_second_t(d_keys, w_key)
-        + mul_second_t(d_values, w_value)
-    )
-    first_value, first_back = jax.vjp(normed, inputs, gain_one)
-    d_inputs_norm, d_gain_one = first_back(d_first)
-    d_inputs = d_middle + d_inputs_norm
-    d_mats = jnp.stack([w.astype(jnp.bfloat16) for w in (d_w_query, d_w_key, d_w_value, d_w_mix, d_w_inner, d_w_outer)])
-    d_gains = jnp.stack([d_gain_one, d_gain_two])
-    d_biases = jnp.stack([d_bias_inner, d_bias_outer])
-    return (d_inputs, d_mats, d_gains, d_biases)
+    f32, b16 = jnp.float32, jnp.bfloat16
+    tiles = [slice(c, c + WIN) for c in range(0, width, WIN)]
+
+    def weight(index):
+        return pltpu.make_async_copy(
+            mats_ref.at[layer, pl.ds(index * width, width)], held.at[index], sems.at[index]
+        )
+
+    loads = [
+        pltpu.make_async_copy(src, dst, in_sems.at[index])
+        for index, (src, dst) in enumerate(
+            ((qkv_in, qkv), (prob_in, prob), (att_in, att), (mid_in, mid), (u_in, u))
+        )
+    ]
+    loads[4].start()
+    weight(5).start()
+    weight(4).start()
+    loads[3].start()
+    weight(3).start()
+    loads[2].start()
+    loads[0].start()
+    loads[1].start()
+    for index in range(3):
+        weight(index).start()
+
+    def put(index, slot):
+        return pltpu.make_async_copy(
+            stage.at[slot], grads_ref.at[layer, pl.ds(index * width, width)], out_sems.at[index]
+        )
+
+    slots = {5: 0, 4: 1, 3: 0, 2: 1, 1: 0, 0: 1}
+    before = {3: 5, 2: 4, 1: 3, 0: 2}
+
+    def weight_grad(index, left_t, right):
+        slot = slots[index]
+        if index in before:
+            put(before[index], slot).wait()
+        for cols in tiles:
+            stage[slot, cols, :] = nn(left_t(cols), right).astype(b16)
+        put(index, slot).start()
+
+    dvec_ref[3:4, :] = jnp.sum(dy_ref[...].astype(f32), axis=0, keepdims=True)
+    loads[4].wait()
+    weight(5).wait()
+    for cols in tiles:
+        pre = u[:, cols]
+        square = pre * pre
+        bent = jnp.tanh(GC * (pre + GA * (square * pre)))
+        half = 0.5 * (1.0 + bent)
+        act[:, cols] = (pre * half).astype(b16)
+        slope = half + (0.5 * GC) * pre * (1.0 - bent * bent) * (1.0 + (3.0 * GA) * square)
+        down = nt(dy_ref[...], held[5, cols, :]) * slope
+        down = down.astype(b16)
+        low[:, cols] = down
+        dvec_ref[2:3, cols] = jnp.sum(down.astype(f32), axis=0, keepdims=True)
+    weight_grad(5, lambda cols: act[:, cols].T, dy_ref[...])
+    weight(4).wait()
+    for cols in tiles:
+        wide[:, cols] = nt(low[...], held[4, cols, :])
+    loads[3].wait()
+    act[...] = norm_rows(mid[...], vec_ref[1:2, :]).astype(b16)
+    weight_grad(4, lambda cols: act[:, cols].T, low[...])
+    part, gain_sum = norm_back(mid[...], vec_ref[1:2, :], wide[...])
+    dvec_ref[1:2, :] = gain_sum
+    total = dy_ref[...].astype(f32) + part
+    dmid[...] = total
+    low[...] = total.astype(b16)
+    loads[2].wait()
+    weight_grad(3, lambda cols: att[:, cols].T, low[...])
+    weight(3).wait()
+    for cols in tiles:
+        act[:, cols] = nt(low[...], held[3, cols, :]).astype(b16)
+    loads[0].wait()
+    loads[1].wait()
+    dqkv[...] = jnp.zeros_like(dqkv)
+
+    def one_head(head, carry):
+        start, lanes = head_window(head, depth, width)
+        cols = pl.ds(start, WIN)
+        for block in range(rows // QB):
+            here = slice(block * QB, (block + 1) * QB)
+            upto = slice(0, (block + 1) * QB)
+            down = jnp.where(lanes, act[here, cols], 0)
+            dprob = nt(down, qkv[2, upto, cols])
+            soft = prob[head, here, upto].astype(f32)
+            lean = jnp.sum(dprob * soft, axis=-1, keepdims=True)
+            ds = (soft * (dprob - lean)).astype(b16)
+            dscore[here, upto] = ds
+            dq = (nn(ds, qkv[1, upto, cols]) * scale).astype(b16)
+            dqkv[0, here, cols] = jnp.where(lanes, dq, dqkv[0, here, cols])
+        for block in range(rows // QB):
+            here = slice(block * QB, (block + 1) * QB)
+            since = slice(block * QB, rows)
+            dk = (tn(dscore[since, here], qkv[0, since, cols]) * scale).astype(b16)
+            dqkv[1, here, cols] = jnp.where(lanes, dk, dqkv[1, here, cols])
+            dv = tn(prob[head, since, here], act[since, cols]).astype(b16)
+            dqkv[2, here, cols] = jnp.where(lanes, dv, dqkv[2, here, cols])
+        return carry
+
+    lax.fori_loop(0, HEADS, one_head, 0)
+    low[...] = norm_rows(x_ref[...].astype(f32), vec_ref[0:1, :]).astype(b16)
+    for cols in tiles:
+        turned[cols, :] = low[:, cols].T
+    for index in (2, 1, 0):
+        weight_grad(index, lambda cols: turned[cols, :], dqkv[index])
+    for index in range(3):
+        weight(index).wait()
+    for cols in tiles:
+        wide[:, cols] = (
+            nt(dqkv[0], held[0, cols, :]) + nt(dqkv[1], held[1, cols, :]) + nt(dqkv[2], held[2, cols, :])
+        )
+    part, gain_sum = norm_back(x_ref[...].astype(f32), vec_ref[0:1, :], wide[...])
+    dvec_ref[0:1, :] = gain_sum
+    dvec_ref[4:8, :] = jnp.zeros_like(dvec_ref[4:8, :])
+    dx_ref[...] = (dmid[...] + part).astype(b16)
+    put(1, 0).wait()
+    put(0, 1).wait()
+
+
+def backward_layer(layer, mats, x, vec, dy, kept, grads):
+    rows, width = x.shape
+    f32, b16 = jnp.float32, jnp.bfloat16
+    vm = pl.BlockSpec(memory_space=pltpu.VMEM)
+    hbm = pl.BlockSpec(memory_space=pl.ANY)
+    aliased = grads is not None
+    return pl.pallas_call(
+        functools.partial(backward_kernel, layer, aliased),
+        out_shape=[
+            jax.ShapeDtypeStruct(mats.shape, b16),
+            jax.ShapeDtypeStruct((rows, width), b16),
+            jax.ShapeDtypeStruct((8, width), f32),
+        ],
+        in_specs=[hbm, vm, vm, vm] + [hbm] * 5 + ([hbm] if aliased else []),
+        out_specs=[hbm, vm, vm],
+        scratch_shapes=[
+            pltpu.VMEM((6, width, width), b16),
+            pltpu.VMEM((3, rows, width), b16),
+            pltpu.VMEM((HEADS, rows, rows), b16),
+            pltpu.VMEM((rows, width), b16),
+            pltpu.VMEM((rows, width), f32),
+            pltpu.VMEM((rows, width), f32),
+            pltpu.VMEM((rows, width), b16),
+            pltpu.VMEM((rows, width), b16),
+            pltpu.VMEM((rows, width), f32),
+            pltpu.VMEM((rows, width), f32),
+            pltpu.VMEM((3, rows, width), b16),
+            pltpu.VMEM((rows, rows), b16),
+            pltpu.VMEM((width, rows), b16),
+            pltpu.VMEM((2, width, width), b16),
+            pltpu.SemaphoreType.DMA((6,)),
+            pltpu.SemaphoreType.DMA((5,)),
+            pltpu.SemaphoreType.DMA((6,)),
+        ],
+        input_output_aliases={9: 0} if aliased else {},
+        compiler_params=pltpu.CompilerParams(vmem_limit_bytes=VMEM_LIMIT),
+        name="layer_backward",
+    )(*((mats, x, vec, dy) + tuple(kept) + ((grads,) if aliased else ())))
 
 
 def one_hot(rank):
@@ -407,6 +676,18 @@
 
 def rank_of(key):
     return jnp.sum((key[None, :] < key[:, None]).astype(jnp.int32), axis=1)
+
+
+def padded(flat):
+    lead, size = flat.shape
+    full = -(-size // 1024) * 1024
+    return jnp.pad(flat, ((0, 0), (0, full - size))).reshape(lead, full // 128, 128)
+
+
+def share_all(packet, peers):
+    if peers == 16:
+        return share(packet, peers)
+    return lax.all_gather(packet, BOTH, axis=0)
 
 
 def gather_weights(own, peers):
@@ -416,12 +697,13 @@
     return lax.all_gather(own, BOTH, axis=0, tiled=True).reshape(2, peers, rows, width)
 
 
-def scatter_grads(terms, peers):
+def scatter_grads(terms, small, peers):
     if peers == 16:
-        return rs(terms, PARTS, peers // 4)
+        return rs(terms, small, PARTS, peers // 4)
     sections, _, rows, width = terms.shape
     terms = terms.reshape(sections * peers * rows, width)
-    return lax.psum_scatter(terms, BOTH, scatter_dimension=0, tiled=True).astype(jnp.float32)
+    total = lax.psum_scatter(terms, BOTH, scatter_dimension=0, tiled=True).astype(jnp.float32)
+    return total, lax.psum_scatter(small, BOTH, scatter_dimension=0, tiled=True)[0]
 
 
 def local(entering, deal, seq_lens, mats, gains, biases):
@@ -431,63 +713,58 @@
     arrival = entering[0]
     batches, rows, width = arrival.shape
     per_peer = rows // peers
-    all_deal = lax.all_gather(deal, "dp", axis=1, tiled=True)
-    small = jnp.concatenate([gains[0], biases[0]]).astype(jnp.bfloat16).astype(jnp.float32)
-    small = lax.all_gather(small, BOTH, axis=0).reshape(2, peers, 2, -1)
-    small = jnp.swapaxes(small, 1, 2).reshape(2, 2, 2, width)
+    per = 2 * width // peers
+    vecs = jnp.concatenate([gains[0], biases[0]]).astype(jnp.bfloat16).astype(jnp.float32)
+    packet = jnp.concatenate([deal.reshape(-1).astype(jnp.float32), vecs])
+    shared = share_all(padded(packet[None])[0], peers).reshape(2, peers, -1)
+    all_deal = jnp.where(section == 0, shared[0, :, : batches * rows], shared[1, :, : batches * rows])
+    all_deal = all_deal.astype(jnp.int32).reshape(peers, batches, rows)
+    small = shared[:, :, batches * rows : batches * rows + 2 * per].reshape(2, peers, 2, per)
+    small = jnp.swapaxes(small, 1, 2).reshape(2, 4, width)
+    small = jnp.pad(small, ((0, 0), (0, 4), (0, 0)))
     all_mats = gather_weights(mats[0].astype(jnp.bfloat16), peers)
-    all_mats = all_mats.reshape(2, 6, width, width)
+    all_mats = all_mats.reshape(2, 6 * width, width)
     own_rows = own_dp * rows + jnp.arange(rows, dtype=jnp.int32)
-    block_ids = jnp.arange(all_deal.shape[1], dtype=jnp.int32) // rows
+    block_ids = jnp.arange(peers, dtype=jnp.int32)
     sends = []
     returns = []
     for batch in range(batches):
-        hit = all_deal[batch][None, :] == own_rows[:, None]
-        target = jnp.sum(jnp.where(hit, block_ids[None, :], 0), axis=1)
+        hit = all_deal[:, batch][None, :, :] == own_rows[:, None, None]
+        target = jnp.sum(jnp.where(hit, block_ids[None, :, None], 0), axis=(1, 2))
         key = target * rows + jnp.arange(rows, dtype=jnp.int32)
         pick = one_hot(rank_of(key))
         returns.append(pick)
-        sends.append(mul_plain(pick, arrival[batch]).astype(jnp.bfloat16))
+        sends.append(nn(pick, arrival[batch]).astype(jnp.bfloat16))
     outgoing = jnp.stack(sends).reshape(2 * peers, per_peer, width)
     arrived = lax.all_to_all(outgoing, BOTH, split_axis=0, concat_axis=0, tiled=True)
     arrived = arrived.reshape(2, rows, width)
     own_deal = jnp.where(section == 0, deal[0], deal[1])
     place = one_hot(rank_of(own_deal))
-    tokens = mul_first_t(place, arrived[0])
-    cotangent = mul_first_t(place, arrived[1])
+    tokens = tn(place, arrived[0]).astype(jnp.bfloat16)
+    cotangent = tn(place, arrived[1]).astype(jnp.bfloat16)
     lens = jnp.where(section == 0, seq_lens[0, 0], seq_lens[1, 0])
     ends = jnp.cumsum(lens)
     positions = jnp.arange(rows, dtype=jnp.int32)
     segment = jnp.sum((positions[:, None] >= ends[None, :]).astype(jnp.int32), axis=1)
-    state = tokens
-    kept = []
-    weights = []
-    for layer in range(2):
-        if layer:
-            state = state.astype(jnp.bfloat16).astype(jnp.float32)
-        mats_l = tuple(all_mats[layer, index] for index in range(6))
-        weights.append(mats_l + (small[layer, 0, 0], small[layer, 0, 1], small[layer, 1, 0], small[layer, 1, 1]))
-        out, saved = forward_parts(state, segment, weights[layer])
-        kept.append((state, saved))
-        state = out
-    final = state.astype(jnp.bfloat16)
-    grads = [None, None]
-    down = cotangent
-    for layer in (1, 0):
-        down, d_mats, d_gains, d_biases = layer_backward(kept[layer][0], kept[layer][1], weights[layer], down)
-        down = down.astype(jnp.bfloat16).astype(jnp.float32)
-        grads[layer] = (d_mats, d_gains, d_biases)
-    terms = jnp.stack([grads[0][0], grads[1][0]]).reshape(2, peers, -1, width)
-    shard_mats = scatter_grads(terms, peers)[None]
-    small_grads = jnp.stack([jnp.stack([grads[layer][1], grads[layer][2]]) for layer in range(2)])
-    small_grads = lax.psum(small_grads.reshape(2, 2, 2 * width), BOTH)
-    per = 2 * width // peers
-    mine = lax.dynamic_slice(small_grads, (section, 0, own_dp * per), (1, 2, per))
-    back = jnp.stack([mul_plain(place, down.astype(jnp.bfloat16)), mul_plain(place, final)]).astype(jnp.bfloat16)
+    middle, *kept_low = forward_layer(0, all_mats, tokens, small[0], segment[:, None], segment[None])
+    final, *kept_high = forward_layer(1, all_mats, middle, small[1], segment[:, None], segment[None])
+    terms, down, vec_high = backward_layer(1, all_mats, middle, small[1], cotangent, kept_high, None)
+    terms, down, vec_low = backward_layer(0, all_mats, tokens, small[0], down, kept_low, terms)
+    terms = terms.reshape(2, peers, -1, width)
+    vec_terms = jnp.stack([vec_low, vec_high])[:, :4].reshape(2, 2, peers, per)
+    vec_terms = padded(jnp.swapaxes(vec_terms, 1, 2).reshape(2 * peers, 2 * per))
+    shard_mats, vec_total = scatter_grads(terms, vec_terms, peers)
+    vec_total = vec_total.reshape(-1)
+    back = jnp.stack([nn(place, down), nn(place, final)]).astype(jnp.bfloat16)
     back = back.reshape(2 * peers, per_peer, width)
     returned = lax.all_to_all(back, BOTH, split_axis=0, concat_axis=0, tiled=True).reshape(2, rows, width)
-    results = jnp.stack([mul_first_t(returns[batch], returned[batch]) for batch in range(batches)])
-    return (results.astype(jnp.bfloat16)[None], shard_mats, mine[:, 0], mine[:, 1])
+    results = jnp.stack([tn(returns[batch], returned[batch]) for batch in range(batches)])
+    return (
+        results.astype(jnp.bfloat16)[None],
+        shard_mats[None],
+        vec_total[None, :per],
+        vec_total[None, per : 2 * per],
+    )
 
 
 def solution(mesh):

time: 754 us -> 576 us (0.76)
  Pallas kernels: 294 us -> 512 us
  matrix products: 218 us -> 11.1 us
  blocking collectives: 137 us -> 0 us
  other arithmetic: 60.4 us -> 26 us
  local copies, waits for them, and re-layouts: 29.7 us -> 8.88 us
    pallas_call x1 -> x6, Pallas kernels: 147 us -> 345 us  [the longest x1 166 us: rs(): pl.pallas_call(functools.partial(rs_kernel, parts, zn), out_shape=[jax.Sh...]
    dot_general x53 -> x8, matrix products: 202 us -> 11.1 us  [the longest x4 6.23 us: nn(): return jnp.dot(left, right, preferred_element_type=jnp.float32)]
    all_gather x2 -> x0, blocking collectives: 96.2 us -> none  [the longest x1 72.6 us: local(): small = lax.all_gather(small, BOTH, axis=0).reshape(2, peers, 2, -1)]
    psum x1 -> x0, blocking collectives: 40.3 us -> none  [local(): small_grads = lax.psum(small_grads.reshape(2, 2, 2 * width), BOTH)]
    another operation x11 -> x5, other arithmetic: 30 us -> 3.78 us  [the longest x1 1.44 us: local(): jnp.stack([tn(returns[batch], returned[batch]) for batch in range(batches)])]
    pallas_call x1, Pallas kernels: 147 us -> 167 us  [ag(): pl.pallas_call(functools.partial(ag_kernel, parts, zn), out_shape=jax.Sha...]
    convert_element_type x3, other arithmetic: 21.1 us -> 0.78 us  [the longest x1 0.69 us: local(): packet = jnp.concatenate([deal.reshape(-1).astype(jnp.float32), vecs])]
    convert_element_type x8 -> x2, local copies, waits for them, and re-layouts: 18 us -> 0.04 us  [the longest x1 0.03 us: local(): all_deal = all_deal.astype(jnp.int32).reshape(peers, batches, rows)]
  transfers between devices with their start and end apart: 2 -> 2, of which waited for: 0 -> 0; matrix products, arithmetic and copies ran while one was open for 9% -> 1% of each run, Pallas kernels for 39% -> 59%
where the time goes in v2:
time: 576 us; the launch traced here: 569 us
  Pallas kernels  512 us (89%)
  other arithmetic  26 us (5%)
  matrix products  11.1 us (2%)
  starting transfers between devices  9.75 us (2%)
  local copies, waits for them, and re-layouts  8.88 us (2%)
    pallas_call x1, Pallas kernels, ag(): pl.pallas_call(functools.partial(ag_kernel, parts, zn), out_shape=jax.Sha...  167 us
    pallas_call x1, Pallas kernels, rs(): pl.pallas_call(functools.partial(rs_kernel, parts, zn), out_shape=[jax.Sh...  166 us
    pallas_call x2, Pallas kernels, backward_layer(): pl.pallas_call(functools.partial(backward_kernel, layer, aliased), out_sh...  94.9 us
    pallas_call x2, Pallas kernels, forward_layer(): pl.pallas_call(functools.partial(forward_kernel, layer), out_shape=[jax.S...  69.8 us
    reduce_sum x1, other arithmetic, local(): target = jnp.sum(jnp.where(hit, block_ids[None, :, None], 0), axis=(1, 2))  16.3 us
    pallas_call x1, Pallas kernels, share(): pl.pallas_call(functools.partial(share_kernel, peers), out_shape=jax.Shap...  14.4 us
  transfers between devices with their start and end apart: 2, of which 0 were waited for; matrix products, arithmetic and copies ran while one was open for 1% of the time, Pallas kernels for 59%

profile of v2, /device:TPU:0, one launch (start us, length us, event | category | flops | bytes accessed | tf_op | source)
XLA Modules:
  0.0 569.1 jit_solution(13549615103152342300)
XLA Ops:
  0.6 0.7 convert_element_type.68
  1.3 0.7 convert_reduce_fusion.4
  2.1 0.1 maximum_convert_fusion
  2.2 0.6 pad.12
  2.8 14.4 %share_small.1 = f32[32,16,128]{2,1,0:T(8,128)} custom-call(f32[16,128]{1,0:T(8,128)} %bitcast.80), custom_call_target="tpu_custom_call" | custom-call | tf_op jit(solution)/shard_map/share_small/pallas_call | solution.py:59
  17.1 1.0 reshape.186
  18.2 0.0 copy-start.5
  18.3 16.3 %select_reduce_fusion.1 = (s32[384]{0:T(512)S(1)}, s32[384]{0:T(512)S(1)}) fusion(s32[16,384]{1,0:T(8,128)S(1)} %bitcast.77, s32[384]{0:T(512)S(1)} %iota_add_fusion.2, s32[16,384]{1,0:T(8,128)S(1)} %bitcast.76), kind=kLoop, calls=%fused_computation.1 | loop fusion | flops 14155008 | bytes 53760 | tf_op jit(solution)/shard_map/reduce_sum | solution.py:733
  34.6 0.2 convert_reduce_fusion.2
  34.8 0.2 convert_reduce_fusion
  35.0 1.9 fusion.1
  36.9 0.7 fusion
  37.6 1.4 pad_maximum_fusion
  39.0 5.6 all-to-all-start
  44.7 0.2 reduce-window.8
  44.9 0.1 convert_reduce_fusion.3
  44.9 0.5 broadcast_in_dim.62.segr_ref
  45.5 0.8 broadcast_in_dim.66.segc_ref
  46.3 0.1 reshape.189
  46.4 0.1 reshape.190
  46.5 2.8 convert_bitcast_fusion.x_ref
  49.3 167.4 %shard_map.93 = bf16[2,16,480,1280]{3,2,1,0:T(8,128)(2,1)} custom-call(bf16[480,1280]{1,0:T(8,128)(2,1)} %convert_bitcast_fusion.x_ref), custom_call_target="tpu_custom_call" | custom-call | tf_op jit(solution)/shard_map/pallas_call | solution.py:171
  216.8 0.2 convert_reduce_fusion.1
  217.0 0.6 fusion.20
  217.7 0.0 all-to-all-done
  217.7 0.1 fusion.24
  217.8 1.7 convolution_convert_fusion.4.refs_3_
  219.5 1.7 convolution_convert_fusion.5.x_ref.refs_1_
  221.2 34.8 %layer_forward.2 = (bf16[384,1280]{1,0:T(8,128)(2,1)}, bf16[3,384,1280]{2,1,0:T(8,128)(2,1)}, bf16[16,384,384]{2,1,0:T(8,128)(2,1)}, bf16[384,1280]{1,0:T(8,128)...) custom-call(bf16[2,7680,1280]{2,1,0:T(8,128)(2,1)} %bitcast.61, ...), custom_call_target="tpu_custom_call" | custom-call | tf_op jit(solution)/shard_map/layer_forward/pallas_call | solution.py:483
  256.0 35.0 %layer_forward.3 = (bf16[384,1280]{1,0:T(8,128)(2,1)}, bf16[3,384,1280]{2,1,0:T(8,128)(2,1)}, bf16[16,384,384]{2,1,0:T(8,128)(2,1)}, bf16[384,1280]{1,0:T(8,128)...) custom-call(bf16[2,7680,1280]{2,1,0:T(8,128)(2,1)} %bitcast.62, bf16[384,1280]{1,0:T(8,128)(2,1)} %get-tuple-element.24.x_ref.refs_1_, ...), custom_call_target="tpu_custom_call" | custom-call | tf_op jit(solution)/shard_map/layer_forward/pallas_call | solution.py:483
  291.0 1.9 fusion.3
  292.8 47.2 %layer_backward.2 = (bf16[2,7680,1280]{2,1,0:T(8,128)(2,1)}, bf16[384,1280]{1,0:T(8,128)(2,1)}, f32[8,1280]{1,0:T(8,128)}) custom-call(bf16[2,7680,1280]{2,1,0:T(8,128)(2,1)} %bitcast.63, bf16[384,1280]{1,0:T(8,128)(2,1)} %get-tuple-element.24.x_ref.refs_1_, f32[8,1280]{1,0:T(8,128)} %get-tuple-element.52.vec_ref.refs_2_, ...), custom_call_target="tpu_custom_call" | custom-call | tf_op jit(solution)/shard_map/layer_backward/pallas_call | solution.py:638
  340.1 47.6 %layer_backward.3 = (bf16[2,7680,1280]{2,1,0:T(8,128)(2,1)}, bf16[384,1280]{1,0:T(8,128)(2,1)}, f32[8,1280]{1,0:T(8,128)}) custom-call(bf16[2,7680,1280]{2,1,0:T(8,128)(2,1)} %bitcast.64, bf16[384,1280]{1,0:T(8,128)(2,1)} %convolution_convert_fusion.5.x_ref.refs_1_, f32[8,1280]{1,0:T(8,128)} %get-tuple-element.53.vec_ref.refs_2_, ...), custom_call_target="tpu_custom_call", output_to_operand_aliasing={{0}: (9, {})} | custom-call | tf_op jit(solution)/shard_map/layer_backward/pallas_call | solution.py:638
  387.7 1.9 fusion.2
  389.6 1.4 pad_maximum_fusion.1
  391.1 4.1 all-to-all-start.1
  395.2 0.1 reshape.193
  395.3 0.1 copy.19
  395.4 0.1 reshape.194
  395.5 0.7 copy.22
  396.2 165.9 %shard_map.94 = (f32[480,1280]{1,0:T(8,128)}, f32[8,128]{1,0:T(8,128)}) custom-call(bf16[2,16,480,1280]{3,2,1,0:T(8,128)(2,1)} %bitcast.65, f32[32,8,128]{2,1,0:T(8,128)} %bitcast.73), custom_call_target="tpu_custom_call" | custom-call | tf_op jit(solution)/shard_map/pallas_call | solution.py:347
  562.1 1.4 fusion.26
  563.5 0.1 fusion.23
  563.6 0.7 fusion.4
  564.4 0.7 fusion.5
  565.1 1.4 pad_maximum_fusion.2
  566.6 1.0 copy-done
  567.5 1.4 copy.29
  (28 shorter events, 0.2 us)
Async XLA Ops:
  18.2 18.7 %copy-start.5 = (bf16[1,2,384,1280]{3,2,1,0:T(8,128)(2,1)S(1)}, bf16[1,2,384,1280]{3,2,1,0:T(8,128)(2,1)}, u32[]{:S(2)}) copy-start(bf16[1,2,384,1280]{3,2,1,0:T(8,128)(2,1)} %param.6) | copy-start | bytes 5898244
  39.0 5.6 copy-start.4
  39.0 178.6 %all-to-all-start = ((bf16[32,24,1280]{2,1,0:T(8,128)(2,1)}), bf16[32,24,1280]{2,1,0:T(8,128)(2,1)S(1)}, u32[]{:S(2)}, u32[]{:S(2)}) async-start(bf16[32,24,1280]{2,1,0:T(8,128)(2,1)} %bitcast.66), calls=%async_computation | async-start | bytes 3932160 | tf_op jit(solution)/shard_map/all_to_all | solution.py:739
  49.3 167.4 %copy-start.3 = (s32[2,384]{1,0:T(2,128)S(1)}, s32[2,384]{1,0:T(2,128)}, u32[]{:S(2)}) copy-start(s32[2,384]{1,0:T(2,128)} %param.7) | copy-start | bytes 9220
  391.0 4.1 copy-start.1
  391.1 4.2 copy-start.2
  391.1 172.5 %all-to-all-start.1 = ((bf16[32,24,1280]{2,1,0:T(8,128)(2,1)}), bf16[32,24,1280]{2,1,0:T(8,128)(2,1)S(1)}, u32[]{:S(2)}, u32[]{:S(2)}) async-start(bf16[32,24,1280]{2,1,0:T(8,128)(2,1)} %bitcast.67), calls=%async_computation.1 | async-start | bytes 3932160 | tf_op jit(solution)/shard_map/all_to_all | solution.py:760
  565.1 2.4 copy-start

commit v3 on v2

--- a/solution.py
+++ b/solution.py
@@ -27,44 +27,6 @@
 
     lax.fori_loop(1, total, one, 0)
     pl.semaphore_wait(barrier, total - 1)
-
-
-def share_kernel(peers, own_ref, all_ref, local_sem, send_sem, recv_sem):
-    total = 2 * peers
-    me = lax.axis_index("section") * peers + lax.axis_index("dp")
-    greet(total, me, peers)
-    keep = pltpu.make_async_copy(own_ref, all_ref.at[me], local_sem)
-    keep.start()
-
-    def one(step, carry):
-        other = lax.rem(me + step, total)
-        pltpu.make_async_remote_copy(
-            own_ref, all_ref.at[me], send_sem, recv_sem,
-            device_id=(other // peers, lax.rem(other, peers)), device_id_type=MESH,
-        ).start()
-        return carry
-
-    lax.fori_loop(1, total, one, 0)
-    rest = all_ref.at[pl.ds(0, total - 1)]
-    bulk = pltpu.make_async_remote_copy(
-        rest, rest, send_sem, recv_sem, device_id=(0, 0), device_id_type=MESH
-    )
-    bulk.wait_recv()
-    bulk.wait_send()
-    keep.wait()
-
-
-def share(own, peers):
-    vm = pl.BlockSpec(memory_space=pltpu.VMEM)
-    return pl.pallas_call(
-        functools.partial(share_kernel, peers),
-        out_shape=jax.ShapeDtypeStruct((2 * peers,) + own.shape, own.dtype),
-        in_specs=[vm],
-        out_specs=vm,
-        scratch_shapes=[pltpu.SemaphoreType.DMA, pltpu.SemaphoreType.DMA, pltpu.SemaphoreType.DMA],
-        compiler_params=pltpu.CompilerParams(collective_id=2, has_side_effects=True),
-        name="share_small",
-    )(own)
 
 
 def coords():
@@ -88,92 +50,6 @@
 
 def neighbours(s,d,z,y,c,zn):
     return [(None,(1-s,d)),(None,(s,(z*2+1-y)*2+c)),(None,(s,(z*2+y)*2+1-c)),(z>0,(s,d-4)),(z<zn-1,(s,d+4))]
-
-def ag_kernel(parts,zn,x_ref,w_ref,ssem,rsem,cs,cr,lsem):
-    s,d,z,y,c=coords()
-    bar=pltpu.get_barrier_semaphore()
-    for cond,dev in neighbours(s,d,z,y,c,zn):
-        def sig(dev=dev): pl.semaphore_signal(bar,inc=1,device_id=dev,device_id_type=MESH)
-        sig() if cond is None else pl.when(cond)(sig)
-    inner=jnp.logical_and(z>0,z<zn-1)
-    pl.when(inner)(lambda: pl.semaphore_wait(bar,5))
-    pl.when(jnp.logical_not(inner))(lambda: pl.semaphore_wait(bar,4))
-    lc=pltpu.make_async_copy(x_ref,w_ref.at[s,d],lsem)
-    lc.start()
-    KIND={"x":0,"y":1,"l":2,"r":3}
-    def where(it):
-        s2=1-s if it[0] else s
-        y2=1-y if it[1] else y
-        z2=z+it[2]
-        return s2,z2,y2
-    def dsc(p,it,kind):
-        r0,rn,order=parts[p]
-        s2,z2,y2=where(it)
-        idx=s2*(2*zn)+z2*2+y2
-        own=it==(0,0,0)
-        src=x_ref.at[pl.ds(r0,rn)] if own else w_ref.at[s2,(z2*2+y2)*2+c,pl.ds(r0,rn)]
-        dst=w_ref.at[s2,(z2*2+y2)*2+c,pl.ds(r0,rn)]
-        if kind=="core":
-            dev=(s,(z*2+y)*2+1-c)
-            return pltpu.make_async_remote_copy(src,dst,cs.at[p,idx],cr.at[p,idx],device_id=dev,device_id_type=MESH)
-        dev={"x":(1-s,d),"y":(s,(z*2+1-y)*2+c),"l":(s,d-4),"r":(s,d+4)}[kind]
-        return pltpu.make_async_remote_copy(src,dst,ssem.at[KIND[kind],p,idx],rsem.at[p,idx],device_id=dev,device_id_type=MESH)
-    def cdsc(p,it):
-        r0,rn,order=parts[p]
-        s2,z2,y2=where(it)
-        idx=s2*(2*zn)+z2*2+y2
-        dst=w_ref.at[s2,(z2*2+y2)*2+1-c,pl.ds(r0,rn)]
-        return pltpu.make_async_remote_copy(dst,dst,cs.at[p,idx],cr.at[p,idx],device_id=(s,(z*2+y)*2+1-c),device_id_type=MESH)
-    def conds(it,kind):
-        cs_=[]
-        if it[2]<0: cs_.append(z+it[2]>=0)
-        if it[2]>0: cs_.append(z+it[2]<=zn-1)
-        if kind=="l": cs_.append(z>0)
-        if kind=="r": cs_.append(z<zn-1)
-        return cs_
-    def guarded(cl,fn):
-        if not cl: fn(); return
-        e=cl[0]
-        for q in cl[1:]: e=jnp.logical_and(e,q)
-        pl.when(e)(fn)
-    def sends(p,it):
-        order=parts[p][2]
-        a=arrival(order,it)
-        ks=[]
-        if a is not None and order[a]=="z": ks.append("l" if it[2]>0 else "r")
-        for dim in order[(a+1) if a is not None else 0:]:
-            ks += ["r","l"] if dim=="z" else [dim]
-        ks.append("core")
-        return ks
-    evs=[]
-    for p in range(len(parts)):
-        for it in items(): evs.append((hops(it),p,it))
-    evs.sort(key=lambda e:e[0])
-    todo=[]
-    for h,p,it in evs:
-        if abs(it[2])>zn-1: continue
-        def ev(p=p,it=it):
-            if it!=(0,0,0): dsc(p,it,"x").wait_recv()
-            for k in sends(p,it):
-                guarded([q for q in conds((0,0,0),k)], lambda k=k: dsc(p,it,k).start())
-        guarded(conds(it,None),ev)
-        todo.append((p,it))
-    for p,it in todo:
-        def fin(p=p,it=it):
-            cdsc(p,it).wait_recv()
-            for k in sends(p,it):
-                guarded(conds((0,0,0),k), lambda k=k: dsc(p,it,k).wait_send())
-        guarded(conds(it,None),fin)
-    lc.wait()
-
-def ag(x,parts,zn,cid=0):
-    n=len(parts)
-    return pl.pallas_call(functools.partial(ag_kernel,parts,zn),
-        out_shape=jax.ShapeDtypeStruct((2,4*zn,480,1280),jnp.bfloat16),
-        in_specs=[pl.BlockSpec(memory_space=pl.ANY)],out_specs=pl.BlockSpec(memory_space=pl.ANY),
-        scratch_shapes=[pltpu.SemaphoreType.DMA((4,n,4*zn)),pltpu.SemaphoreType.DMA((n,4*zn)),
-          pltpu.SemaphoreType.DMA((n,4*zn)),pltpu.SemaphoreType.DMA((n,4*zn)),pltpu.SemaphoreType.DMA],
-        compiler_params=pltpu.CompilerParams(collective_id=cid,has_side_effects=True))(x)
 
 
 def rs_kernel(parts,zn,g_ref,v_ref,o_ref,vo_ref,land,buf,obuf,vland,*rest):
@@ -669,6 +545,241 @@
     )(*((mats, x, vec, dy) + tuple(kept) + ((grads,) if aliased else ())))
 
 
+def as_row(column):
+    rows = column.shape[0]
+    return jnp.broadcast_to(column, (rows, 128)).T[0:1, :]
+
+
+def as_column(row):
+    size = row.shape[1]
+    return jnp.broadcast_to(row, (128, size)).T[:, 0:1]
+
+
+def ones_where(flag):
+    return jnp.where(flag, 1.0, 0.0)
+
+
+def gather_events(parts,zn,place,own,w_ref,ssem,rsem,cs,cr):
+    s,d,z,y,c=place
+    KIND={"x":0,"y":1,"l":2,"r":3}
+    def where(it):
+        s2=1-s if it[0] else s
+        y2=1-y if it[1] else y
+        z2=z+it[2]
+        return s2,z2,y2
+    def dsc(p,it,kind):
+        r0,rn,order=parts[p]
+        s2,z2,y2=where(it)
+        idx=s2*(2*zn)+z2*2+y2
+        is_own=it==(0,0,0)
+        src=own.at[pl.ds(r0,rn)] if is_own else w_ref.at[s2,(z2*2+y2)*2+c,pl.ds(r0,rn)]
+        dst=w_ref.at[s2,(z2*2+y2)*2+c,pl.ds(r0,rn)]
+        if kind=="core":
+            dev=(s,(z*2+y)*2+1-c)
+            return pltpu.make_async_remote_copy(src,dst,cs.at[p,idx],cr.at[p,idx],device_id=dev,device_id_type=MESH)
+        dev={"x":(1-s,d),"y":(s,(z*2+1-y)*2+c),"l":(s,d-4),"r":(s,d+4)}[kind]
+        return pltpu.make_async_remote_copy(src,dst,ssem.at[KIND[kind],p,idx],rsem.at[p,idx],device_id=dev,device_id_type=MESH)
+    def cdsc(p,it):
+        r0,rn,order=parts[p]
+        s2,z2,y2=where(it)
+        idx=s2*(2*zn)+z2*2+y2
+        dst=w_ref.at[s2,(z2*2+y2)*2+1-c,pl.ds(r0,rn)]
+        return pltpu.make_async_remote_copy(dst,dst,cs.at[p,idx],cr.at[p,idx],device_id=(s,(z*2+y)*2+1-c),device_id_type=MESH)
+    def conds(it,kind):
+        cs_=[]
+        if it[2]<0: cs_.append(z+it[2]>=0)
+        if it[2]>0: cs_.append(z+it[2]<=zn-1)
+        if kind=="l": cs_.append(z>0)
+        if kind=="r": cs_.append(z<zn-1)
+        return cs_
+    def guarded(cl,fn):
+        if not cl: fn(); return
+        e=cl[0]
+        for q in cl[1:]: e=jnp.logical_and(e,q)
+        pl.when(e)(fn)
+    def sends(p,it):
+        order=parts[p][2]
+        a=arrival(order,it)
+        ks=[]
+        if a is not None and order[a]=="z": ks.append("l" if it[2]>0 else "r")
+        for dim in order[(a+1) if a is not None else 0:]:
+            ks += ["r","l"] if dim=="z" else [dim]
+        ks.append("core")
+        return ks
+    evs=[]
+    for p in range(len(parts)):
+        for it in items():
+            if abs(it[2])<zn: evs.append((hops(it),p,it))
+    evs.sort(key=lambda e:e[0])
+    first=[]
+    later=[]
+    for h,p,it in evs:
+        def ev(p=p,it=it):
+            if it!=(0,0,0): dsc(p,it,"x").wait_recv()
+            for k in sends(p,it):
+                guarded(conds((0,0,0),k), lambda k=k: dsc(p,it,k).start())
+        (later if h else first).append(lambda it=it,ev=ev: guarded(conds(it,None),ev))
+    def finish():
+        for _,p,it in evs:
+            def fin(p=p,it=it):
+                cdsc(p,it).wait_recv()
+                for k in sends(p,it):
+                    guarded(conds((0,0,0),k), lambda k=k: dsc(p,it,k).wait_send())
+            guarded(conds(it,None),fin)
+    return first,later,finish
+
+
+def enter_kernel(
+    parts, zn, mats_ref, packet_ref, deal_ref, tokens_ref,
+    w_ref, shared_ref, x_ref, cot_ref, picks_ref, place_ref,
+    own, wide_rows, strips32, sendbuf, landed, order,
+    own_sem, lsem, ssem, rsem, cs, cr, psend, precv, tsend, trecv,
+):
+    s, d, z, y, c = coords()
+    peers = 4 * zn
+    total = 2 * peers
+    me = s * peers + d
+    batches, rows, width = tokens_ref.shape
+    per_peer = rows // peers
+    strips = width // 128
+    f32, b16 = jnp.float32, jnp.bfloat16
+    cast_in = pltpu.make_async_copy(mats_ref, wide_rows, own_sem)
+    cast_in.start()
+    greet(total, me, peers)
+    shared_ref[me] = packet_ref[...]
+
+    def tell(step, carry):
+        other = lax.rem(me + step, total)
+        pltpu.make_async_remote_copy(
+            packet_ref, shared_ref.at[me], psend, precv,
+            device_id=(other // peers, lax.rem(other, peers)), device_id_type=MESH,
+        ).start()
+        return carry
+
+    lax.fori_loop(1, total, tell, 0)
+    cast_in.wait()
+    own[...] = wide_rows[...].astype(b16)
+    lc = pltpu.make_async_copy(own, w_ref.at[s, d], lsem)
+    lc.start()
+    start_events, rest_events, finish = gather_events(
+        parts, zn, (s, d, z, y, c), own, w_ref, ssem, rsem, cs, cr
+    )
+    for event in start_events:
+        event()
+    sub = lax.broadcasted_iota(jnp.int32, (rows, rows), 0).astype(f32)
+    lane = lax.broadcasted_iota(jnp.int32, (rows, rows), 1).astype(f32)
+    mine_row = jnp.where(s == 0, deal_ref[0:1, :], deal_ref[1:2, :])
+    mine_col = as_column(mine_row)
+    rank_col = jnp.sum(ones_where(mine_row < mine_col), axis=1, keepdims=True)
+    order[...] = ones_where(lane == rank_col).astype(b16)
+    rank_row = jnp.sum(ones_where(mine_col < mine_row), axis=0, keepdims=True)
+    place_ref[...] = ones_where(sub == rank_row).astype(b16)
+    rest = shared_ref.at[pl.ds(0, total - 1)]
+    bulk = pltpu.make_async_remote_copy(
+        rest, rest, psend, precv, device_id=(0, 0), device_id_type=MESH
+    )
+    bulk.wait_recv()
+    index_col = lax.broadcasted_iota(jnp.int32, (rows, 1), 0).astype(f32)
+    ids_col = index_col + (d * rows).astype(f32)
+    for batch in range(batches):
+
+        def look(block, found):
+            known = shared_ref[s * peers + block]
+            for line in range(rows // 128):
+                at = batch * (rows // 128) + line
+                found = jnp.where(ids_col == known[at : at + 1, :], block.astype(f32), found)
+            return found
+
+        found = lax.fori_loop(0, peers, look, jnp.zeros((rows, 128), f32))
+        key_col = jnp.sum(found, axis=1, keepdims=True) * rows + index_col
+        key_row = as_row(key_col)
+        rank_row = jnp.sum(ones_where(key_col < key_row), axis=0, keepdims=True)
+        rank_col = jnp.sum(ones_where(key_row < key_col), axis=1, keepdims=True)
+        picks_ref[batch] = ones_where(lane == rank_col).astype(b16)
+        pick = ones_where(sub == rank_row).astype(b16)
+        for strip in range(strips):
+            part = nn(pick, tokens_ref[batch, :, strip * 128 : (strip + 1) * 128])
+            strips32[:, strip * per_peer : (strip + 1) * per_peer, :] = part.reshape(peers, per_peer, 128)
+        sendbuf[batch] = strips32[...].astype(b16)
+
+    landed[me] = sendbuf[s, d]
+
+    def give(step, carry):
+        other = lax.rem(me + step, total)
+        sec, dp = other // peers, lax.rem(other, peers)
+        pltpu.make_async_remote_copy(
+            sendbuf.at[sec, dp], landed.at[me], tsend, trecv.at[s],
+            device_id=(sec, dp), device_id_type=MESH,
+        ).start()
+        return carry
+
+    lax.fori_loop(1, total, give, 0)
+    for event in rest_events:
+        event()
+
+    def take(kind, out_ref):
+        def wait(count):
+            some = landed.at[pl.ds(0, count)]
+            pltpu.make_async_remote_copy(
+                some, some, tsend, trecv.at[kind], device_id=(0, 0), device_id_type=MESH
+            ).wait_recv()
+
+        pl.when(s == kind)(lambda: wait(peers - 1))
+        pl.when(s != kind)(lambda: wait(peers))
+        strips32[...] = landed[pl.ds(kind * peers, peers)].astype(f32)
+        for strip in range(strips):
+            part = strips32[:, strip * per_peer : (strip + 1) * per_peer, :].reshape(rows, 128)
+            out_ref[:, strip * 128 : (strip + 1) * 128] = nn(order[...], part.astype(b16)).astype(b16)
+
+    take(0, x_ref)
+    take(1, cot_ref)
+    finish()
+    lc.wait()
+    bulk.wait_send()
+    most = landed.at[pl.ds(0, total - 1)]
+    pltpu.make_async_remote_copy(
+        most, most, tsend, trecv.at[0], device_id=(0, 0), device_id_type=MESH
+    ).wait_send()
+
+
+def enter(mats, packet, deal, tokens, parts, zn):
+    n = len(parts)
+    peers = 4 * zn
+    batches, rows, width = tokens.shape
+    strip_rows = rows // peers * (width // 128)
+    f32, b16 = jnp.float32, jnp.bfloat16
+    vm = pl.BlockSpec(memory_space=pltpu.VMEM)
+    hbm = pl.BlockSpec(memory_space=pl.ANY)
+    dma = pltpu.SemaphoreType.DMA
+    return pl.pallas_call(
+        functools.partial(enter_kernel, parts, zn),
+        out_shape=[
+            jax.ShapeDtypeStruct((2, peers) + mats.shape, b16),
+            jax.ShapeDtypeStruct((2 * peers,) + packet.shape, f32),
+            jax.ShapeDtypeStruct((rows, width), b16),
+            jax.ShapeDtypeStruct((rows, width), b16),
+            jax.ShapeDtypeStruct((batches, rows, rows), b16),
+            jax.ShapeDtypeStruct((rows, rows), b16),
+        ],
+        in_specs=[hbm, vm, vm, vm],
+        out_specs=[hbm, vm, vm, vm, vm, vm],
+        scratch_shapes=[
+            pltpu.VMEM(mats.shape, b16),
+            pltpu.VMEM(mats.shape, f32),
+            pltpu.VMEM((peers, strip_rows, 128), f32),
+            pltpu.VMEM((batches, peers, strip_rows, 128), b16),
+            pltpu.VMEM((2 * peers, strip_rows, 128), b16),
+            pltpu.VMEM((rows, rows), b16),
+            dma, dma, dma((4, n, peers)), dma((n, peers)), dma((n, peers)), dma((n, peers)),
+            dma, dma, dma, dma((2,)),
+        ],
+        compiler_params=pltpu.CompilerParams(
+            collective_id=0, has_side_effects=True, vmem_limit_bytes=VMEM_LIMIT
+        ),
+        name="enter",
+    )(mats, packet, deal, tokens)
+
+
 def one_hot(rank):
     rows = rank.shape[0]
     return (rank[None, :] == jnp.arange(rows, dtype=jnp.int32)[:, None]).astype(jnp.bfloat16)
@@ -684,17 +795,31 @@
     return jnp.pad(flat, ((0, 0), (0, full - size))).reshape(lead, full // 128, 128)
 
 
-def share_all(packet, peers):
-    if peers == 16:
-        return share(packet, peers)
-    return lax.all_gather(packet, BOTH, axis=0)
-
-
-def gather_weights(own, peers):
-    if peers == 16:
-        return ag(own, PARTS, peers // 4)
-    rows, width = own.shape
-    return lax.all_gather(own, BOTH, axis=0, tiled=True).reshape(2, peers, rows, width)
+def enter_plain(own, packet, deal, tokens, peers):
+    section = lax.axis_index("section")
+    batches, rows, width = tokens.shape
+    per_peer = rows // peers
+    shared = lax.all_gather(packet, BOTH, axis=0)
+    low = own.astype(jnp.bfloat16)
+    mats = lax.all_gather(low, BOTH, axis=0, tiled=True).reshape((2, peers) + own.shape)
+    flat = shared.reshape(2, peers, -1)[:, :, : batches * rows]
+    dealt = jnp.where(section == 0, flat[0], flat[1]).astype(jnp.int32).reshape(peers, batches, rows)
+    own_rows = lax.axis_index("dp") * rows + jnp.arange(rows, dtype=jnp.int32)
+    blocks = jnp.arange(peers, dtype=jnp.int32)
+    picks = []
+    sends = []
+    for batch in range(batches):
+        hit = dealt[:, batch][None, :, :] == own_rows[:, None, None]
+        target = jnp.sum(jnp.where(hit, blocks[None, :, None], 0), axis=(1, 2))
+        pick = one_hot(rank_of(target * rows + jnp.arange(rows, dtype=jnp.int32)))
+        picks.append(pick.T)
+        sends.append(nn(pick, tokens[batch]).astype(jnp.bfloat16))
+    outgoing = jnp.stack(sends).reshape(2 * peers, per_peer, width)
+    arrived = lax.all_to_all(outgoing, BOTH, split_axis=0, concat_axis=0, tiled=True)
+    arrived = arrived.reshape(2, rows, width)
+    place = one_hot(rank_of(jnp.where(section == 0, deal[0], deal[1])))
+    x, cot = (tn(place, arrived[kind]).astype(jnp.bfloat16) for kind in range(2))
+    return mats, shared, x, cot, jnp.stack(picks), place
 
 
 def scatter_grads(terms, small, peers):
@@ -708,7 +833,6 @@
 
 def local(entering, deal, seq_lens, mats, gains, biases):
     section = lax.axis_index("section")
-    own_dp = lax.axis_index("dp")
     peers = lax.axis_size("dp")
     arrival = entering[0]
     batches, rows, width = arrival.shape
@@ -716,32 +840,16 @@
     per = 2 * width // peers
     vecs = jnp.concatenate([gains[0], biases[0]]).astype(jnp.bfloat16).astype(jnp.float32)
     packet = jnp.concatenate([deal.reshape(-1).astype(jnp.float32), vecs])
-    shared = share_all(padded(packet[None])[0], peers).reshape(2, peers, -1)
-    all_deal = jnp.where(section == 0, shared[0, :, : batches * rows], shared[1, :, : batches * rows])
-    all_deal = all_deal.astype(jnp.int32).reshape(peers, batches, rows)
+    packet = padded(packet[None])[0]
+    packet = jnp.pad(packet, ((0, -packet.shape[0] % 8), (0, 0)))
+    args = (mats[0], packet, deal.astype(jnp.float32), arrival)
+    entered = enter(*args, PARTS, peers // 4) if peers == 16 else enter_plain(*args, peers)
+    all_mats, shared, tokens, cotangent, returns, place = entered
+    shared = shared.reshape(2, peers, -1)
     small = shared[:, :, batches * rows : batches * rows + 2 * per].reshape(2, peers, 2, per)
     small = jnp.swapaxes(small, 1, 2).reshape(2, 4, width)
     small = jnp.pad(small, ((0, 0), (0, 4), (0, 0)))
-    all_mats = gather_weights(mats[0].astype(jnp.bfloat16), peers)
     all_mats = all_mats.reshape(2, 6 * width, width)
-    own_rows = own_dp * rows + jnp.arange(rows, dtype=jnp.int32)
-    block_ids = jnp.arange(peers, dtype=jnp.int32)
-    sends = []
-    returns = []
-    for batch in range(batches):
-        hit = all_deal[:, batch][None, :, :] == own_rows[:, None, None]
-        target = jnp.sum(jnp.where(hit, block_ids[None, :, None], 0), axis=(1, 2))
-        key = target * rows + jnp.arange(rows, dtype=jnp.int32)
-        pick = one_hot(rank_of(key))
-        returns.append(pick)
-        sends.append(nn(pick, arrival[batch]).astype(jnp.bfloat16))
-    outgoing = jnp.stack(sends).reshape(2 * peers, per_peer, width)
-    arrived = lax.all_to_all(outgoing, BOTH, split_axis=0, concat_axis=0, tiled=True)
-    arrived = arrived.reshape(2, rows, width)
-    own_deal = jnp.where(section == 0, deal[0], deal[1])
-    place = one_hot(rank_of(own_deal))
-    tokens = tn(place, arrived[0]).astype(jnp.bfloat16)
-    cotangent = tn(place, arrived[1]).astype(jnp.bfloat16)
     lens = jnp.where(section == 0, seq_lens[0, 0], seq_lens[1, 0])
     ends = jnp.cumsum(lens)
     positions = jnp.arange(rows, dtype=jnp.int32)
@@ -758,7 +866,7 @@
     back = jnp.stack([nn(place, down), nn(place, final)]).astype(jnp.bfloat16)
     back = back.reshape(2 * peers, per_peer, width)
     returned = lax.all_to_all(back, BOTH, split_axis=0, concat_axis=0, tiled=True).reshape(2, rows, width)
-    results = jnp.stack([tn(returns[batch], returned[batch]) for batch in range(batches)])
+    results = jnp.stack([nn(returns[batch], returned[batch]) for batch in range(batches)])
     return (
         results.astype(jnp.bfloat16)[None],
         shard_mats[None],

time: 576 us -> 543 us (0.943)
  other arithmetic: 26 us -> 5.32 us
  starting transfers between devices: 9.75 us -> 3.52 us
  matrix products: 11.1 us -> 5.11 us
    reduce_sum x4 -> x0, other arithmetic: 17 us -> none  [the longest x1 16.3 us: local(): target = jnp.sum(jnp.where(hit, block_ids[None, :, None], 0), axis=(1, 2))]
    pallas_call x2 -> x1, Pallas kernels: 182 us -> 183 us  [enter(): pl.pallas_call(functools.partial(enter_kernel, parts, zn), out_shape=[jax...]
  transfers between devices with their start and end apart: 2 -> 1, of which waited for: 0 -> 0; matrix products, arithmetic and copies ran while one was open for 1% -> 0% of each run, Pallas kernels for 59% -> 31%
where the time goes in v3:
time: 543 us; the launch traced here: 538 us
  Pallas kernels  514 us (95%)
  local copies, waits for them, and re-layouts  9.66 us (2%)
    pallas_call x1, Pallas kernels, enter(): pl.pallas_call(functools.partial(enter_kernel, parts, zn), out_shape=[jax...  183 us
    pallas_call x1, Pallas kernels, rs(): pl.pallas_call(functools.partial(rs_kernel, parts, zn), out_shape=[jax.Sh...  166 us
    pallas_call x2, Pallas kernels, backward_layer(): pl.pallas_call(functools.partial(backward_kernel, layer, aliased), out_sh...  94.9 us
    pallas_call x2, Pallas kernels, forward_layer(): pl.pallas_call(functools.partial(forward_kernel, layer), out_shape=[jax.S...  69.5 us
  transfers between devices with their start and end apart: 1, of which 0 were waited for; matrix products, arithmetic and copies ran while one was open for 0% of the time, Pallas kernels for 31%

profile of v3, /device:TPU:0, one launch (start us, length us, event | category | flops | bytes accessed | tf_op | source)
XLA Modules:
  0.0 538.4 jit_solution(13695475300273910342)
XLA Ops:
  0.6 0.7 fusion.10
  1.3 0.2 reduce-window.8
  1.5 0.1 convert_reduce_fusion
  1.6 0.6 broadcast_in_dim.25.segr_ref
  2.2 0.8 broadcast_in_dim.29.segc_ref
  3.0 0.7 convert_element_type.33.deal_ref
  3.6 0.0 copy-start.5
  3.7 0.7 convert_reduce_fusion.1
  4.4 0.1 maximum_convert_fusion
  4.5 0.6 pad.12
  5.1 0.0 copy-done.5
  5.1 183.4 %enter.1 = (bf16[2,16,480,1280]{3,2,1,0:T(8,128)(2,1)}, f32[32,16,128]{2,1,0:T(8,128)}, bf16[384,1280]{1,0:T(8,128)(2,1)}, bf16[384,1280]{1,0:T(8,128)(2,1)}, bf...) custom-call(f32[480,1280]{1,0:T(8,128)} %bitcast.56, f32[16,128]{1,0:T(8,128)} %bitcast.64, f32[2,384]{1,0:T(2,128)} %copy-done.5, ...), custom_call_target="tpu_custom_call" | custom-call | tf_op jit(solution)/shard_map/enter/pallas_call | solution.py:754
  188.5 1.0 reshape.120
  189.5 0.1 reshape.121
  189.6 0.1 reshape.122
  189.7 0.6 fusion.9
  190.4 34.7 %layer_forward.2 = (bf16[384,1280]{1,0:T(8,128)(2,1)}, bf16[3,384,1280]{2,1,0:T(8,128)(2,1)}, bf16[16,384,384]{2,1,0:T(8,128)(2,1)}, bf16[384,1280]{1,0:T(8,128)...) custom-call(bf16[2,7680,1280]{2,1,0:T(8,128)(2,1)} %bitcast.48, bf16[384,1280]{1,0:T(8,128)(2,1)} %get-tuple-element.33.x_ref.refs_1_, ...), custom_call_target="tpu_custom_call" | custom-call | tf_op jit(solution)/shard_map/layer_forward/pallas_call | solution.py:359
  225.1 0.0 copy-start.1
  225.1 34.8 %layer_forward.3 = (bf16[384,1280]{1,0:T(8,128)(2,1)}, bf16[3,384,1280]{2,1,0:T(8,128)(2,1)}, bf16[16,384,384]{2,1,0:T(8,128)(2,1)}, bf16[384,1280]{1,0:T(8,128)...) custom-call(bf16[2,7680,1280]{2,1,0:T(8,128)(2,1)} %bitcast.49, bf16[384,1280]{1,0:T(8,128)(2,1)} %get-tuple-element.35.x_ref.refs_1_, ...), custom_call_target="tpu_custom_call" | custom-call | tf_op jit(solution)/shard_map/layer_forward/pallas_call | solution.py:359
  259.9 0.0 copy-done.1
  259.9 1.9 fusion.1
  261.8 47.5 %layer_backward.2 = (bf16[2,7680,1280]{2,1,0:T(8,128)(2,1)}, bf16[384,1280]{1,0:T(8,128)(2,1)}, f32[8,1280]{1,0:T(8,128)}) custom-call(bf16[2,7680,1280]{2,1,0:T(8,128)(2,1)} %bitcast.50, bf16[384,1280]{1,0:T(8,128)(2,1)} %get-tuple-element.35.x_ref.refs_1_, f32[8,1280]{1,0:T(8,128)} %get-tuple-element.58.vec_ref.refs_2_, ...), custom_call_target="tpu_custom_call" | custom-call | tf_op jit(solution)/shard_map/layer_backward/pallas_call | solution.py:514
  309.3 47.4 %layer_backward.3 = (bf16[2,7680,1280]{2,1,0:T(8,128)(2,1)}, bf16[384,1280]{1,0:T(8,128)(2,1)}, f32[8,1280]{1,0:T(8,128)}) custom-call(bf16[2,7680,1280]{2,1,0:T(8,128)(2,1)} %bitcast.51, bf16[384,1280]{1,0:T(8,128)(2,1)} %get-tuple-element.33.x_ref.refs_1_, f32[8,1280]{1,0:T(8,128)} %get-tuple-element.59.vec_ref.refs_2_, ...), custom_call_target="tpu_custom_call", output_to_operand_aliasing={{0}: (9, {})} | custom-call | tf_op jit(solution)/shard_map/layer_backward/pallas_call | solution.py:514
  356.7 1.9 fusion
  358.6 1.4 pad_maximum_fusion
  360.0 0.0 copy-start.3
  360.0 0.0 copy-start.4
  360.0 3.5 all-to-all-start
  363.6 0.0 copy-done.3
  363.6 0.0 copy-done.4
  363.6 0.1 reshape.125
  363.7 0.1 copy.19
  363.8 0.1 reshape.126
  363.9 0.7 copy.20
  364.6 165.9 %shard_map.93 = (f32[480,1280]{1,0:T(8,128)}, f32[8,128]{1,0:T(8,128)}) custom-call(bf16[2,16,480,1280]{3,2,1,0:T(8,128)(2,1)} %bitcast.52, f32[32,8,128]{2,1,0:T(8,128)} %bitcast.59), custom_call_target="tpu_custom_call" | custom-call | tf_op jit(solution)/shard_map/pallas_call | solution.py:223
  530.5 1.4 fusion.12
  531.9 0.0 copy-start.2
  531.9 0.0 all-to-all-done
  531.9 0.1 fusion.11
  532.0 0.9 copy-done.2
  532.9 0.7 fusion.2
  533.6 0.7 fusion.3
  534.3 0.0 copy-start
  534.3 1.4 pad_maximum_fusion.1
  535.7 1.0 copy-done
  536.7 1.4 copy.23
  (7 shorter events, 0.1 us)
Async XLA Ops:
  3.6 1.4 copy-start.5
  225.1 34.9 %copy-start.1 = (bf16[384,384]{1,0:T(8,128)(2,1)S(1)}, bf16[384,384]{1,0:T(8,128)(2,1)}, u32[]{:S(2)}) copy-start(bf16[384,384]{1,0:T(8,128)(2,1)} %get-tuple-element.31) | copy-start | bytes 884740
  360.0 3.5 copy-start.3
  360.0 3.5 copy-start.4
  360.0 171.8 %all-to-all-start = ((bf16[32,24,1280]{2,1,0:T(8,128)(2,1)}), bf16[32,24,1280]{2,1,0:T(8,128)(2,1)S(1)}, u32[]{:S(2)}, u32[]{:S(2)}) async-start(bf16[32,24,1280]{2,1,0:T(8,128)(2,1)} %bitcast.53), calls=%async_computation | async-start | bytes 3932160 | tf_op jit(solution)/shard_map/all_to_all | solution.py:868
  531.9 1.1 copy-start.2
  534.3 2.4 copy-start

commit v4 on v3

--- a/solution.py
+++ b/solution.py
@@ -233,6 +233,9 @@
 
 WIN = 256
 QB = 128
+GROUP = 4
+LOG2E = 1.4426950408889634
+LN2 = 0.6931471805599453
 GC = 0.7978845608028654
 GA = 0.044715
 VMEM_LIMIT = 62 * 2**20
@@ -299,31 +302,40 @@
     norm[...] = norm_rows(x_ref[...].astype(jnp.float32), vec_ref[0:1, :]).astype(jnp.bfloat16)
     qi = lax.broadcasted_iota(jnp.int32, (rows, rows), 0)
     ki = lax.broadcasted_iota(jnp.int32, (rows, rows), 1)
-    mask[...] = jnp.where((segc_ref[...] == segr_ref[...]) & (ki <= qi), 1.0, 0.0)
+    mask[...] = jnp.where((segc_ref[...] == segr_ref[...]) & (ki <= qi), 3e38, NEG)
     for index in range(3):
         weight(index).wait()
         for cols in tiles:
-            qkv[index, :, cols] = nn(norm[...], held[index, :, cols]).astype(jnp.bfloat16)
+            part = nn(norm[...], held[index, :, cols])
+            if index == 0:
+                part = part * (scale * LOG2E)
+            qkv[index, :, cols] = part.astype(jnp.bfloat16)
     keeps[0].start()
     att[...] = jnp.zeros_like(att)
 
-    def one_head(head, carry):
-        start, lanes = head_window(head, depth, width)
-        cols = pl.ds(start, WIN)
-        for block in range(rows // QB):
-            here = slice(block * QB, (block + 1) * QB)
-            upto = slice(0, (block + 1) * QB)
-            query = jnp.where(lanes, qkv[0, here, cols], 0)
-            score = nt(query, qkv[1, upto, cols]) * scale
-            score = jnp.where(mask[here, upto] > 0.5, score, NEG)
-            expd = jnp.exp(score - jnp.max(score, axis=-1, keepdims=True))
-            soft = (expd * (1.0 / jnp.sum(expd, axis=-1, keepdims=True))).astype(jnp.bfloat16)
+    def head_group(group, carry):
+        blocks = range(rows // QB)
+        heres = [slice(block * QB, (block + 1) * QB) for block in blocks]
+        uptos = [slice(0, (block + 1) * QB) for block in blocks]
+        work = []
+        for k in range(GROUP):
+            head = group * GROUP + k
+            start, lanes = head_window(head, depth, width)
+            work += [(head, pl.ds(start, WIN), lanes, heres[b], uptos[b]) for b in blocks]
+        scores = [nt(jnp.where(lanes, qkv[0, here, cols], 0), qkv[1, upto, cols]) for head, cols, lanes, here, upto in work]
+        scores = [jnp.minimum(score, mask[w[3], w[4]]) for score, w in zip(scores, work)]
+        tops = [jnp.max(score, axis=-1, keepdims=True) for score in scores]
+        expds = [jnp.exp2(score - top) for score, top in zip(scores, tops)]
+        sums = [1.0 / jnp.sum(e, axis=-1, keepdims=True) for e in expds]
+        softs = [(e * r).astype(jnp.bfloat16) for e, r in zip(expds, sums)]
+        for soft, (head, cols, lanes, here, upto) in zip(softs, work):
             prob[head, here, upto] = soft
-            mixed = nn(soft, qkv[2, upto, cols])
-            att[here, cols] = jnp.where(lanes, mixed.astype(jnp.bfloat16), att[here, cols])
+        mixes = [nn(soft, qkv[2, w[4], w[1]]).astype(jnp.bfloat16) for soft, w in zip(softs, work)]
+        for mixed, (head, cols, lanes, here, upto) in zip(mixes, work):
+            att[here, cols] = jnp.where(lanes, mixed, att[here, cols])
         return carry
 
-    lax.fori_loop(0, HEADS, one_head, 0)
+    lax.fori_loop(0, HEADS // GROUP, head_group, 0)
     keeps[1].start()
     keeps[2].start()
     weight(3).wait()
@@ -462,30 +474,31 @@
     loads[1].wait()
     dqkv[...] = jnp.zeros_like(dqkv)
 
-    def one_head(head, carry):
-        start, lanes = head_window(head, depth, width)
-        cols = pl.ds(start, WIN)
-        for block in range(rows // QB):
-            here = slice(block * QB, (block + 1) * QB)
-            upto = slice(0, (block + 1) * QB)
-            down = jnp.where(lanes, act[here, cols], 0)
-            dprob = nt(down, qkv[2, upto, cols])
-            soft = prob[head, here, upto].astype(f32)
-            lean = jnp.sum(dprob * soft, axis=-1, keepdims=True)
-            ds = (soft * (dprob - lean)).astype(b16)
-            dscore[here, upto] = ds
-            dq = (nn(ds, qkv[1, upto, cols]) * scale).astype(b16)
-            dqkv[0, here, cols] = jnp.where(lanes, dq, dqkv[0, here, cols])
-        for block in range(rows // QB):
-            here = slice(block * QB, (block + 1) * QB)
-            since = slice(block * QB, rows)
-            dk = (tn(dscore[since, here], qkv[0, since, cols]) * scale).astype(b16)
-            dqkv[1, here, cols] = jnp.where(lanes, dk, dqkv[1, here, cols])
-            dv = tn(prob[head, since, here], act[since, cols]).astype(b16)
-            dqkv[2, here, cols] = jnp.where(lanes, dv, dqkv[2, here, cols])
+    def head_group(group, carry):
+        blocks = range(rows // QB)
+        heres = [slice(block * QB, (block + 1) * QB) for block in blocks]
+        uptos = [slice(0, (block + 1) * QB) for block in blocks]
+        sinces = [slice(block * QB, rows) for block in blocks]
+        work = []
+        for k in range(GROUP):
+            head = group * GROUP + k
+            start, lanes = head_window(head, depth, width)
+            work += [(head, pl.ds(start, WIN), lanes, heres[b], uptos[b], sinces[b], k) for b in blocks]
+        dprobs = [nt(jnp.where(w[2], act[w[3], w[1]], 0), qkv[2, w[4], w[1]]) for w in work]
+        softs = [prob[w[0], w[3], w[4]].astype(f32) for w in work]
+        leans = [jnp.sum(dp * soft, axis=-1, keepdims=True) for dp, soft in zip(dprobs, softs)]
+        dss = [(soft * (dp - lean)).astype(b16) for dp, soft, lean in zip(dprobs, softs, leans)]
+        for ds, w in zip(dss, work):
+            dscore[w[6], w[3], w[4]] = ds
+        dvs = [tn(prob[w[0], w[5], w[3]], act[w[5], w[1]]).astype(b16) for w in work]
+        dqs = [(nn(ds, qkv[1, w[4], w[1]]) * scale).astype(b16) for ds, w in zip(dss, work)]
+        dks = [(tn(dscore[w[6], w[5], w[3]], qkv[0, w[5], w[1]]) * LN2).astype(b16) for w in work]
+        for dq, dk, dv, w in zip(dqs, dks, dvs, work):
+            for index, value in enumerate((dq, dk, dv)):
+                dqkv[index, w[3], w[1]] = jnp.where(w[2], value, dqkv[index, w[3], w[1]])
         return carry
 
-    lax.fori_loop(0, HEADS, one_head, 0)
+    lax.fori_loop(0, HEADS // GROUP, head_group, 0)
     low[...] = norm_rows(x_ref[...].astype(f32), vec_ref[0:1, :]).astype(b16)
     for cols in tiles:
         turned[cols, :] = low[:, cols].T
@@ -532,7 +545,7 @@
             pltpu.VMEM((rows, width), f32),
             pltpu.VMEM((rows, width), f32),
             pltpu.VMEM((3, rows, width), b16),
-            pltpu.VMEM((rows, rows), b16),
+            pltpu.VMEM((GROUP, rows, rows), b16),
             pltpu.VMEM((width, rows), b16),
             pltpu.VMEM((2, width, width), b16),
             pltpu.SemaphoreType.DMA((6,)),

time: 543 us -> 488 us (0.90)
  Pallas kernels: 514 us -> 459 us
    pallas_call x2, Pallas kernels: 69.5 us -> 38.1 us  [forward_layer(): pl.pallas_call(functools.partial(forward_kernel, layer), out_shape=[jax.S...]
    pallas_call x2, Pallas kernels: 94.9 us -> 71.7 us  [backward_layer(): pl.pallas_call(functools.partial(backward_kernel, layer, aliased), out_sh...]
  transfers between devices with their start and end apart: 1 -> 1, of which waited for: 0 -> 0; matrix products, arithmetic and copies ran while one was open for 0% -> 0% of each run, Pallas kernels for 31% -> 34%
where the time goes in v4:
time: 488 us; the launch traced here: 484 us
  Pallas kernels  459 us (94%)
  local copies, waits for them, and re-layouts  9.66 us (2%)
  other arithmetic  5.32 us (1%)
  matrix products  5.1 us (1%)
    pallas_call x1, Pallas kernels, enter(): pl.pallas_call(functools.partial(enter_kernel, parts, zn), out_shape=[jax...  183 us
    pallas_call x1, Pallas kernels, rs(): pl.pallas_call(functools.partial(rs_kernel, parts, zn), out_shape=[jax.Sh...  166 us
    pallas_call x2, Pallas kernels, backward_layer(): pl.pallas_call(functools.partial(backward_kernel, layer, aliased), out_sh...  71.7 us
    pallas_call x2, Pallas kernels, forward_layer(): pl.pallas_call(functools.partial(forward_kernel, layer), out_shape=[jax.S...  38.1 us
  transfers between devices with their start and end apart: 1, of which 0 were waited for; matrix products, arithmetic and copies ran while one was open for 0% of the time, Pallas kernels for 34%

profile of v4, /device:TPU:0, one launch (start us, length us, event | category | flops | bytes accessed | tf_op | source)
XLA Modules:
  0.0 483.7 jit_solution(13553063488943448944)
XLA Ops:
  0.6 0.7 fusion.10
  1.3 0.2 reduce-window.8
  1.5 0.1 convert_reduce_fusion
  1.6 0.6 broadcast_in_dim.25.segr_ref
  2.2 0.8 broadcast_in_dim.29.segc_ref
  3.0 0.7 convert_element_type.33.deal_ref
  3.6 0.0 copy-start.5
  3.7 0.7 convert_reduce_fusion.1
  4.4 0.1 maximum_convert_fusion
  4.5 0.6 pad.12
  5.1 0.0 copy-done.5
  5.1 183.4 %enter.1 = (bf16[2,16,480,1280]{3,2,1,0:T(8,128)(2,1)}, f32[32,16,128]{2,1,0:T(8,128)}, bf16[384,1280]{1,0:T(8,128)(2,1)}, bf16[384,1280]{1,0:T(8,128)(2,1)}, bf...) custom-call(f32[480,1280]{1,0:T(8,128)} %bitcast.56, f32[16,128]{1,0:T(8,128)} %bitcast.64, f32[2,384]{1,0:T(2,128)} %copy-done.5, ...), custom_call_target="tpu_custom_call" | custom-call | tf_op jit(solution)/shard_map/enter/pallas_call | solution.py:767
  188.5 1.0 reshape.120
  189.5 0.1 reshape.121
  189.6 0.1 reshape.122
  189.7 0.6 fusion.9
  190.4 18.9 %layer_forward.2 = (bf16[384,1280]{1,0:T(8,128)(2,1)}, bf16[3,384,1280]{2,1,0:T(8,128)(2,1)}, bf16[16,384,384]{2,1,0:T(8,128)(2,1)}, bf16[384,1280]{1,0:T(8,128)...) custom-call(bf16[2,7680,1280]{2,1,0:T(8,128)(2,1)} %bitcast.48, bf16[384,1280]{1,0:T(8,128)(2,1)} %get-tuple-element.33.x_ref.refs_1_, ...), custom_call_target="tpu_custom_call" | custom-call | tf_op jit(solution)/shard_map/layer_forward/pallas_call | solution.py:371
  209.2 0.0 copy-start.1
  209.3 19.2 %layer_forward.3 = (bf16[384,1280]{1,0:T(8,128)(2,1)}, bf16[3,384,1280]{2,1,0:T(8,128)(2,1)}, bf16[16,384,384]{2,1,0:T(8,128)(2,1)}, bf16[384,1280]{1,0:T(8,128)...) custom-call(bf16[2,7680,1280]{2,1,0:T(8,128)(2,1)} %bitcast.49, bf16[384,1280]{1,0:T(8,128)(2,1)} %get-tuple-element.35.x_ref.refs_1_, ...), custom_call_target="tpu_custom_call" | custom-call | tf_op jit(solution)/shard_map/layer_forward/pallas_call | solution.py:371
  228.4 0.0 copy-done.1
  228.5 1.9 fusion.1
  230.3 35.6 %layer_backward.2 = (bf16[2,7680,1280]{2,1,0:T(8,128)(2,1)}, bf16[384,1280]{1,0:T(8,128)(2,1)}, f32[8,1280]{1,0:T(8,128)}) custom-call(bf16[2,7680,1280]{2,1,0:T(8,128)(2,1)} %bitcast.50, bf16[384,1280]{1,0:T(8,128)(2,1)} %get-tuple-element.35.x_ref.refs_1_, f32[8,1280]{1,0:T(8,128)} %get-tuple-element.58.vec_ref.refs_2_, ...), custom_call_target="tpu_custom_call" | custom-call | tf_op jit(solution)/shard_map/layer_backward/pallas_call | solution.py:527
  266.0 36.0 %layer_backward.3 = (bf16[2,7680,1280]{2,1,0:T(8,128)(2,1)}, bf16[384,1280]{1,0:T(8,128)(2,1)}, f32[8,1280]{1,0:T(8,128)}) custom-call(bf16[2,7680,1280]{2,1,0:T(8,128)(2,1)} %bitcast.51, bf16[384,1280]{1,0:T(8,128)(2,1)} %get-tuple-element.33.x_ref.refs_1_, f32[8,1280]{1,0:T(8,128)} %get-tuple-element.59.vec_ref.refs_2_, ...), custom_call_target="tpu_custom_call", output_to_operand_aliasing={{0}: (9, {})} | custom-call | tf_op jit(solution)/shard_map/layer_backward/pallas_call | solution.py:527
  302.0 1.9 fusion
  303.9 1.4 pad_maximum_fusion
  305.3 0.0 copy-start.3
  305.3 0.0 copy-start.4
  305.3 3.5 all-to-all-start
  308.9 0.0 copy-done.3
  308.9 0.0 copy-done.4
  308.9 0.1 reshape.125
  309.0 0.1 copy.19
  309.1 0.1 reshape.126
  309.2 0.7 copy.20
  309.9 165.9 %shard_map.93 = (f32[480,1280]{1,0:T(8,128)}, f32[8,128]{1,0:T(8,128)}) custom-call(bf16[2,16,480,1280]{3,2,1,0:T(8,128)(2,1)} %bitcast.52, f32[32,8,128]{2,1,0:T(8,128)} %bitcast.59), custom_call_target="tpu_custom_call" | custom-call | tf_op jit(solution)/shard_map/pallas_call | solution.py:223
  475.8 1.4 fusion.12
  477.2 0.0 copy-start.2
  477.2 0.0 all-to-all-done
  477.2 0.1 fusion.11
  477.3 0.9 copy-done.2
  478.2 0.7 fusion.2
  478.9 0.7 fusion.3
  479.6 0.0 copy-start
  479.6 1.4 pad_maximum_fusion.1
  481.0 1.0 copy-done
  482.0 1.4 copy.23
  (7 shorter events, 0.1 us)
Async XLA Ops:
  3.6 1.4 copy-start.5
  209.2 19.2 %copy-start.1 = (bf16[384,384]{1,0:T(8,128)(2,1)S(1)}, bf16[384,384]{1,0:T(8,128)(2,1)}, u32[]{:S(2)}) copy-start(bf16[384,384]{1,0:T(8,128)(2,1)} %get-tuple-element.31) | copy-start | bytes 884740
  305.3 3.5 copy-start.3
  305.3 3.5 copy-start.4
  305.3 171.8 %all-to-all-start = ((bf16[32,24,1280]{2,1,0:T(8,128)(2,1)}), bf16[32,24,1280]{2,1,0:T(8,128)(2,1)S(1)}, u32[]{:S(2)}, u32[]{:S(2)}) async-start(bf16[32,24,1280]{2,1,0:T(8,128)(2,1)} %bitcast.53), calls=%async_computation | async-start | bytes 3932160 | tf_op jit(solution)/shard_map/all_to_all | solution.py:881
  477.2 1.1 copy-start.2
  479.6 2.4 copy-start

commit v5 on v4

v5 whole, which is shorter than its diff:
```python
import functools

import jax
import jax.numpy as jnp
from jax import lax
from jax.experimental import pallas as pl
from jax.experimental.pallas import tpu as pltpu
from jax.sharding import PartitionSpec as P

HEADS = 16
EPS = 1e-06
NEG = -1000000000.0
BOTH = ("section", "dp")
MESH = pl.DeviceIdType.MESH
PARTS = ((0, 112, "zxy"), (112, 112, "zyx"), (224, 128, "xzy"), (352, 128, "yzx"))


WIN = 256
QB = 128
GROUP = 4
LOG2E = 1.4426950408889634
LN2 = 0.6931471805599453
GC = 0.7978845608028654
GA = 0.044715
VMEM_LIMIT = 62 * 2**20


def nn(left, right):
    return jnp.dot(left, right, preferred_element_type=jnp.float32)


def nt(left, right):
    return lax.dot_general(
        left, right, (((1,), (1,)), ((), ())), preferred_element_type=jnp.float32
    )


def tn(left, right):
    return lax.dot_general(
        left, right, (((0,), (0,)), ((), ())), preferred_element_type=jnp.float32
    )


def head_window(head, depth, width):
    start = jnp.minimum((head * depth) // 128, (width - WIN) // 128) * 128
    start = pl.multiple_of(start, 128)
    lane = lax.broadcasted_iota(jnp.int32, (1, WIN), 1) + (start - head * depth)
    return start, (lane >= 0) & (lane < depth)


def norm_rows(value, gain):
    return value * lax.rsqrt(jnp.mean(value * value, axis=-1, keepdims=True) + EPS) * gain


def norm_back(value, gain, down):
    inv = lax.rsqrt(jnp.mean(value * value, axis=-1, keepdims=True) + EPS)
    unit = value * inv
    scaled = down * gain
    lean = jnp.mean(scaled * unit, axis=-1, keepdims=True)
    return inv * (scaled - unit * lean), jnp.sum(down * unit, axis=0, keepdims=True)


def signal_all(total, me, peers):
    barrier = pltpu.get_barrier_semaphore()

    def one(step, carry):
        other = lax.rem(me + step, total)
        pl.semaphore_signal(
            barrier, inc=1, device_id=(other // peers, lax.rem(other, peers)), device_id_type=MESH
        )
        return carry

    lax.fori_loop(1, total, one, 0)


def wait_all(total):
    pl.semaphore_wait(pltpu.get_barrier_semaphore(), total - 1)


def greet(total, me, peers):
    signal_all(total, me, peers)
    wait_all(total)


def cut_strips(pick, source, strips32):
    peers = strips32.shape[0]
    strips = source.shape[-1] // 128
    each = strips32.shape[1] // strips
    for strip in range(strips):
        part = nn(pick, source[:, strip * 128 : (strip + 1) * 128])
        strips32[:, strip * each : (strip + 1) * each, :] = part.reshape(peers, each, 128)


def join_strips(order, strips32, out_ref):
    peers = strips32.shape[0]
    strips = out_ref.shape[-1] // 128
    each = strips32.shape[1] // strips
    for strip in range(strips):
        part = strips32[:, strip * each : (strip + 1) * each, :].reshape(peers * each, 128)
        part = nn(order, part.astype(jnp.bfloat16)).astype(jnp.bfloat16)
        out_ref[:, strip * 128 : (strip + 1) * 128] = part


def bulk_copy(ref, count, send_sem, recv_sem):
    some = ref.at[pl.ds(0, count)]
    return pltpu.make_async_remote_copy(
        some, some, send_sem, recv_sem, device_id=(0, 0), device_id_type=MESH
    )


def coords():
    s=lax.axis_index("section"); d=lax.axis_index("dp")
    return s,d,d//4,(d//2)%2,d%2

def items():
    out=[]
    for bx in (0,1):
        for by in (0,1):
            for dz in (0,-1,1,-2,2,-3,3):
                out.append((bx,by,dz))
    return out
def hops(it): return it[0]+it[1]+abs(it[2])
def arrival(order,it):
    diff={"x":it[0]!=0,"y":it[1]!=0,"z":it[2]!=0}
    last=None
    for k,dim in enumerate(order):
        if diff[dim]: last=k
    return last

def neighbours(s,d,z,y,c,zn):
    return [(None,(1-s,d)),(None,(s,(z*2+1-y)*2+c)),(None,(s,(z*2+y)*2+1-c)),(z>0,(s,d-4)),(z<zn-1,(s,d+4))]


def forward_kernel(layer, peers, *refs):
    mats_ref, x_ref, vec_ref, segc_ref, segr_ref = refs[:5]
    if peers:
        give_ref, order_ref = refs[5:7]
        cot_ref = refs[13]
        landed, strips32, send_sem, recv_sem = refs[-4:]
        refs = refs[:5] + refs[7:13] + refs[14:-4]
        s, d = lax.axis_index("section"), lax.axis_index("dp")
        total, me = 2 * peers, s * peers + d
        signal_all(total, me, peers)
    y_ref, qkv_out, prob_out, att_out, mid_out, u_out = refs[5:11]
    held, qkv, prob, att, mid, u, norm, mask, sems, out_sems = refs[11:]
    rows, width = x_ref.shape
    depth = width // HEADS
    scale = depth ** (-0.5)

    def weight(index):
        return pltpu.make_async_copy(
            mats_ref.at[layer, pl.ds(index * width, width)], held.at[index], sems.at[index]
        )

    keeps = [
        pltpu.make_async_copy(src, dst, out_sems.at[index])
        for index, (src, dst) in enumerate(
            ((qkv, qkv_out), (prob, prob_out), (att, att_out), (mid, mid_out), (u, u_out))
        )
    ]
    for index in range(6):
        weight(index).start()
    tiles = [slice(c, c + WIN) for c in range(0, width, WIN)]
    norm[...] = norm_rows(x_ref[...].astype(jnp.float32), vec_ref[0:1, :]).astype(jnp.bfloat16)
    qi = lax.broadcasted_iota(jnp.int32, (rows, rows), 0)
    ki = lax.broadcasted_iota(jnp.int32, (rows, rows), 1)
    mask[...] = jnp.where((segc_ref[...] == segr_ref[...]) & (ki <= qi), 3e38, NEG)
    for index in range(3):
        weight(index).wait()
        for cols in tiles:
            part = nn(norm[...], held[index, :, cols])
            if index == 0:
                part = part * (scale * LOG2E)
            qkv[index, :, cols] = part.astype(jnp.bfloat16)
    keeps[0].start()
    if peers:
        wait_all(total)

        @pl.when(s == 1)
        def _():
            landed[d] = give_ref[1, d]

            def give(step, carry):
                other = lax.rem(me + step, total)
                sec, dp = other // peers, lax.rem(other, peers)
                pltpu.make_async_remote_copy(
                    give_ref.at[sec, dp], landed.at[d], send_sem, recv_sem,
                    device_id=(sec, dp), device_id_type=MESH,
                ).start()
                return carry

            lax.fori_loop(1, total, give, 0)

    att[...] = jnp.zeros_like(att)

    def head_group(group, carry):
        blocks = range(rows // QB)
        heres = [slice(block * QB, (block + 1) * QB) for block in blocks]
        uptos = [slice(0, (block + 1) * QB) for block in blocks]
        work = []
        for k in range(GROUP):
            head = group * GROUP + k
            start, lanes = head_window(head, depth, width)
            work += [(head, pl.ds(start, WIN), lanes, heres[b], uptos[b]) for b in blocks]
        scores = [nt(jnp.where(lanes, qkv[0, here, cols], 0), qkv[1, upto, cols]) for head, cols, lanes, here, upto in work]
        scores = [jnp.minimum(score, mask[w[3], w[4]]) for score, w in zip(scores, work)]
        tops = [jnp.max(score, axis=-1, keepdims=True) for score in scores]
        expds = [jnp.exp2(score - top) for score, top in zip(scores, tops)]
        sums = [1.0 / jnp.sum(e, axis=-1, keepdims=True) for e in expds]
        softs = [(e * r).astype(jnp.bfloat16) for e, r in zip(expds, sums)]
        for soft, (head, cols, lanes, here, upto) in zip(softs, work):
            prob[head, here, upto] = soft
        mixes = [nn(soft, qkv[2, w[4], w[1]]).astype(jnp.bfloat16) for soft, w in zip(softs, work)]
        for mixed, (head, cols, lanes, here, upto) in zip(mixes, work):
            att[here, cols] = jnp.where(lanes, mixed, att[here, cols])
        return carry

    lax.fori_loop(0, HEADS // GROUP, head_group, 0)
    keeps[1].start()
    keeps[2].start()
    weight(3).wait()
    for cols in tiles:
        mid[:, cols] = x_ref[:, cols].astype(jnp.float32) + nn(att[...], held[3, :, cols])
    keeps[3].start()
    norm[...] = norm_rows(mid[...], vec_ref[1:2, :]).astype(jnp.bfloat16)
    weight(4).wait()
    for cols in tiles:
        u[:, cols] = nn(norm[...], held[4, :, cols]) + vec_ref[2:3, cols]
    keeps[4].start()
    for cols in tiles:
        pre = u[:, cols]
        act = 0.5 * pre * (1.0 + jnp.tanh(GC * (pre + GA * (pre * pre * pre))))
        norm[:, cols] = act.astype(jnp.bfloat16)
    weight(5).wait()
    for cols in tiles:
        out = mid[:, cols] + (nn(norm[...], held[5, :, cols]) + vec_ref[3:4, cols])
        y_ref[:, cols] = out.astype(jnp.bfloat16)
    if peers:
        pl.when(s == 1)(lambda: bulk_copy(landed, peers - 1, send_sem, recv_sem).wait_recv())
        pl.when(s != 1)(lambda: bulk_copy(landed, peers, send_sem, recv_sem).wait_recv())
        strips32[...] = landed[...].astype(jnp.float32)
        join_strips(order_ref[...], strips32, cot_ref)

        @pl.when(s == 1)
        def _():
            bulk_copy(give_ref.at[0], peers, send_sem, recv_sem).wait_send()
            bulk_copy(give_ref.at[0], peers - 1, send_sem, recv_sem).wait_send()

    for keep in keeps:
        keep.wait()


def forward_layer(layer, mats, x, vec, segc, segr, trade=None):
    rows, width = x.shape
    f32, b16 = jnp.float32, jnp.bfloat16
    vm = pl.BlockSpec(memory_space=pltpu.VMEM)
    hbm = pl.BlockSpec(memory_space=pl.ANY)
    kept = [
        ((3, rows, width), b16), ((HEADS, rows, rows), b16), ((rows, width), b16),
        ((rows, width), f32), ((rows, width), f32),
    ]
    peers = trade[0].shape[1] if trade else 0
    block = trade[0].shape[1:] if trade else None
    dma = pltpu.SemaphoreType.DMA
    return pl.pallas_call(
        functools.partial(forward_kernel, layer, peers),
        out_shape=[jax.ShapeDtypeStruct((rows, width), b16)]
        + [jax.ShapeDtypeStruct(shape, dtype) for shape, dtype in kept]
        + [jax.ShapeDtypeStruct((rows, width), b16)] * bool(trade),
        in_specs=[hbm, vm, vm, vm, vm] + [vm, vm] * bool(trade),
        out_specs=[vm] + [hbm] * 5 + [vm] * bool(trade),
        scratch_shapes=[pltpu.VMEM((6, width, width), b16)]
        + [pltpu.VMEM(shape, dtype) for shape, dtype in kept]
        + [
            pltpu.VMEM((rows, width), b16),
            pltpu.VMEM((rows, rows), f32),
            dma((6,)),
            dma((5,)),
        ]
        + ([pltpu.VMEM(block, b16), pltpu.VMEM(block, f32), dma, dma] if trade else []),
        compiler_params=pltpu.CompilerParams(
            vmem_limit_bytes=VMEM_LIMIT,
            **(dict(collective_id=3, has_side_effects=True) if trade else {}),
        ),
        name="layer_forward",
    )(mats, x, vec, segc, segr, *(trade or ()))


def give_back(to, s, d, me, peers, sendbuf, returned, local_sem, send_sem, recv_sem):
    keep = pltpu.make_async_copy(sendbuf.at[d], returned.at[me], local_sem)
    pl.when(s == to)(lambda: keep.start())

    def give(step, carry):
        dp = lax.rem(d + step, peers)
        pltpu.make_async_remote_copy(
            sendbuf.at[dp], returned.at[me], send_sem, recv_sem,
            device_id=(to, dp), device_id_type=MESH,
        ).start()
        return carry

    @pl.when(s != to)
    def _():
        give(0, 0)

    lax.fori_loop(1, peers, give, 0)

    def finish():
        @pl.when(s == to)
        def _():
            keep.wait()
            bulk_copy(returned, 2 * peers - 1, send_sem, recv_sem).wait_recv()
            bulk_copy(sendbuf, peers - 1, send_sem, recv_sem).wait_send()

        pl.when(s != to)(lambda: bulk_copy(sendbuf, peers, send_sem, recv_sem).wait_send())

    return finish


def backward_kernel(layer, aliased, peers, *refs):
    if peers:
        final_ref, place_ref = refs[9:11]
        returned = refs[14]
        strips32, sendbuf, local_sem, send_sem, recv_sem = refs[-5:]
        refs = refs[:9] + refs[11:14] + refs[15:-5]
        s, d = lax.axis_index("section"), lax.axis_index("dp")
        total, me = 2 * peers, s * peers + d
        signal_all(total, me, peers)
    mats_ref, x_ref, vec_ref, dy_ref, qkv_in, prob_in, att_in, mid_in, u_in = refs[:9]
    rest = refs[10:] if aliased else refs[9:]
    (
        grads_ref, dx_ref, dvec_ref,
        held, qkv, prob, att, mid, u, act, low, wide, dmid, dqkv, dscore, turned, stage,
        sems, in_sems, out_sems,
    ) = rest
    rows, width = x_ref.shape
    depth = width // HEADS
    scale = depth ** (-0.5)
    f32, b16 = jnp.float32, jnp.bfloat16
    tiles = [slice(c, c + WIN) for c in range(0, width, WIN)]

    def weight(index):
        return pltpu.make_async_copy(
            mats_ref.at[layer, pl.ds(index * width, width)], held.at[index], sems.at[index]
        )

    loads = [
        pltpu.make_async_copy(src, dst, in_sems.at[index])
        for index, (src, dst) in enumerate(
            ((qkv_in, qkv), (prob_in, prob), (att_in, att), (mid_in, mid), (u_in, u))
        )
    ]
    loads[4].start()
    weight(5).start()
    weight(4).start()
    loads[3].start()
    weight(3).start()
    loads[2].start()
    loads[0].start()
    loads[1].start()
    for index in range(3):
        weight(index).start()

    if peers:
        cut_strips(place_ref[...], final_ref, strips32)
        sendbuf[...] = strips32[...].astype(b16)
        wait_all(total)
        back = give_back(1, s, d, me, peers, sendbuf, returned, local_sem, send_sem, recv_sem)

    def put(index, slot):
        return pltpu.make_async_copy(
            stage.at[slot], grads_ref.at[layer, pl.ds(index * width, width)], out_sems.at[index]
        )

    slots = {5: 0, 4: 1, 3: 0, 2: 1, 1: 0, 0: 1}
    before = {3: 5, 2: 4, 1: 3, 0: 2}

    def weight_grad(index, left_t, right):
        slot = slots[index]
        if index in before:
            put(before[index], slot).wait()
        for cols in tiles:
            stage[slot, cols, :] = nn(left_t(cols), right).astype(b16)
        put(index, slot).start()

    dvec_ref[3:4, :] = jnp.sum(dy_ref[...].astype(f32), axis=0, keepdims=True)
    loads[4].wait()
    weight(5).wait()
    for cols in tiles:
        pre = u[:, cols]
        square = pre * pre
        bent = jnp.tanh(GC * (pre + GA * (square * pre)))
        half = 0.5 * (1.0 + bent)
        act[:, cols] = (pre * half).astype(b16)
        slope = half + (0.5 * GC) * pre * (1.0 - bent * bent) * (1.0 + (3.0 * GA) * square)
        down = nt(dy_ref[...], held[5, cols, :]) * slope
        down = down.astype(b16)
        low[:, cols] = down
        dvec_ref[2:3, cols] = jnp.sum(down.astype(f32), axis=0, keepdims=True)
    weight_grad(5, lambda cols: act[:, cols].T, dy_ref[...])
    weight(4).wait()
    for cols in tiles:
        wide[:, cols] = nt(low[...], held[4, cols, :])
    loads[3].wait()
    act[...] = norm_rows(mid[...], vec_ref[1:2, :]).astype(b16)
    weight_grad(4, lambda cols: act[:, cols].T, low[...])
    part, gain_sum = norm_back(mid[...], vec_ref[1:2, :], wide[...])
    dvec_ref[1:2, :] = gain_sum
    total = dy_ref[...].astype(f32) + part
    dmid[...] = total
    low[...] = total.astype(b16)
    loads[2].wait()
    weight_grad(3, lambda cols: att[:, cols].T, low[...])
    weight(3).wait()
    for cols in tiles:
        act[:, cols] = nt(low[...], held[3, cols, :]).astype(b16)
    loads[0].wait()
    loads[1].wait()
    dqkv[...] = jnp.zeros_like(dqkv)

    def head_group(group, carry):
        blocks = range(rows // QB)
        heres = [slice(block * QB, (block + 1) * QB) for block in blocks]
        uptos = [slice(0, (block + 1) * QB) for block in blocks]
        sinces = [slice(block * QB, rows) for block in blocks]
        work = []
        for k in range(GROUP):
            head = group * GROUP + k
            start, lanes = head_window(head, depth, width)
            work += [(head, pl.ds(start, WIN), lanes, heres[b], uptos[b], sinces[b], k) for b in blocks]
        dprobs = [nt(jnp.where(w[2], act[w[3], w[1]], 0), qkv[2, w[4], w[1]]) for w in work]
        softs = [prob[w[0], w[3], w[4]].astype(f32) for w in work]
        leans = [jnp.sum(dp * soft, axis=-1, keepdims=True) for dp, soft in zip(dprobs, softs)]
        dss = [(soft * (dp - lean)).astype(b16) for dp, soft, lean in zip(dprobs, softs, leans)]
        for ds, w in zip(dss, work):
            dscore[w[6], w[3], w[4]] = ds
        dvs = [tn(prob[w[0], w[5], w[3]], act[w[5], w[1]]).astype(b16) for w in work]
        dqs = [(nn(ds, qkv[1, w[4], w[1]]) * scale).astype(b16) for ds, w in zip(dss, work)]
        dks = [(tn(dscore[w[6], w[5], w[3]], qkv[0, w[5], w[1]]) * LN2).astype(b16) for w in work]
        for dq, dk, dv, w in zip(dqs, dks, dvs, work):
            for index, value in enumerate((dq, dk, dv)):
                dqkv[index, w[3], w[1]] = jnp.where(w[2], value, dqkv[index, w[3], w[1]])
        return carry

    lax.fori_loop(0, HEADS // GROUP, head_group, 0)
    low[...] = norm_rows(x_ref[...].astype(f32), vec_ref[0:1, :]).astype(b16)
    for cols in tiles:
        turned[cols, :] = low[:, cols].T
    for index in (2, 1, 0):
        weight_grad(index, lambda cols: turned[cols, :], dqkv[index])
    for index in range(3):
        weight(index).wait()
    for cols in tiles:
        wide[:, cols] = (
            nt(dqkv[0], held[0, cols, :]) + nt(dqkv[1], held[1, cols, :]) + nt(dqkv[2], held[2, cols, :])
        )
    part, gain_sum = norm_back(x_ref[...].astype(f32), vec_ref[0:1, :], wide[...])
    dvec_ref[0:1, :] = gain_sum
    dvec_ref[4:8, :] = jnp.zeros_like(dvec_ref[4:8, :])
    dx_ref[...] = (dmid[...] + part).astype(b16)
    put(1, 0).wait()
    put(0, 1).wait()
    if peers:
        back()


def backward_layer(layer, mats, x, vec, dy, kept, grads, trade=None):
    rows, width = x.shape
    f32, b16 = jnp.float32, jnp.bfloat16
    vm = pl.BlockSpec(memory_space=pltpu.VMEM)
    hbm = pl.BlockSpec(memory_space=pl.ANY)
    aliased = grads is not None
    peers, block = (trade[2], trade[3]) if trade else (0, None)
    dma = pltpu.SemaphoreType.DMA
    return pl.pallas_call(
        functools.partial(backward_kernel, layer, aliased, peers),
        out_shape=[
            jax.ShapeDtypeStruct(mats.shape, b16),
            jax.ShapeDtypeStruct((rows, width), b16),
            jax.ShapeDtypeStruct((8, width), f32),
        ]
        + ([jax.ShapeDtypeStruct((2 * peers,) + block, b16)] if trade else []),
        in_specs=[hbm, vm, vm, vm] + [hbm] * 5 + ([hbm] if aliased else []) + [vm, vm] * bool(trade),
        out_specs=[hbm, vm, vm] + [hbm] * bool(trade),
        scratch_shapes=[
            pltpu.VMEM((6, width, width), b16),
            pltpu.VMEM((3, rows, width), b16),
            pltpu.VMEM((HEADS, rows, rows), b16),
            pltpu.VMEM((rows, width), b16),
            pltpu.VMEM((rows, width), f32),
            pltpu.VMEM((rows, width), f32),
            pltpu.VMEM((rows, width), b16),
            pltpu.VMEM((rows, width), b16),
            pltpu.VMEM((rows, width), f32),
            pltpu.VMEM((rows, width), f32),
            pltpu.VMEM((3, rows, width), b16),
            pltpu.VMEM((GROUP, rows, rows), b16),
            pltpu.VMEM((width, rows), b16),
            pltpu.VMEM((2, width, width), b16),
            dma((6,)),
            dma((5,)),
            dma((6,)),
        ]
        + (
            [pltpu.VMEM((peers,) + block, f32), pltpu.VMEM((peers,) + block, b16), dma, dma, dma]
            if trade
            else []
        ),
        input_output_aliases={9: 0} if aliased else {},
        compiler_params=pltpu.CompilerParams(
            vmem_limit_bytes=VMEM_LIMIT,
            **(dict(collective_id=4, has_side_effects=True) if trade else {}),
        ),
        name="layer_backward",
    )(*((mats, x, vec, dy) + tuple(kept) + ((grads,) if aliased else ()) + (tuple(trade[:2]) if trade else ())))


def rs_kernel(parts,zn,g_ref,v_ref,dx_ref,place_ref,picks_ref,early_ref,o_ref,vo_ref,res_ref,land,buf,obuf,vland,strips32,sendbuf,returned,*rest):
    nP=len(parts)
    lks=rest[:nP]
    ssem,rsem,cs,cr,lsem,osem,vsend,vrecv,tlocal,tsend,trecv,tearly=rest[nP:]
    s,d,z,y,c=coords()
    peers=4*zn
    total_dev=2*peers
    me=s*peers+d
    signal_all(total_dev,me,peers)
    early=pltpu.make_async_copy(early_ref,returned,tearly)
    pl.when(s==1)(lambda: early.start())
    cut_strips(place_ref[...],dx_ref,strips32)
    sendbuf[...]=strips32[...].astype(jnp.bfloat16)
    wait_all(total_dev)
    vland[me]=v_ref[me]
    def small(step,carry):
        other=lax.rem(me+step,total_dev)
        pltpu.make_async_remote_copy(v_ref.at[other],vland.at[me],vsend,vrecv,device_id=(other//peers,lax.rem(other,peers)),device_id_type=MESH).start()
        return carry
    lax.fori_loop(1,total_dev,small,0)
    sib=(s,(z*2+y)*2+1-c)
    def where(it):
        s2=1-s if it[0] else s
        y2=1-y if it[1] else y
        return s2,z+it[2],y2
    def conds(it):
        cl=[]
        if it[2]<0: cl.append(z+it[2]>=0)
        if it[2]>0: cl.append(z+it[2]<=zn-1)
        return cl
    def guarded(cl,fn):
        if not cl: fn(); return
        e=cl[0]
        for q in cl[1:]: e=jnp.logical_and(e,q)
        pl.when(e)(fn)
    def slot_base(order):
        sizes={"x":2,"y":2,"z":zn}
        base={};cur=0
        for k,dim in enumerate(order):
            n=1
            for q in order[k+1:]: n*=sizes[q]
            if dim=="z": n*=2*zn
            base[dim]=cur; cur+=n
        return base,cur
    def slot(p,dim,side,dest):
        order=parts[p][2][::-1]
        base,_=slot_base(order)
        k=order.index(dim)
        v={"x":dest[0],"z":dest[1],"y":dest[2]}
        idx=0
        for q in order[k+1:]:
            idx=idx*(zn if q=="z" else 2)+v[q]
        if dim=="z": idx=(idx*zn+dest[1])*2+side
        return base[dim]+idx
    evs=[]
    for p in range(nP):
        for it in items():
            if abs(it[2])<=zn-1: evs.append((-hops(it),p,it))
    evs.sort(key=lambda e:e[0])
    seq=[(p,it) for _,p,it in evs]
    def core_dsc(p,it,mine):
        r0,rn,_=parts[p]
        s2,z2,y2=where(it)
        idx=(s2*zn+z2)*2+y2
        cc=c if mine else 1-c
        return pltpu.make_async_remote_copy(g_ref.at[s2,(z2*2+y2)*2+cc,pl.ds(r0,rn)],land.at[idx,pl.ds(r0,rn)],cs.at[p,idx],cr.at[p,idx],device_id=sib,device_id_type=MESH)
    for p,it in seq:
        guarded(conds(it),lambda p=p,it=it: core_dsc(p,it,False).start())
    back=give_back(0,s,d,me,peers,sendbuf,returned,tlocal,tsend,trecv)
    def load(i):
        p,it=seq[i]
        r0,rn,_=parts[p]
        s2,z2,y2=where(it)
        return pltpu.make_async_copy(g_ref.at[s2,(z2*2+y2)*2+c,pl.ds(r0,rn)],buf.at[i%NB,pl.ds(0,rn)],lsem.at[i%NB])
    NB=buf.shape[0]
    for i in range(min(NB-1,len(seq))):
        guarded(conds(seq[i][1]),lambda i=i: load(i).start())
    def contribs(p,it):
        order=parts[p][2][::-1]
        diff={"x":it[0],"y":it[1],"z":it[2]}
        out=[];nxt=None
        for dim in order:
            if dim=="z":
                if it[2]==0: out+=[("z",0,z>0),("z",1,z<zn-1)]
                elif it[2]>0: out.append(("z",0,z>0))
                else: out.append(("z",1,z<zn-1))
                if it[2]!=0: nxt="r" if it[2]>0 else "l"; break
            else:
                if diff[dim]: nxt=dim; break
                out.append((dim,0,None))
        return out,nxt
    semoff=[0]
    for p in range(nP): semoff.append(semoff[-1]+slot_base(parts[p][2][::-1])[1])
    def out_dsc(p,it,nxt):
        r0,rn,_=parts[p]
        dest=where(it)
        s2,z2,y2=dest
        idx=(s2*zn+z2)*2+y2
        dim="z" if nxt in "lr" else nxt
        side=1 if nxt=="l" else 0
        sl=slot(p,dim,side,dest)
        dev={"x":(1-s,d),"y":(s,(z*2+1-y)*2+c),"l":(s,d-4),"r":(s,d+4)}[nxt]
        return pltpu.make_async_remote_copy(land.at[idx,pl.ds(r0,rn)],lks[p].at[sl],ssem.at[p,idx],rsem.at[semoff[p]+sl],device_id=dev,device_id_type=MESH)
    for i,(p,it) in enumerate(seq):
        r0,rn,_=parts[p]
        if i+NB-1<len(seq):
            guarded(conds(seq[i+NB-1][1]),lambda i=i: load(i+NB-1).start())
        def ev(i=i,p=p,it=it,r0=r0,rn=rn):
            dest=where(it)
            s2,z2,y2=dest
            idx=(s2*zn+z2)*2+y2
            con,nxt=contribs(p,it)
            lk=lks[p]
            load(i).wait()
            core_dsc(p,it,True).wait_recv()
            plain=[x for x in con if x[2] is None]
            cond=[x for x in con if x[2] is not None]
            def rdsc(dim,side):
                sl=slot(p,dim,side,dest)
                return pltpu.make_async_remote_copy(lk.at[sl],lk.at[sl],ssem.at[p,idx],rsem.at[semoff[p]+sl],device_id=sib,device_id_type=MESH),sl
            for dim,side,_ in plain: rdsc(dim,side)[0].wait_recv()
            for dim,side,cnd in cond:
                pl.when(cnd)(lambda dim=dim,side=side: rdsc(dim,side)[0].wait_recv())
            if not cond: variants=[(None,plain)]
            elif len(cond)==1:
                variants=[(cond[0][2],plain+cond),(jnp.logical_not(cond[0][2]),plain)]
            else:
                a,b=cond
                variants=[(jnp.logical_and(a[2],b[2]),plain+cond),(jnp.logical_and(a[2],jnp.logical_not(b[2])),plain+[a]),
                          (jnp.logical_and(jnp.logical_not(a[2]),b[2]),plain+[b])]
            def total(lst):
                slots=[slot(p,dim,side,dest) for dim,side,_ in lst]
                CH=16
                def body(k,_):
                    ro=pl.multiple_of(k*CH,CH)
                    acc=buf[i%NB,pl.ds(ro,CH),:].astype(jnp.float32)+land[idx,pl.ds(r0+ro,CH),:].astype(jnp.float32)
                    for sl in slots: acc=acc+lk[sl,pl.ds(ro,CH),:].astype(jnp.float32)
                    if nxt is None: obuf[pl.ds(r0+ro,CH),:]=acc
                    else: land[idx,pl.ds(r0+ro,CH),:]=acc.astype(jnp.bfloat16)
                    return 0
                lax.fori_loop(0,rn//CH,body,0)
            for cnd,lst in variants:
                if cnd is None: total(lst)
                else: pl.when(cnd)(lambda lst=lst: total(lst))
            if nxt is not None: out_dsc(p,it,nxt).start()
            else: pltpu.make_async_copy(obuf.at[pl.ds(r0,rn)],o_ref.at[pl.ds(r0,rn)],osem.at[p]).start()
        guarded(conds(it),ev)
    for p,it in seq:
        def fin(p=p,it=it):
            core_dsc(p,it,False).wait_send()
            nxt=contribs(p,it)[1]
            if nxt is not None: out_dsc(p,it,nxt).wait_send()
        guarded(conds(it),fin)
    for p,(r0,rn,_) in enumerate(parts):
        pltpu.make_async_copy(obuf.at[pl.ds(r0,rn)],o_ref.at[pl.ds(r0,rn)],osem.at[p]).wait()
    rest_of=vland.at[pl.ds(0,total_dev-1)]
    bulk=pltpu.make_async_remote_copy(rest_of,rest_of,vsend,vrecv,device_id=(0,0),device_id_type=MESH)
    bulk.wait_recv()
    bulk.wait_send()
    vo_ref[...]=jnp.sum(vland[...],axis=0)
    back()
    pl.when(s==1)(lambda: early.wait())
    for batch in range(2):
        strips32[...]=returned[batch*peers:(batch+1)*peers].astype(jnp.float32)
        join_strips(picks_ref[batch],strips32,res_ref.at[batch])


def slot_count(order,zn):
    sizes={"x":2,"y":2,"z":zn};cur=0
    for k,dim in enumerate(order):
        n=1
        for q in order[k+1:]: n*=sizes[q]
        if dim=="z": n*=2*zn
        cur+=n
    return cur
def rs(g,v,dx,place,picks,early,parts,zn,cid=1,nb=4):
    n=len(parts)
    cnt=[slot_count(p[2][::-1],zn) for p in parts]
    mx=max(p[1] for p in parts)
    return pl.pallas_call(functools.partial(rs_kernel,parts,zn),
        out_shape=[jax.ShapeDtypeStruct((480,1280),jnp.float32),jax.ShapeDtypeStruct(v.shape[1:],jnp.float32),
            jax.ShapeDtypeStruct((2,)+dx.shape,jnp.bfloat16)],
        in_specs=[pl.BlockSpec(memory_space=pl.ANY)]+[pl.BlockSpec(memory_space=pltpu.VMEM)]*4+[pl.BlockSpec(memory_space=pl.ANY)],
        out_specs=[pl.BlockSpec(memory_space=pl.ANY)]+[pl.BlockSpec(memory_space=pltpu.VMEM)]*2,
        scratch_shapes=[pltpu.VMEM((4*zn,480,1280),jnp.bfloat16),pltpu.VMEM((nb,mx,1280),jnp.bfloat16),pltpu.VMEM((480,1280),jnp.float32),pltpu.VMEM(v.shape,jnp.float32),
            pltpu.VMEM((4*zn,)+early.shape[1:],jnp.float32),pltpu.VMEM((4*zn,)+early.shape[1:],jnp.bfloat16),pltpu.VMEM(early.shape,jnp.bfloat16)]
          +[pltpu.VMEM((cnt[p],parts[p][1],1280),jnp.bfloat16) for p in range(n)]
          +[pltpu.SemaphoreType.DMA((n,4*zn)),pltpu.SemaphoreType.DMA((sum(cnt),)),
          pltpu.SemaphoreType.DMA((n,4*zn)),pltpu.SemaphoreType.DMA((n,4*zn)),pltpu.SemaphoreType.DMA((nb,)),pltpu.SemaphoreType.DMA((n,))]+[pltpu.SemaphoreType.DMA]*6,
        compiler_params=pltpu.CompilerParams(collective_id=cid,has_side_effects=True,vmem_limit_bytes=62*2**20))(g,v,dx,place,picks,early)


def as_row(column):
    rows = column.shape[0]
    return jnp.broadcast_to(column, (rows, 128)).T[0:1, :]


def as_column(row):
    size = row.shape[1]
    return jnp.broadcast_to(row, (128, size)).T[:, 0:1]


def ones_where(flag):
    return jnp.where(flag, 1.0, 0.0)


def gather_events(parts,zn,place,own,w_ref,ssem,rsem,cs,cr):
    s,d,z,y,c=place
    KIND={"x":0,"y":1,"l":2,"r":3}
    def where(it):
        s2=1-s if it[0] else s
        y2=1-y if it[1] else y
        z2=z+it[2]
        return s2,z2,y2
    def dsc(p,it,kind):
        r0,rn,order=parts[p]
        s2,z2,y2=where(it)
        idx=s2*(2*zn)+z2*2+y2
        is_own=it==(0,0,0)
        src=own.at[pl.ds(r0,rn)] if is_own else w_ref.at[s2,(z2*2+y2)*2+c,pl.ds(r0,rn)]
        dst=w_ref.at[s2,(z2*2+y2)*2+c,pl.ds(r0,rn)]
        if kind=="core":
            dev=(s,(z*2+y)*2+1-c)
            return pltpu.make_async_remote_copy(src,dst,cs.at[p,idx],cr.at[p,idx],device_id=dev,device_id_type=MESH)
        dev={"x":(1-s,d),"y":(s,(z*2+1-y)*2+c),"l":(s,d-4),"r":(s,d+4)}[kind]
        return pltpu.make_async_remote_copy(src,dst,ssem.at[KIND[kind],p,idx],rsem.at[p,idx],device_id=dev,device_id_type=MESH)
    def cdsc(p,it):
        r0,rn,order=parts[p]
        s2,z2,y2=where(it)
        idx=s2*(2*zn)+z2*2+y2
        dst=w_ref.at[s2,(z2*2+y2)*2+1-c,pl.ds(r0,rn)]
        return pltpu.make_async_remote_copy(dst,dst,cs.at[p,idx],cr.at[p,idx],device_id=(s,(z*2+y)*2+1-c),device_id_type=MESH)
    def conds(it,kind):
        cs_=[]
        if it[2]<0: cs_.append(z+it[2]>=0)
        if it[2]>0: cs_.append(z+it[2]<=zn-1)
        if kind=="l": cs_.append(z>0)
        if kind=="r": cs_.append(z<zn-1)
        return cs_
    def guarded(cl,fn):
        if not cl: fn(); return
        e=cl[0]
        for q in cl[1:]: e=jnp.logical_and(e,q)
        pl.when(e)(fn)
    def sends(p,it):
        order=parts[p][2]
        a=arrival(order,it)
        ks=[]
        if a is not None and order[a]=="z": ks.append("l" if it[2]>0 else "r")
        for dim in order[(a+1) if a is not None else 0:]:
            ks += ["r","l"] if dim=="z" else [dim]
        ks.append("core")
        return ks
    evs=[]
    for p in range(len(parts)):
        for it in items():
            if abs(it[2])<zn: evs.append((hops(it),p,it))
    evs.sort(key=lambda e:e[0])
    first=[]
    later=[]
    for h,p,it in evs:
        def ev(p=p,it=it):
            if it!=(0,0,0): dsc(p,it,"x").wait_recv()
            for k in sends(p,it):
                guarded(conds((0,0,0),k), lambda k=k: dsc(p,it,k).start())
        (later if h else first).append(lambda it=it,ev=ev: guarded(conds(it,None),ev))
    def finish():
        for _,p,it in evs:
            def fin(p=p,it=it):
                cdsc(p,it).wait_recv()
                for k in sends(p,it):
                    guarded(conds((0,0,0),k), lambda k=k: dsc(p,it,k).wait_send())
            guarded(conds(it,None),fin)
    return first,later,finish


def enter_kernel(
    parts, zn, mats_ref, packet_ref, deal_ref, tokens_ref,
    w_ref, shared_ref, x_ref, order, picks_ref, place_ref, sendbuf,
    own, wide_rows, strips32, landed,
    own_sem, lsem, ssem, rsem, cs, cr, psend, precv, tsend, trecv,
):
    s, d, z, y, c = coords()
    peers = 4 * zn
    total = 2 * peers
    me = s * peers + d
    batches, rows, width = tokens_ref.shape
    f32, b16 = jnp.float32, jnp.bfloat16
    cast_in = pltpu.make_async_copy(mats_ref, wide_rows, own_sem)
    cast_in.start()
    greet(total, me, peers)
    shared_ref[me] = packet_ref[...]

    def tell(step, carry):
        other = lax.rem(me + step, total)
        pltpu.make_async_remote_copy(
            packet_ref, shared_ref.at[me], psend, precv,
            device_id=(other // peers, lax.rem(other, peers)), device_id_type=MESH,
        ).start()
        return carry

    lax.fori_loop(1, total, tell, 0)
    cast_in.wait()
    own[...] = wide_rows[...].astype(b16)
    lc = pltpu.make_async_copy(own, w_ref.at[s, d], lsem)
    lc.start()
    start_events, rest_events, finish = gather_events(
        parts, zn, (s, d, z, y, c), own, w_ref, ssem, rsem, cs, cr
    )
    for event in start_events:
        event()
    sub = lax.broadcasted_iota(jnp.int32, (rows, rows), 0).astype(f32)
    lane = lax.broadcasted_iota(jnp.int32, (rows, rows), 1).astype(f32)
    mine_row = jnp.where(s == 0, deal_ref[0:1, :], deal_ref[1:2, :])
    mine_col = as_column(mine_row)
    rank_col = jnp.sum(ones_where(mine_row < mine_col), axis=1, keepdims=True)
    order[...] = ones_where(lane == rank_col).astype(b16)
    rank_row = jnp.sum(ones_where(mine_col < mine_row), axis=0, keepdims=True)
    place_ref[...] = ones_where(sub == rank_row).astype(b16)
    rest = shared_ref.at[pl.ds(0, total - 1)]
    bulk = pltpu.make_async_remote_copy(
        rest, rest, psend, precv, device_id=(0, 0), device_id_type=MESH
    )
    bulk.wait_recv()
    index_col = lax.broadcasted_iota(jnp.int32, (rows, 1), 0).astype(f32)
    ids_col = index_col + (d * rows).astype(f32)
    for batch in range(batches):

        def look(block, found):
            known = shared_ref[s * peers + block]
            for line in range(rows // 128):
                at = batch * (rows // 128) + line
                found = jnp.where(ids_col == known[at : at + 1, :], block.astype(f32), found)
            return found

        found = lax.fori_loop(0, peers, look, jnp.zeros((rows, 128), f32))
        key_col = jnp.sum(found, axis=1, keepdims=True) * rows + index_col
        key_row = as_row(key_col)
        rank_row = jnp.sum(ones_where(key_col < key_row), axis=0, keepdims=True)
        rank_col = jnp.sum(ones_where(key_row < key_col), axis=1, keepdims=True)
        picks_ref[batch] = ones_where(lane == rank_col).astype(b16)
        pick = ones_where(sub == rank_row).astype(b16)
        cut_strips(pick, tokens_ref.at[batch], strips32)
        sendbuf[batch] = strips32[...].astype(b16)

    @pl.when(s == 0)
    def _():
        landed[d] = sendbuf[0, d]

        def give(step, carry):
            other = lax.rem(me + step, total)
            sec, dp = other // peers, lax.rem(other, peers)
            pltpu.make_async_remote_copy(
                sendbuf.at[sec, dp], landed.at[d], tsend, trecv,
                device_id=(sec, dp), device_id_type=MESH,
            ).start()
            return carry

        lax.fori_loop(1, total, give, 0)

    for event in rest_events:
        event()

    pl.when(s == 0)(lambda: bulk_copy(landed, peers - 1, tsend, trecv).wait_recv())
    pl.when(s != 0)(lambda: bulk_copy(landed, peers, tsend, trecv).wait_recv())
    strips32[...] = landed[...].astype(f32)
    join_strips(order[...], strips32, x_ref)
    finish()
    lc.wait()
    bulk.wait_send()

    @pl.when(s == 0)
    def _():
        bulk_copy(sendbuf.at[0], peers, tsend, trecv).wait_send()
        bulk_copy(sendbuf.at[0], peers - 1, tsend, trecv).wait_send()


def enter(mats, packet, deal, tokens, parts, zn):
    n = len(parts)
    peers = 4 * zn
    batches, rows, width = tokens.shape
    strip_rows = rows // peers * (width // 128)
    f32, b16 = jnp.float32, jnp.bfloat16
    vm = pl.BlockSpec(memory_space=pltpu.VMEM)
    hbm = pl.BlockSpec(memory_space=pl.ANY)
    dma = pltpu.SemaphoreType.DMA
    return pl.pallas_call(
        functools.partial(enter_kernel, parts, zn),
        out_shape=[
            jax.ShapeDtypeStruct((2, peers) + mats.shape, b16),
            jax.ShapeDtypeStruct((2 * peers,) + packet.shape, f32),
            jax.ShapeDtypeStruct((rows, width), b16),
            jax.ShapeDtypeStruct((rows, rows), b16),
            jax.ShapeDtypeStruct((batches, rows, rows), b16),
            jax.ShapeDtypeStruct((rows, rows), b16),
            jax.ShapeDtypeStruct((batches, peers, strip_rows, 128), b16),
        ],
        in_specs=[hbm, vm, vm, vm],
        out_specs=[hbm, vm, vm, vm, vm, vm, vm],
        scratch_shapes=[
            pltpu.VMEM(mats.shape, b16),
            pltpu.VMEM(mats.shape, f32),
            pltpu.VMEM((peers, strip_rows, 128), f32),
            pltpu.VMEM((peers, strip_rows, 128), b16),
            dma, dma, dma((4, n, peers)), dma((n, peers)), dma((n, peers)), dma((n, peers)),
            dma, dma, dma, dma,
        ],
        compiler_params=pltpu.CompilerParams(
            collective_id=0, has_side_effects=True, vmem_limit_bytes=VMEM_LIMIT
        ),
        name="enter",
    )(mats, packet, deal, tokens)


def one_hot(rank):
    rows = rank.shape[0]
    return (rank[None, :] == jnp.arange(rows, dtype=jnp.int32)[:, None]).astype(jnp.bfloat16)


def rank_of(key):
    return jnp.sum((key[None, :] < key[:, None]).astype(jnp.int32), axis=1)


def padded(flat):
    lead, size = flat.shape
    full = -(-size // 1024) * 1024
    return jnp.pad(flat, ((0, 0), (0, full - size))).reshape(lead, full // 128, 128)


def enter_plain(own, packet, deal, tokens, peers):
    section = lax.axis_index("section")
    batches, rows, width = tokens.shape
    per_peer = rows // peers
    shared = lax.all_gather(packet, BOTH, axis=0)
    low = own.astype(jnp.bfloat16)
    mats = lax.all_gather(low, BOTH, axis=0, tiled=True).reshape((2, peers) + own.shape)
    flat = shared.reshape(2, peers, -1)[:, :, : batches * rows]
    dealt = jnp.where(section == 0, flat[0], flat[1]).astype(jnp.int32).reshape(peers, batches, rows)
    own_rows = lax.axis_index("dp") * rows + jnp.arange(rows, dtype=jnp.int32)
    blocks = jnp.arange(peers, dtype=jnp.int32)
    picks = []
    sends = []
    for batch in range(batches):
        hit = dealt[:, batch][None, :, :] == own_rows[:, None, None]
        target = jnp.sum(jnp.where(hit, blocks[None, :, None], 0), axis=(1, 2))
        pick = one_hot(rank_of(target * rows + jnp.arange(rows, dtype=jnp.int32)))
        picks.append(pick.T)
        sends.append(nn(pick, tokens[batch]).astype(jnp.bfloat16))
    outgoing = jnp.stack(sends).reshape(2 * peers, per_peer, width)
    arrived = lax.all_to_all(outgoing, BOTH, split_axis=0, concat_axis=0, tiled=True)
    arrived = arrived.reshape(2, rows, width)
    place = one_hot(rank_of(jnp.where(section == 0, deal[0], deal[1])))
    x, cot = (tn(place, arrived[kind]).astype(jnp.bfloat16) for kind in range(2))
    return mats, shared, x, cot, jnp.stack(picks), place


def leave_plain(terms, small, down, final, place, picks, peers):
    sections, _, rows, width = terms.shape
    terms = terms.reshape(sections * peers * rows, width)
    total = lax.psum_scatter(terms, BOTH, scatter_dimension=0, tiled=True).astype(jnp.float32)
    small = lax.psum_scatter(small, BOTH, scatter_dimension=0, tiled=True)[0]
    back = jnp.stack([nn(place, down), nn(place, final)]).astype(jnp.bfloat16)
    count = down.shape[0]
    back = back.reshape(2 * peers, count // peers, width)
    back = lax.all_to_all(back, BOTH, split_axis=0, concat_axis=0, tiled=True)
    back = back.reshape(-1, count, width)
    results = jnp.stack([nn(picks[batch], back[batch]) for batch in range(back.shape[0])])
    return total, small, results.astype(jnp.bfloat16)


def local(entering, deal, seq_lens, mats, gains, biases):
    section = lax.axis_index("section")
    peers = lax.axis_size("dp")
    arrival = entering[0]
    batches, rows, width = arrival.shape
    per = 2 * width // peers
    vecs = jnp.concatenate([gains[0], biases[0]]).astype(jnp.bfloat16).astype(jnp.float32)
    packet = jnp.concatenate([deal.reshape(-1).astype(jnp.float32), vecs])
    packet = padded(packet[None])[0]
    packet = jnp.pad(packet, ((0, -packet.shape[0] % 8), (0, 0)))
    args = (mats[0], packet, deal.astype(jnp.float32), arrival)
    direct = peers == 16
    if direct:
        all_mats, shared, tokens, order, picks, place, gives = enter(*args, PARTS, peers // 4)
    else:
        all_mats, shared, tokens, cotangent, picks, place = enter_plain(*args, peers)
    shared = shared.reshape(2, peers, -1)
    small = shared[:, :, batches * rows : batches * rows + 2 * per].reshape(2, peers, 2, per)
    small = jnp.swapaxes(small, 1, 2).reshape(2, 4, width)
    small = jnp.pad(small, ((0, 0), (0, 4), (0, 0)))
    all_mats = all_mats.reshape(2, 6 * width, width)
    lens = jnp.where(section == 0, seq_lens[0, 0], seq_lens[1, 0])
    ends = jnp.cumsum(lens)
    positions = jnp.arange(rows, dtype=jnp.int32)
    segment = jnp.sum((positions[:, None] >= ends[None, :]).astype(jnp.int32), axis=1)
    segc, segr = segment[:, None], segment[None]
    if direct:
        middle, *kept_low, cotangent = forward_layer(
            0, all_mats, tokens, small[0], segc, segr, (gives, order)
        )
    else:
        middle, *kept_low = forward_layer(0, all_mats, tokens, small[0], segc, segr)
    final, *kept_high = forward_layer(1, all_mats, middle, small[1], segc, segr)
    trade = (final, place, peers, gives.shape[2:]) if direct else None
    terms, down, vec_high, *early = backward_layer(
        1, all_mats, middle, small[1], cotangent, kept_high, None, trade
    )
    terms, down, vec_low = backward_layer(0, all_mats, tokens, small[0], down, kept_low, terms)
    terms = terms.reshape(2, peers, -1, width)
    vec_terms = jnp.stack([vec_low, vec_high])[:, :4].reshape(2, 2, peers, per)
    vec_terms = padded(jnp.swapaxes(vec_terms, 1, 2).reshape(2 * peers, 2 * per))
    if direct:
        shard_mats, vec_total, results = rs(
            terms, vec_terms, down, place, picks, early[0], PARTS, peers // 4
        )
    else:
        shard_mats, vec_total, results = leave_plain(
            terms, vec_terms, down, final, place, picks, peers
        )
    vec_total = vec_total.reshape(-1)
    return (
        results[None],
        shard_mats[None],
        vec_total[None, :per],
        vec_total[None, per : 2 * per],
    )


def solution(mesh):
    in_specs = (
        P("section", None, "dp", None),
        P(None, "dp"),
        P(None, "dp", None),
        P("section", "dp", None),
        P("section", "dp"),
        P("section", "dp"),
    )
    out_specs = (
        P("section", None, "dp", None),
        P("section", "dp", None),
        P("section", "dp"),
        P("section", "dp"),
    )
    return jax.shard_map(local, mesh=mesh, in_specs=in_specs, out_specs=out_specs, check_vma=False)
```

time: 488 us -> 527 us (1.080)
  Pallas kernels: 459 us -> 503 us
    pallas_call x4, Pallas kernels: 110 us -> 146 us  [the longest x2 97.6 us: backward_layer(): pl.pallas_call(functools.partial(backward_kernel, layer, aliased, peers),...]
    pallas_call x1, Pallas kernels: 166 us -> 176 us  [rs(): pl.pallas_call(functools.partial(rs_kernel, parts, zn), out_shape=[jax.Sh...]
  transfers between devices with their start and end apart: 1 -> 0, of which waited for: 0 -> 0; matrix products, arithmetic and copies ran while one was open for 0% -> 0% of each run, Pallas kernels for 34% -> 0%
where the time goes in v5:
time: 527 us; the launch traced here: 518 us
  Pallas kernels  503 us (95%)
  local copies, waits for them, and re-layouts  10.7 us (2%)
    pallas_call x1, Pallas kernels, enter(): pl.pallas_call(functools.partial(enter_kernel, parts, zn), out_shape=[jax...  181 us
    pallas_call x1, Pallas kernels, rs(): pl.pallas_call(functools.partial(rs_kernel, parts, zn), out_shape=[jax.Sh...  176 us
    pallas_call x2, Pallas kernels, backward_layer(): pl.pallas_call(functools.partial(backward_kernel, layer, aliased, peers),...  97.6 us
    pallas_call x2, Pallas kernels, forward_layer(): pl.pallas_call(functools.partial(forward_kernel, layer, peers), out_shape...  48.1 us

profile of v5, /device:TPU:0, one launch (start us, length us, event | category | flops | bytes accessed | tf_op | source)
XLA Modules:
  0.0 517.8 jit_solution(4226020846638043244)
XLA Ops:
  0.6 0.7 fusion.2
  1.3 0.2 reduce-window.8
  1.5 0.7 convert_reduce_fusion.1
  2.2 0.1 maximum_convert_fusion
  2.3 0.1 convert_reduce_fusion
  2.4 0.6 broadcast_in_dim.25.refs_4_
  3.0 0.7 convert_element_type.20.deal_ref
  3.6 0.0 copy-start.2
  3.7 0.6 pad.12
  4.3 0.8 broadcast_in_dim.30.refs_3_
  5.1 0.0 copy-done.2
  5.1 181.1 %enter.1 = (bf16[2,16,480,1280]{3,2,1,0:T(8,128)(2,1)}, f32[32,16,128]{2,1,0:T(8,128)}, bf16[384,1280]{1,0:T(8,128)(2,1)}, bf16[384,384]{1,0:T(8,128)(2,1)}, bf1...) custom-call(f32[480,1280]{1,0:T(8,128)} %bitcast.31, f32[16,128]{1,0:T(8,128)} %bitcast.40, ...), custom_call_target="tpu_custom_call" | custom-call | tf_op jit(solution)/shard_map/enter/pallas_call | solution.py:903
  186.2 1.0 reshape.79
  187.2 0.1 reshape.80
  187.3 0.1 reshape.81
  187.4 0.6 fusion.1
  188.1 29.3 %layer_forward.2 = (bf16[384,1280]{1,0:T(8,128)(2,1)}, bf16[3,384,1280]{2,1,0:T(8,128)(2,1)}, bf16[16,384,384]{2,1,0:T(8,128)(2,1)}, bf16[384,1280]{1,0:T(8,128)...) custom-call(bf16[2,7680,1280]{2,1,0:T(8,128)(2,1)} %bitcast.26, ...), custom_call_target="tpu_custom_call" | custom-call | tf_op jit(solution)/shard_map/layer_forward/pallas_call | solution.py:265
  217.4 18.7 %layer_forward.3 = (bf16[384,1280]{1,0:T(8,128)(2,1)}, bf16[3,384,1280]{2,1,0:T(8,128)(2,1)}, bf16[16,384,384]{2,1,0:T(8,128)(2,1)}, bf16[384,1280]{1,0:T(8,128)...) custom-call(bf16[2,7680,1280]{2,1,0:T(8,128)(2,1)} %bitcast.27, bf16[384,1280]{1,0:T(8,128)(2,1)} %get-tuple-element.39.refs_1_, ...), custom_call_target="tpu_custom_call" | custom-call | tf_op jit(solution)/shard_map/layer_forward/pallas_call | solution.py:265
  236.2 61.7 %layer_backward.2 = (bf16[2,7680,1280]{2,1,0:T(8,128)(2,1)}, bf16[384,1280]{1,0:T(8,128)(2,1)}, f32[8,1280]{1,0:T(8,128)}, bf16[32,240,128]{2,1,0:T(8,128)(2,1)}) custom-call(bf16[2,7680,1280]{2,1,0:T(8,128)(2,1)} %bitcast.28, bf16[384,1280]{1,0:T(8,128)(2,1)} %get-tuple-element.39.refs_1_, f32[8,1280]{1,0:T(8,128)} %get-tuple-element.64.refs_2_, ...), custom_call_target="tpu_custom_call" | custom-call | tf_op jit(solution)/shard_map/layer_backward/pallas_call | solution.py:474
  297.8 0.0 copy-start.1
  297.8 36.0 %layer_backward.3 = (bf16[2,7680,1280]{2,1,0:T(8,128)(2,1)}, bf16[384,1280]{1,0:T(8,128)(2,1)}, f32[8,1280]{1,0:T(8,128)}) custom-call(bf16[2,7680,1280]{2,1,0:T(8,128)(2,1)} %bitcast.29, bf16[384,1280]{1,0:T(8,128)(2,1)} %get-tuple-element.35.refs_1_, f32[8,1280]{1,0:T(8,128)} %get-tuple-element.65.refs_2_, ...), custom_call_target="tpu_custom_call", output_to_operand_aliasing={{0}: (9, {})} | custom-call | tf_op jit(solution)/shard_map/layer_backward/pallas_call | solution.py:474
  333.8 0.0 copy-done.1
  333.8 0.8 pad_maximum_fusion
  334.6 0.1 reshape.84
  334.7 0.1 copy.19
  334.8 0.1 reshape.85
  334.9 0.7 copy.20
  335.6 176.1 %shard_map.93 = (f32[480,1280]{1,0:T(8,128)}, f32[8,128]{1,0:T(8,128)}, bf16[2,384,1280]{2,1,0:T(8,128)(2,1)}) custom-call(bf16[2,16,480,1280]{3,2,1,0:T(8,128)(2,1)} %bitcast.30, f32[32,8,128]{2,1,0:T(8,128)} %bitcast.35, bf16[384,1280]{1,0:T(8,128)(2,1)} %get-tuple-element.58.dx_ref, bf16[384,384]{1,0:T(8,128)(2,1)} %get-tuple-element.47.refs_10_.place_ref, ...), custom_call_target="tpu_custom_call" | custom-call | tf_op jit(solution)/shard_map/pallas_call | solution.py:696
  511.7 0.0 copy-start
  511.7 1.5 fusion.3
  513.2 2.9 copy.24
  516.1 0.0 copy-done
  516.1 1.4 copy.25
  (6 shorter events, 0.0 us)
Async XLA Ops:
  3.6 1.4 copy-start.2
  297.8 36.0 %copy-start.1 = (f32[8,1280]{1,0:T(8,128)S(1)}, f32[8,1280]{1,0:T(8,128)}, u32[]{:S(2)}) copy-start(f32[8,1280]{1,0:T(8,128)} %get-tuple-element.57) | copy-start | bytes 122884
  511.7 4.4 copy-start

commit v6 on v5

v6 whole, which is shorter than its diff:
```python
import functools

import jax
import jax.numpy as jnp
from jax import lax
from jax.experimental import pallas as pl
from jax.experimental.pallas import tpu as pltpu
from jax.sharding import PartitionSpec as P

HEADS = 16
EPS = 1e-06
NEG = -1000000000.0
BOTH = ("section", "dp")
MESH = pl.DeviceIdType.MESH
GATHER_PARTS = ((0, 112, "zxy"), (112, 112, "zyx"), (224, 128, "xzy"), (352, 128, "yzx"))
SCATTER_PARTS = ((0, 112, "zxy"), (112, 112, "zyx"), (224, 128, "xzy"), (352, 128, "yzx"))
TAKE_NUM, TAKE_DEN = 3, 4
SETTLE_NUM, SETTLE_DEN = 7, 8
GIVE_NUM, GIVE_DEN = 0, 1
HAND_NUM, HAND_DEN = 0, 1


WIN = 256
QB = 128
GROUP = 4
LOG2E = 1.4426950408889634
LN2 = 0.6931471805599453
GC = 0.7978845608028654
GA = 0.044715
VMEM_LIMIT = 62 * 2**20


def nn(left, right):
    return jnp.dot(left, right, preferred_element_type=jnp.float32)


def nt(left, right):
    return lax.dot_general(
        left, right, (((1,), (1,)), ((), ())), preferred_element_type=jnp.float32
    )


def tn(left, right):
    return lax.dot_general(
        left, right, (((0,), (0,)), ((), ())), preferred_element_type=jnp.float32
    )


def head_window(head, depth, width):
    start = jnp.minimum((head * depth) // 128, (width - WIN) // 128) * 128
    start = pl.multiple_of(start, 128)
    lane = lax.broadcasted_iota(jnp.int32, (1, WIN), 1) + (start - head * depth)
    return start, (lane >= 0) & (lane < depth)


def norm_rows(value, gain):
    return value * lax.rsqrt(jnp.mean(value * value, axis=-1, keepdims=True) + EPS) * gain


def norm_back(value, gain, down):
    inv = lax.rsqrt(jnp.mean(value * value, axis=-1, keepdims=True) + EPS)
    unit = value * inv
    scaled = down * gain
    lean = jnp.mean(scaled * unit, axis=-1, keepdims=True)
    return inv * (scaled - unit * lean), jnp.sum(down * unit, axis=0, keepdims=True)


def signal_all(total, me, peers):
    barrier = pltpu.get_barrier_semaphore()

    def one(step, carry):
        other = lax.rem(me + step, total)
        pl.semaphore_signal(
            barrier, inc=1, device_id=(other // peers, lax.rem(other, peers)), device_id_type=MESH
        )
        return carry

    lax.fori_loop(1, total, one, 0)


def wait_all(total):
    pl.semaphore_wait(pltpu.get_barrier_semaphore(), total - 1)


def greet(total, me, peers):
    signal_all(total, me, peers)
    wait_all(total)


def cut_strips(pick, source, strips32):
    peers = strips32.shape[0]
    strips = source.shape[-1] // 128
    each = strips32.shape[1] // strips
    for strip in range(strips):
        part = nn(pick, source[:, strip * 128 : (strip + 1) * 128])
        strips32[:, strip * each : (strip + 1) * each, :] = part.reshape(peers, each, 128)


def join_strips(order, strips32, out_ref):
    peers = strips32.shape[0]
    strips = out_ref.shape[-1] // 128
    each = strips32.shape[1] // strips
    for strip in range(strips):
        part = strips32[:, strip * each : (strip + 1) * each, :].reshape(peers * each, 128)
        part = nn(order, part.astype(jnp.bfloat16)).astype(jnp.bfloat16)
        out_ref[:, strip * 128 : (strip + 1) * 128] = part


def bulk_copy(ref, count, send_sem, recv_sem):
    some = ref.at[pl.ds(0, count)]
    return pltpu.make_async_remote_copy(
        some, some, send_sem, recv_sem, device_id=(0, 0), device_id_type=MESH
    )


def coords():
    s=lax.axis_index("section"); d=lax.axis_index("dp")
    return s,d,d//4,(d//2)%2,d%2

def items():
    out=[]
    for bx in (0,1):
        for by in (0,1):
            for dz in (0,-1,1,-2,2,-3,3):
                out.append((bx,by,dz))
    return out
def hops(it): return it[0]+it[1]+abs(it[2])
def arrival(order,it):
    diff={"x":it[0]!=0,"y":it[1]!=0,"z":it[2]!=0}
    last=None
    for k,dim in enumerate(order):
        if diff[dim]: last=k
    return last

def neighbours(s,d,z,y,c,zn):
    return [(None,(1-s,d)),(None,(s,(z*2+1-y)*2+c)),(None,(s,(z*2+y)*2+1-c)),(z>0,(s,d-4)),(z<zn-1,(s,d+4))]


SLOTS = 4
USES = (
    [(0, index) for index in range(6)] + [(1, index) for index in range(6)]
    + [(1, index) for index in (5, 4, 3, 2, 1, 0)] + [(0, index) for index in (5, 4, 3, 2, 1, 0)]
)


def plan_loads():
    def next_use(what, since):
        return next((t for t in range(since, len(USES)) if USES[t] == what), len(USES))

    held = [None] * SLOTS
    loads = []
    for done in range(-1, len(USES)):
        for t in range(done + 1, len(USES)):
            if USES[t] in held:
                continue
            away = [next_use(what, done + 1) if what else len(USES) + 1 for what in held]
            slot = max(range(SLOTS), key=lambda k: away[k])
            if away[slot] <= t:
                break
            held[slot] = USES[t]
            loads.append((done, t, slot))
    return loads


def both_layers_kernel(*refs):
    mats_ref, x_ref, vec_ref, segc_ref, segr_ref, cot_ref = refs[:6]
    y_ref, grads_ref, dx_ref, dvec_ref = refs[6:10]
    (
        held, qkvs, probs, atts, mids, us, between, act, low, mask, dqkv, dscore, turned,
    stage, sems, out_sems,
    ) = refs[10:]
    rows, width = x_ref.shape
    depth = width // HEADS
    scale = depth ** (-0.5)
    f32, b16 = jnp.float32, jnp.bfloat16
    tiles = [slice(c, c + WIN) for c in range(0, width, WIN)]
    loads = plan_loads()
    pending = {}

    def load(number):
        done, use, slot = loads[number]
        layer, index = USES[use]
        return pltpu.make_async_copy(
            mats_ref.at[layer, pl.ds(index * width, width)], held.at[slot], sems.at[number]
        )

    def after(done):
        for number, (when, use, slot) in enumerate(loads):
            if when == done:
                load(number).start()
                pending[slot] = number

    def acquire(use):
        number = max(
            k for k, (when, first, slot) in enumerate(loads) if USES[first] == USES[use] and first <= use
        )
        slot = loads[number][2]
        if pending.get(slot) == number:
            load(number).wait()
            pending.pop(slot)
        return held.at[slot]

    after(-1)
    qi = lax.broadcasted_iota(jnp.int32, (rows, rows), 0)
    ki = lax.broadcasted_iota(jnp.int32, (rows, rows), 1)
    mask[...] = jnp.where((segc_ref[...] == segr_ref[...]) & (ki <= qi), 3e38, NEG)

    def forward(layer, source, out_ref):
        qkv, prob, att, mid, u = (ref.at[layer] for ref in (qkvs, probs, atts, mids, us))
        gain_one, gain_two = vec_ref[layer, 0:1, :], vec_ref[layer, 1:2, :]
        bias_one, bias_two = vec_ref[layer, 2:3, :], vec_ref[layer, 3:4, :]
        use = 6 * layer
        low[...] = norm_rows(source[...].astype(f32), gain_one).astype(b16)
        for index in range(3):
            weight = acquire(use + index)
            for cols in tiles:
                part = nn(low[...], weight[:, cols])
                if index == 0:
                    part = part * (scale * LOG2E)
                qkv[index, :, cols] = part.astype(b16)
            after(use + index)
        att[...] = jnp.zeros_like(att)

        def head_group(group, carry):
            blocks = range(rows // QB)
            heres = [slice(block * QB, (block + 1) * QB) for block in blocks]
            uptos = [slice(0, (block + 1) * QB) for block in blocks]
            work = []
            for k in range(GROUP):
                head = group * GROUP + k
                start, lanes = head_window(head, depth, width)
                work += [(head, pl.ds(start, WIN), lanes, heres[b], uptos[b]) for b in blocks]
            scores = [nt(jnp.where(lanes, qkv[0, here, cols], 0), qkv[1, upto, cols]) for head, cols, lanes, here, upto in work]
            scores = [jnp.minimum(score, mask[w[3], w[4]]) for score, w in zip(scores, work)]
            tops = [jnp.max(score, axis=-1, keepdims=True) for score in scores]
            expds = [jnp.exp2(score - top) for score, top in zip(scores, tops)]
            sums = [1.0 / jnp.sum(e, axis=-1, keepdims=True) for e in expds]
            softs = [(e * r).astype(jnp.bfloat16) for e, r in zip(expds, sums)]
            for soft, (head, cols, lanes, here, upto) in zip(softs, work):
                prob[head, here, upto] = soft
            mixes = [nn(soft, qkv[2, w[4], w[1]]).astype(jnp.bfloat16) for soft, w in zip(softs, work)]
            for mixed, (head, cols, lanes, here, upto) in zip(mixes, work):
                att[here, cols] = jnp.where(lanes, mixed, att[here, cols])
            return carry
        lax.fori_loop(0, HEADS // GROUP, head_group, 0)
        weight = acquire(use + 3)
        for cols in tiles:
            mid[:, cols] = source[:, cols].astype(f32) + nn(att[...], weight[:, cols])
        after(use + 3)
        low[...] = norm_rows(mid[...], gain_two).astype(b16)
        weight = acquire(use + 4)
        for cols in tiles:
            pre = nn(low[...], weight[:, cols]) + bias_one[:, cols]
            u[:, cols] = pre
            bent = 0.5 * pre * (1.0 + jnp.tanh(GC * (pre + GA * (pre * pre * pre))))
            act[:, cols] = bent.astype(b16)
        after(use + 4)
        weight = acquire(use + 5)
        for cols in tiles:
            out = mid[:, cols] + (nn(act[...], weight[:, cols]) + bias_two[:, cols])
            out_ref[:, cols] = out.astype(b16)
        after(use + 5)

    pieces = (tiles[:3], tiles[3:])
    in_slot = [None, None]

    def put(layer, index, slot):
        first = pieces[slot][0].start
        count = pieces[slot][-1].stop - first
        return pltpu.make_async_copy(
            stage.at[slot, pl.ds(0, count)],
            grads_ref.at[layer, pl.ds(index * width + first, count)],
            out_sems.at[layer, index, slot],
        )

    def weight_grad(layer, index, left_t, right):
        for slot, piece in enumerate(pieces):
            if in_slot[slot] is not None:
                put(*in_slot[slot], slot).wait()
            for cols in piece:
                at = slice(cols.start - piece[0].start, cols.stop - piece[0].start)
                stage[slot, at, :] = nn(left_t(cols), right).astype(b16)
            put(layer, index, slot).start()
            in_slot[slot] = (layer, index)

    def backward(layer, source, dy_ref, out_ref, use):
        qkv, prob, att, mid, u = (ref.at[layer] for ref in (qkvs, probs, atts, mids, us))
        wide, dmid = u, mid
        gain_one, gain_two = vec_ref[layer, 0:1, :], vec_ref[layer, 1:2, :]
        dvec_ref[layer, 3:4, :] = jnp.sum(dy_ref[...].astype(f32), axis=0, keepdims=True)
        weight = acquire(use)
        for cols in tiles:
            pre = u[:, cols]
            square = pre * pre
            bent = jnp.tanh(GC * (pre + GA * (square * pre)))
            half = 0.5 * (1.0 + bent)
            act[:, cols] = (pre * half).astype(b16)
            slope = half + (0.5 * GC) * pre * (1.0 - bent * bent) * (1.0 + (3.0 * GA) * square)
            down = (nt(dy_ref[...], weight[cols, :]) * slope).astype(b16)
            low[:, cols] = down
            dvec_ref[layer, 2:3, cols] = jnp.sum(down.astype(f32), axis=0, keepdims=True)
        after(use)
        weight_grad(layer, 5, lambda cols: act[:, cols].T, dy_ref[...])
        weight = acquire(use + 1)
        for cols in tiles:
            wide[:, cols] = nt(low[...], weight[cols, :])
        after(use + 1)
        act[...] = norm_rows(mid[...], gain_two).astype(b16)
        weight_grad(layer, 4, lambda cols: act[:, cols].T, low[...])
        part, gain_sum = norm_back(mid[...], gain_two, wide[...])
        dvec_ref[layer, 1:2, :] = gain_sum
        total = dy_ref[...].astype(f32) + part
        dmid[...] = total
        low[...] = total.astype(b16)
        weight_grad(layer, 3, lambda cols: att[:, cols].T, low[...])
        weight = acquire(use + 2)
        for cols in tiles:
            act[:, cols] = nt(low[...], weight[cols, :]).astype(b16)
        after(use + 2)
        dqkv[...] = jnp.zeros_like(dqkv)

        def head_group(group, carry):
            blocks = range(rows // QB)
            heres = [slice(block * QB, (block + 1) * QB) for block in blocks]
            uptos = [slice(0, (block + 1) * QB) for block in blocks]
            sinces = [slice(block * QB, rows) for block in blocks]
            work = []
            for k in range(GROUP):
                head = group * GROUP + k
                start, lanes = head_window(head, depth, width)
                work += [(head, pl.ds(start, WIN), lanes, heres[b], uptos[b], sinces[b], k) for b in blocks]
            dprobs = [nt(jnp.where(w[2], act[w[3], w[1]], 0), qkv[2, w[4], w[1]]) for w in work]
            softs = [prob[w[0], w[3], w[4]].astype(f32) for w in work]
            leans = [jnp.sum(dp * soft, axis=-1, keepdims=True) for dp, soft in zip(dprobs, softs)]
            dss = [(soft * (dp - lean)).astype(b16) for dp, soft, lean in zip(dprobs, softs, leans)]
            for ds, w in zip(dss, work):
                dscore[w[6], w[3], w[4]] = ds
            dvs = [tn(prob[w[0], w[5], w[3]], act[w[5], w[1]]).astype(b16) for w in work]
            dqs = [(nn(ds, qkv[1, w[4], w[1]]) * scale).astype(b16) for ds, w in zip(dss, work)]
            dks = [(tn(dscore[w[6], w[5], w[3]], qkv[0, w[5], w[1]]) * LN2).astype(b16) for w in work]
            for dq, dk, dv, w in zip(dqs, dks, dvs, work):
                for index, value in enumerate((dq, dk, dv)):
                    dqkv[index, w[3], w[1]] = jnp.where(w[2], value, dqkv[index, w[3], w[1]])
            return carry
        lax.fori_loop(0, HEADS // GROUP, head_group, 0)
        low[...] = norm_rows(source[...].astype(f32), gain_one).astype(b16)
        for cols in tiles:
            turned[cols, :] = low[:, cols].T
        for index in (2, 1, 0):
            weight_grad(layer, index, lambda cols: turned[cols, :], dqkv[index])
        w_value, w_key, w_query = acquire(use + 3), acquire(use + 4), acquire(use + 5)
        for cols in tiles:
            wide[:, cols] = (
                nt(dqkv[0], w_query[cols, :]) + nt(dqkv[1], w_key[cols, :]) + nt(dqkv[2], w_value[cols, :])
            )
        for k in (3, 4, 5):
            after(use + k)
        part, gain_sum = norm_back(source[...].astype(f32), gain_one, wide[...])
        dvec_ref[layer, 0:1, :] = gain_sum
        dvec_ref[layer, 4:8, :] = jnp.zeros_like(dvec_ref[layer, 4:8, :])
        out_ref[...] = (dmid[...] + part).astype(b16)

    forward(0, x_ref, between)
    forward(1, between, y_ref)
    backward(1, between, cot_ref, dx_ref, 12)
    backward(0, x_ref, dx_ref, dx_ref, 18)
    for slot in range(2):
        put(*in_slot[slot], slot).wait()


def both_layers(mats, x, vec, segc, segr, cot):
    rows, width = x.shape
    f32, b16 = jnp.float32, jnp.bfloat16
    vm = pl.BlockSpec(memory_space=pltpu.VMEM)
    hbm = pl.BlockSpec(memory_space=pl.ANY)
    flat = (rows, width)
    dma = pltpu.SemaphoreType.DMA
    return pl.pallas_call(
        both_layers_kernel,
        out_shape=[
            jax.ShapeDtypeStruct(flat, b16),
            jax.ShapeDtypeStruct(mats.shape, b16),
            jax.ShapeDtypeStruct(flat, b16),
            jax.ShapeDtypeStruct((2, 8, width), f32),
        ],
        in_specs=[hbm, vm, vm, vm, vm, vm],
        out_specs=[vm, hbm, vm, vm],
        scratch_shapes=[
            pltpu.VMEM((SLOTS, width, width), b16),
            pltpu.VMEM((2, 3) + flat, b16),
            pltpu.VMEM((2, HEADS, rows, rows), b16),
            pltpu.VMEM((2,) + flat, b16),
            pltpu.VMEM((2,) + flat, f32),
            pltpu.VMEM((2,) + flat, f32),
            pltpu.VMEM(flat, b16),
            pltpu.VMEM(flat, b16),
            pltpu.VMEM(flat, b16),
            pltpu.VMEM((rows, rows), f32),
            pltpu.VMEM((3,) + flat, b16),
            pltpu.VMEM((GROUP, rows, rows), b16),
            pltpu.VMEM((width, rows), b16),
            pltpu.VMEM((2, 3 * WIN, width), b16),
            dma((len(plan_loads()),)),
            dma((2, 6, 2)),
        ],
        compiler_params=pltpu.CompilerParams(
            vmem_limit_bytes=63 * 2**20,
        ),
        name="both_layers",
    )(mats, x, vec, segc, segr, cot)


def give_back(s, d, me, peers, sendbuf, returned, local_sem, send_sem, recv_sem):
    total = 2 * peers
    keep = pltpu.make_async_copy(sendbuf.at[s, d], returned.at[me], local_sem)
    keep.start()

    def give(step, carry):
        other = lax.rem(me + step, total)
        sec, dp = other // peers, lax.rem(other, peers)
        pltpu.make_async_remote_copy(
            sendbuf.at[sec, dp], returned.at[me], send_sem, recv_sem,
            device_id=(sec, dp), device_id_type=MESH,
        ).start()
        return carry

    lax.fori_loop(1, total, give, 0)

    def finish():
        keep.wait()
        bulk_copy(returned, total - 1, send_sem, recv_sem).wait_recv()
        bulk_copy(returned, total - 1, send_sem, recv_sem).wait_send()

    return finish


def rs_kernel(parts,zn,g_ref,v_ref,dx_ref,y_ref,place_ref,picks_ref,o_ref,vo_ref,res_ref,land,buf,obuf,vland,strips32,sendbuf,returned,*rest):
    nP=len(parts)
    lks=rest[:nP]
    ssem,rsem,cs,cr,lsem,osem,vsend,vrecv,tlocal,tsend,trecv=rest[nP:]
    s,d,z,y,c=coords()
    peers=4*zn
    total_dev=2*peers
    me=s*peers+d
    greet(total_dev,me,peers)
    vland[me]=v_ref[me]
    def small(step,carry):
        other=lax.rem(me+step,total_dev)
        pltpu.make_async_remote_copy(v_ref.at[other],vland.at[me],vsend,vrecv,device_id=(other//peers,lax.rem(other,peers)),device_id_type=MESH).start()
        return carry
    lax.fori_loop(1,total_dev,small,0)
    sib=(s,(z*2+y)*2+1-c)
    def where(it):
        s2=1-s if it[0] else s
        y2=1-y if it[1] else y
        return s2,z+it[2],y2
    def conds(it):
        cl=[]
        if it[2]<0: cl.append(z+it[2]>=0)
        if it[2]>0: cl.append(z+it[2]<=zn-1)
        return cl
    def guarded(cl,fn):
        if not cl: fn(); return
        e=cl[0]
        for q in cl[1:]: e=jnp.logical_and(e,q)
        pl.when(e)(fn)
    def slot_base(order):
        sizes={"x":2,"y":2,"z":zn}
        base={};cur=0
        for k,dim in enumerate(order):
            n=1
            for q in order[k+1:]: n*=sizes[q]
            if dim=="z": n*=2*zn
            base[dim]=cur; cur+=n
        return base,cur
    def slot(p,dim,side,dest):
        order=parts[p][2][::-1]
        base,_=slot_base(order)
        k=order.index(dim)
        v={"x":dest[0],"z":dest[1],"y":dest[2]}
        idx=0
        for q in order[k+1:]:
            idx=idx*(zn if q=="z" else 2)+v[q]
        if dim=="z": idx=(idx*zn+dest[1])*2+side
        return base[dim]+idx
    evs=[]
    for p in range(nP):
        for it in items():
            if abs(it[2])<=zn-1: evs.append((-hops(it),p,it))
    evs.sort(key=lambda e:e[0])
    seq=[(p,it) for _,p,it in evs]
    def core_dsc(p,it,mine):
        r0,rn,_=parts[p]
        s2,z2,y2=where(it)
        idx=(s2*zn+z2)*2+y2
        cc=c if mine else 1-c
        return pltpu.make_async_remote_copy(g_ref.at[s2,(z2*2+y2)*2+cc,pl.ds(r0,rn)],land.at[idx,pl.ds(r0,rn)],cs.at[p,idx],cr.at[p,idx],device_id=sib,device_id_type=MESH)
    for p,it in seq:
        guarded(conds(it),lambda p=p,it=it: core_dsc(p,it,False).start())
    for kind,ref in enumerate((dx_ref,y_ref)):
        cut_strips(place_ref[...],ref,strips32)
        sendbuf[kind]=strips32[...].astype(jnp.bfloat16)
    def load(i):
        p,it=seq[i]
        r0,rn,_=parts[p]
        s2,z2,y2=where(it)
        return pltpu.make_async_copy(g_ref.at[s2,(z2*2+y2)*2+c,pl.ds(r0,rn)],buf.at[i%NB,pl.ds(0,rn)],lsem.at[i%NB])
    NB=buf.shape[0]
    for i in range(min(NB-1,len(seq))):
        guarded(conds(seq[i][1]),lambda i=i: load(i).start())
    def contribs(p,it):
        order=parts[p][2][::-1]
        diff={"x":it[0],"y":it[1],"z":it[2]}
        out=[];nxt=None
        for dim in order:
            if dim=="z":
                if it[2]==0: out+=[("z",0,z>0),("z",1,z<zn-1)]
                elif it[2]>0: out.append(("z",0,z>0))
                else: out.append(("z",1,z<zn-1))
                if it[2]!=0: nxt="r" if it[2]>0 else "l"; break
            else:
                if diff[dim]: nxt=dim; break
                out.append((dim,0,None))
        return out,nxt
    semoff=[0]
    for p in range(nP): semoff.append(semoff[-1]+slot_base(parts[p][2][::-1])[1])
    def out_dsc(p,it,nxt):
        r0,rn,_=parts[p]
        dest=where(it)
        s2,z2,y2=dest
        idx=(s2*zn+z2)*2+y2
        dim="z" if nxt in "lr" else nxt
        side=1 if nxt=="l" else 0
        sl=slot(p,dim,side,dest)
        dev={"x":(1-s,d),"y":(s,(z*2+1-y)*2+c),"l":(s,d-4),"r":(s,d+4)}[nxt]
        return pltpu.make_async_remote_copy(land.at[idx,pl.ds(r0,rn)],lks[p].at[sl],ssem.at[p,idx],rsem.at[semoff[p]+sl],device_id=dev,device_id_type=MESH)
    def settle():
        rest_of=vland.at[pl.ds(0,total_dev-1)]
        bulk=pltpu.make_async_remote_copy(rest_of,rest_of,vsend,vrecv,device_id=(0,0),device_id_type=MESH)
        bulk.wait_recv()
        bulk.wait_send()
        vo_ref[...]=jnp.sum(vland[...],axis=0)
        back()
        for batch in range(2):
            strips32[...]=returned[batch*peers:(batch+1)*peers].astype(jnp.float32)
            join_strips(picks_ref[batch],strips32,res_ref.at[batch])
    for i,(p,it) in enumerate(seq):
        r0,rn,_=parts[p]
        if i==len(seq)*GIVE_NUM//GIVE_DEN: back=give_back(s,d,me,peers,sendbuf,returned,tlocal,tsend,trecv)
        if i==len(seq)*SETTLE_NUM//SETTLE_DEN: settle()
        if i+NB-1<len(seq):
            guarded(conds(seq[i+NB-1][1]),lambda i=i: load(i+NB-1).start())
        def ev(i=i,p=p,it=it,r0=r0,rn=rn):
            dest=where(it)
            s2,z2,y2=dest
            idx=(s2*zn+z2)*2+y2
            con,nxt=contribs(p,it)
            lk=lks[p]
            load(i).wait()
            core_dsc(p,it,True).wait_recv()
            plain=[x for x in con if x[2] is None]
            cond=[x for x in con if x[2] is not None]
            def rdsc(dim,side):
                sl=slot(p,dim,side,dest)
                return pltpu.make_async_remote_copy(lk.at[sl],lk.at[sl],ssem.at[p,idx],rsem.at[semoff[p]+sl],device_id=sib,device_id_type=MESH),sl
            for dim,side,_ in plain: rdsc(dim,side)[0].wait_recv()
            for dim,side,cnd in cond:
                pl.when(cnd)(lambda dim=dim,side=side: rdsc(dim,side)[0].wait_recv())
            if not cond: variants=[(None,plain)]
            elif len(cond)==1:
                variants=[(cond[0][2],plain+cond),(jnp.logical_not(cond[0][2]),plain)]
            else:
                a,b=cond
                variants=[(jnp.logical_and(a[2],b[2]),plain+cond),(jnp.logical_and(a[2],jnp.logical_not(b[2])),plain+[a]),
                          (jnp.logical_and(jnp.logical_not(a[2]),b[2]),plain+[b])]
            def total(lst):
                slots=[slot(p,dim,side,dest) for dim,side,_ in lst]
                CH=16
                def body(k,_):
                    ro=pl.multiple_of(k*CH,CH)
                    acc=buf[i%NB,pl.ds(ro,CH),:].astype(jnp.float32)+land[idx,pl.ds(r0+ro,CH),:].astype(jnp.float32)
                    for sl in slots: acc=acc+lk[sl,pl.ds(ro,CH),:].astype(jnp.float32)
                    if nxt is None: obuf[pl.ds(r0+ro,CH),:]=acc
                    else: land[idx,pl.ds(r0+ro,CH),:]=acc.astype(jnp.bfloat16)
                    return 0
                lax.fori_loop(0,rn//CH,body,0)
            for cnd,lst in variants:
                if cnd is None: total(lst)
                else: pl.when(cnd)(lambda lst=lst: total(lst))
            if nxt is not None: out_dsc(p,it,nxt).start()
            else: pltpu.make_async_copy(obuf.at[pl.ds(r0,rn)],o_ref.at[pl.ds(r0,rn)],osem.at[p]).start()
        guarded(conds(it),ev)
    for p,it in seq:
        def fin(p=p,it=it):
            core_dsc(p,it,False).wait_send()
            nxt=contribs(p,it)[1]
            if nxt is not None: out_dsc(p,it,nxt).wait_send()
        guarded(conds(it),fin)
    for p,(r0,rn,_) in enumerate(parts):
        pltpu.make_async_copy(obuf.at[pl.ds(r0,rn)],o_ref.at[pl.ds(r0,rn)],osem.at[p]).wait()


def slot_count(order,zn):
    sizes={"x":2,"y":2,"z":zn};cur=0
    for k,dim in enumerate(order):
        n=1
        for q in order[k+1:]: n*=sizes[q]
        if dim=="z": n*=2*zn
        cur+=n
    return cur
def rs(g,v,dx,y,place,picks,block,parts,zn,cid=1,nb=4):
    n=len(parts)
    cnt=[slot_count(p[2][::-1],zn) for p in parts]
    mx=max(p[1] for p in parts)
    return pl.pallas_call(functools.partial(rs_kernel,parts,zn),
        out_shape=[jax.ShapeDtypeStruct((480,1280),jnp.float32),jax.ShapeDtypeStruct(v.shape[1:],jnp.float32),
            jax.ShapeDtypeStruct((2,)+dx.shape,jnp.bfloat16)],
        in_specs=[pl.BlockSpec(memory_space=pl.ANY)]+[pl.BlockSpec(memory_space=pltpu.VMEM)]*5,
        out_specs=[pl.BlockSpec(memory_space=pl.ANY)]+[pl.BlockSpec(memory_space=pltpu.VMEM)]*2,
        scratch_shapes=[pltpu.VMEM((4*zn,480,1280),jnp.bfloat16),pltpu.VMEM((nb,mx,1280),jnp.bfloat16),pltpu.VMEM((480,1280),jnp.float32),pltpu.VMEM(v.shape,jnp.float32),
            pltpu.VMEM((4*zn,)+block,jnp.float32),pltpu.VMEM((2,4*zn)+block,jnp.bfloat16),pltpu.VMEM((8*zn,)+block,jnp.bfloat16)]
          +[pltpu.VMEM((cnt[p],parts[p][1],1280),jnp.bfloat16) for p in range(n)]
          +[pltpu.SemaphoreType.DMA((n,4*zn)),pltpu.SemaphoreType.DMA((sum(cnt),)),
          pltpu.SemaphoreType.DMA((n,4*zn)),pltpu.SemaphoreType.DMA((n,4*zn)),pltpu.SemaphoreType.DMA((nb,)),pltpu.SemaphoreType.DMA((n,))]+[pltpu.SemaphoreType.DMA]*5,
        compiler_params=pltpu.CompilerParams(collective_id=cid,has_side_effects=True,vmem_limit_bytes=62*2**20))(g,v,dx,y,place,picks)


def as_row(column):
    rows = column.shape[0]
    return jnp.broadcast_to(column, (rows, 128)).T[0:1, :]


def as_column(row):
    size = row.shape[1]
    return jnp.broadcast_to(row, (128, size)).T[:, 0:1]


def ones_where(flag):
    return jnp.where(flag, 1.0, 0.0)


def gather_events(parts,zn,place,own,w_ref,ssem,rsem,cs,cr):
    s,d,z,y,c=place
    KIND={"x":0,"y":1,"l":2,"r":3}
    def where(it):
        s2=1-s if it[0] else s
        y2=1-y if it[1] else y
        z2=z+it[2]
        return s2,z2,y2
    def dsc(p,it,kind):
        r0,rn,order=parts[p]
        s2,z2,y2=where(it)
        idx=s2*(2*zn)+z2*2+y2
        is_own=it==(0,0,0)
        src=own.at[pl.ds(r0,rn)] if is_own else w_ref.at[s2,(z2*2+y2)*2+c,pl.ds(r0,rn)]
        dst=w_ref.at[s2,(z2*2+y2)*2+c,pl.ds(r0,rn)]
        if kind=="core":
            dev=(s,(z*2+y)*2+1-c)
            return pltpu.make_async_remote_copy(src,dst,cs.at[p,idx],cr.at[p,idx],device_id=dev,device_id_type=MESH)
        dev={"x":(1-s,d),"y":(s,(z*2+1-y)*2+c),"l":(s,d-4),"r":(s,d+4)}[kind]
        return pltpu.make_async_remote_copy(src,dst,ssem.at[KIND[kind],p,idx],rsem.at[p,idx],device_id=dev,device_id_type=MESH)
    def cdsc(p,it):
        r0,rn,order=parts[p]
        s2,z2,y2=where(it)
        idx=s2*(2*zn)+z2*2+y2
        dst=w_ref.at[s2,(z2*2+y2)*2+1-c,pl.ds(r0,rn)]
        return pltpu.make_async_remote_copy(dst,dst,cs.at[p,idx],cr.at[p,idx],device_id=(s,(z*2+y)*2+1-c),device_id_type=MESH)
    def conds(it,kind):
        cs_=[]
        if it[2]<0: cs_.append(z+it[2]>=0)
        if it[2]>0: cs_.append(z+it[2]<=zn-1)
        if kind=="l": cs_.append(z>0)
        if kind=="r": cs_.append(z<zn-1)
        return cs_
    def guarded(cl,fn):
        if not cl: fn(); return
        e=cl[0]
        for q in cl[1:]: e=jnp.logical_and(e,q)
        pl.when(e)(fn)
    def sends(p,it):
        order=parts[p][2]
        a=arrival(order,it)
        ks=[]
        if a is not None and order[a]=="z": ks.append("l" if it[2]>0 else "r")
        for dim in order[(a+1) if a is not None else 0:]:
            ks += ["r","l"] if dim=="z" else [dim]
        ks.append("core")
        return ks
    evs=[]
    for p in range(len(parts)):
        for it in items():
            if abs(it[2])<zn: evs.append((hops(it),p,it))
    evs.sort(key=lambda e:e[0])
    first=[]
    later=[]
    for h,p,it in evs:
        def ev(p=p,it=it):
            if it!=(0,0,0): dsc(p,it,"x").wait_recv()
            for k in sends(p,it):
                guarded(conds((0,0,0),k), lambda k=k: dsc(p,it,k).start())
        (later if h else first).append(lambda it=it,ev=ev: guarded(conds(it,None),ev))
    def finish():
        for _,p,it in evs:
            def fin(p=p,it=it):
                cdsc(p,it).wait_recv()
                for k in sends(p,it):
                    guarded(conds((0,0,0),k), lambda k=k: dsc(p,it,k).wait_send())
            guarded(conds(it,None),fin)
    return first,later,finish


def enter_kernel(
    parts, zn, mats_ref, packet_ref, deal_ref, tokens_ref,
    w_ref, shared_ref, x_ref, cot_ref, picks_ref, place_ref,
    own, wide_rows, strips32, sendbuf, landed, order,
    own_sem, lsem, ssem, rsem, cs, cr, psend, precv, tsend, trecv,
):
    s, d, z, y, c = coords()
    peers = 4 * zn
    total = 2 * peers
    me = s * peers + d
    batches, rows, width = tokens_ref.shape
    f32, b16 = jnp.float32, jnp.bfloat16
    cast_in = pltpu.make_async_copy(mats_ref, wide_rows, own_sem)
    cast_in.start()
    greet(total, me, peers)
    shared_ref[me] = packet_ref[...]

    def tell(step, carry):
        other = lax.rem(me + step, total)
        pltpu.make_async_remote_copy(
            packet_ref, shared_ref.at[me], psend, precv,
            device_id=(other // peers, lax.rem(other, peers)), device_id_type=MESH,
        ).start()
        return carry

    lax.fori_loop(1, total, tell, 0)
    cast_in.wait()
    own[...] = wide_rows[...].astype(b16)
    lc = pltpu.make_async_copy(own, w_ref.at[s, d], lsem)
    lc.start()
    start_events, rest_events, finish = gather_events(
        parts, zn, (s, d, z, y, c), own, w_ref, ssem, rsem, cs, cr
    )
    for event in start_events:
        event()
    sub = lax.broadcasted_iota(jnp.int32, (rows, rows), 0).astype(f32)
    lane = lax.broadcasted_iota(jnp.int32, (rows, rows), 1).astype(f32)
    mine_row = jnp.where(s == 0, deal_ref[0:1, :], deal_ref[1:2, :])
    mine_col = as_column(mine_row)
    rank_col = jnp.sum(ones_where(mine_row < mine_col), axis=1, keepdims=True)
    order[...] = ones_where(lane == rank_col).astype(b16)
    rank_row = jnp.sum(ones_where(mine_col < mine_row), axis=0, keepdims=True)
    place_ref[...] = ones_where(sub == rank_row).astype(b16)
    rest = shared_ref.at[pl.ds(0, total - 1)]
    bulk = pltpu.make_async_remote_copy(
        rest, rest, psend, precv, device_id=(0, 0), device_id_type=MESH
    )
    bulk.wait_recv()
    index_col = lax.broadcasted_iota(jnp.int32, (rows, 1), 0).astype(f32)
    ids_col = index_col + (d * rows).astype(f32)
    for batch in range(batches):

        def look(block, found):
            known = shared_ref[s * peers + block]
            for line in range(rows // 128):
                at = batch * (rows // 128) + line
                found = jnp.where(ids_col == known[at : at + 1, :], block.astype(f32), found)
            return found

        found = lax.fori_loop(0, peers, look, jnp.zeros((rows, 128), f32))
        key_col = jnp.sum(found, axis=1, keepdims=True) * rows + index_col
        key_row = as_row(key_col)
        rank_row = jnp.sum(ones_where(key_col < key_row), axis=0, keepdims=True)
        rank_col = jnp.sum(ones_where(key_row < key_col), axis=1, keepdims=True)
        picks_ref[batch] = ones_where(lane == rank_col).astype(b16)
        pick = ones_where(sub == rank_row).astype(b16)
        cut_strips(pick, tokens_ref.at[batch], strips32)
        sendbuf[batch] = strips32[...].astype(b16)

    landed[me] = sendbuf[s, d]

    early = len(rest_events) * HAND_NUM // HAND_DEN
    for event in rest_events[:early]:
        event()

    def give(step, carry):
        other = lax.rem(me + step, total)
        sec, dp = other // peers, lax.rem(other, peers)
        pltpu.make_async_remote_copy(
            sendbuf.at[sec, dp], landed.at[me], tsend, trecv.at[s],
            device_id=(sec, dp), device_id_type=MESH,
        ).start()
        return carry

    lax.fori_loop(1, total, give, 0)
    def take(kind, out_ref):
        pl.when(s == kind)(
            lambda: bulk_copy(landed, peers - 1, tsend, trecv.at[kind]).wait_recv()
        )
        pl.when(s != kind)(lambda: bulk_copy(landed, peers, tsend, trecv.at[kind]).wait_recv())
        strips32[...] = landed[pl.ds(kind * peers, peers)].astype(f32)
        join_strips(order[...], strips32, out_ref)

    middle = len(rest_events) * TAKE_NUM // TAKE_DEN
    for event in rest_events[early:middle]:
        event()
    take(0, x_ref)
    take(1, cot_ref)
    for event in rest_events[middle:]:
        event()
    finish()
    lc.wait()
    bulk.wait_send()
    most = landed.at[pl.ds(0, total - 1)]
    pltpu.make_async_remote_copy(
        most, most, tsend, trecv.at[0], device_id=(0, 0), device_id_type=MESH
    ).wait_send()


def enter(mats, packet, deal, tokens, parts, zn):
    n = len(parts)
    peers = 4 * zn
    batches, rows, width = tokens.shape
    strip_rows = rows // peers * (width // 128)
    f32, b16 = jnp.float32, jnp.bfloat16
    vm = pl.BlockSpec(memory_space=pltpu.VMEM)
    hbm = pl.BlockSpec(memory_space=pl.ANY)
    dma = pltpu.SemaphoreType.DMA
    return pl.pallas_call(
        functools.partial(enter_kernel, parts, zn),
        out_shape=[
            jax.ShapeDtypeStruct((2, peers) + mats.shape, b16),
            jax.ShapeDtypeStruct((2 * peers,) + packet.shape, f32),
            jax.ShapeDtypeStruct((rows, width), b16),
            jax.ShapeDtypeStruct((rows, width), b16),
            jax.ShapeDtypeStruct((batches, rows, rows), b16),
            jax.ShapeDtypeStruct((rows, rows), b16),
        ],
        in_specs=[hbm, vm, vm, vm],
        out_specs=[hbm, vm, vm, vm, vm, vm],
        scratch_shapes=[
            pltpu.VMEM(mats.shape, b16),
            pltpu.VMEM(mats.shape, f32),
            pltpu.VMEM((peers, strip_rows, 128), f32),
            pltpu.VMEM((batches, peers, strip_rows, 128), b16),
            pltpu.VMEM((2 * peers, strip_rows, 128), b16),
            pltpu.VMEM((rows, rows), b16),
            dma, dma, dma((4, n, peers)), dma((n, peers)), dma((n, peers)), dma((n, peers)),
            dma, dma, dma, dma((2,)),
        ],
        compiler_params=pltpu.CompilerParams(
            collective_id=0, has_side_effects=True, vmem_limit_bytes=VMEM_LIMIT
        ),
        name="enter",
    )(mats, packet, deal, tokens)


def one_hot(rank):
    rows = rank.shape[0]
    return (rank[None, :] == jnp.arange(rows, dtype=jnp.int32)[:, None]).astype(jnp.bfloat16)


def rank_of(key):
    return jnp.sum((key[None, :] < key[:, None]).astype(jnp.int32), axis=1)


def padded(flat):
    lead, size = flat.shape
    full = -(-size // 1024) * 1024
    return jnp.pad(flat, ((0, 0), (0, full - size))).reshape(lead, full // 128, 128)


def enter_plain(own, packet, deal, tokens, peers):
    section = lax.axis_index("section")
    batches, rows, width = tokens.shape
    per_peer = rows // peers
    shared = lax.all_gather(packet, BOTH, axis=0)
    low = own.astype(jnp.bfloat16)
    mats = lax.all_gather(low, BOTH, axis=0, tiled=True).reshape((2, peers) + own.shape)
    flat = shared.reshape(2, peers, -1)[:, :, : batches * rows]
    dealt = jnp.where(section == 0, flat[0], flat[1]).astype(jnp.int32).reshape(peers, batches, rows)
    own_rows = lax.axis_index("dp") * rows + jnp.arange(rows, dtype=jnp.int32)
    blocks = jnp.arange(peers, dtype=jnp.int32)
    picks = []
    sends = []
    for batch in range(batches):
        hit = dealt[:, batch][None, :, :] == own_rows[:, None, None]
        target = jnp.sum(jnp.where(hit, blocks[None, :, None], 0), axis=(1, 2))
        pick = one_hot(rank_of(target * rows + jnp.arange(rows, dtype=jnp.int32)))
        picks.append(pick.T)
        sends.append(nn(pick, tokens[batch]).astype(jnp.bfloat16))
    outgoing = jnp.stack(sends).reshape(2 * peers, per_peer, width)
    arrived = lax.all_to_all(outgoing, BOTH, split_axis=0, concat_axis=0, tiled=True)
    arrived = arrived.reshape(2, rows, width)
    place = one_hot(rank_of(jnp.where(section == 0, deal[0], deal[1])))
    x, cot = (tn(place, arrived[kind]).astype(jnp.bfloat16) for kind in range(2))
    return mats, shared, x, cot, jnp.stack(picks), place


def leave_plain(terms, small, down, final, place, picks, peers):
    sections, _, rows, width = terms.shape
    terms = terms.reshape(sections * peers * rows, width)
    total = lax.psum_scatter(terms, BOTH, scatter_dimension=0, tiled=True).astype(jnp.float32)
    small = lax.psum_scatter(small, BOTH, scatter_dimension=0, tiled=True)[0]
    back = jnp.stack([nn(place, down), nn(place, final)]).astype(jnp.bfloat16)
    count = down.shape[0]
    back = back.reshape(2 * peers, count // peers, width)
    back = lax.all_to_all(back, BOTH, split_axis=0, concat_axis=0, tiled=True)
    back = back.reshape(-1, count, width)
    results = jnp.stack([nn(picks[batch], back[batch]) for batch in range(back.shape[0])])
    return total, small, results.astype(jnp.bfloat16)


def local(entering, deal, seq_lens, mats, gains, biases):
    section = lax.axis_index("section")
    peers = lax.axis_size("dp")
    arrival = entering[0]
    batches, rows, width = arrival.shape
    per = 2 * width // peers
    vecs = jnp.concatenate([gains[0], biases[0]]).astype(jnp.bfloat16).astype(jnp.float32)
    packet = jnp.concatenate([deal.reshape(-1).astype(jnp.float32), vecs])
    packet = padded(packet[None])[0]
    packet = jnp.pad(packet, ((0, -packet.shape[0] % 8), (0, 0)))
    args = (mats[0], packet, deal.astype(jnp.float32), arrival)
    direct = peers == 16
    entered = enter(*args, GATHER_PARTS, peers // 4) if direct else enter_plain(*args, peers)
    all_mats, shared, tokens, cotangent, picks, place = entered
    shared = shared.reshape(2, peers, -1)
    small = shared[:, :, batches * rows : batches * rows + 2 * per].reshape(2, peers, 2, per)
    small = jnp.swapaxes(small, 1, 2).reshape(2, 4, width)
    small = jnp.pad(small, ((0, 0), (0, 4), (0, 0)))
    all_mats = all_mats.reshape(2, 6 * width, width)
    lens = jnp.where(section == 0, seq_lens[0, 0], seq_lens[1, 0])
    ends = jnp.cumsum(lens)
    positions = jnp.arange(rows, dtype=jnp.int32)
    segment = jnp.sum((positions[:, None] >= ends[None, :]).astype(jnp.int32), axis=1)
    segc, segr = segment[:, None], segment[None]
    final, terms, down, vec_grads = both_layers(
        all_mats, tokens, small, segc, segr, cotangent
    )
    terms = terms.reshape(2, peers, -1, width)
    vec_terms = vec_grads[:, :4].reshape(2, 2, peers, per)
    vec_terms = padded(jnp.swapaxes(vec_terms, 1, 2).reshape(2 * peers, 2 * per))
    block = (rows // peers * (width // 128), 128)
    if direct:
        shard_mats, vec_total, results = rs(
            terms, vec_terms, down, final, place, picks, block, SCATTER_PARTS, peers // 4
        )
    else:
        shard_mats, vec_total, results = leave_plain(
            terms, vec_terms, down, final, place, picks, peers
        )
    vec_total = vec_total.reshape(-1)
    return (
        results[None],
        shard_mats[None],
        vec_total[None, :per],
        vec_total[None, per : 2 * per],
    )


def solution(mesh):
    in_specs = (
        P("section", None, "dp", None),
        P(None, "dp"),
        P(None, "dp", None),
        P("section", "dp", None),
        P("section", "dp"),
        P("section", "dp"),
    )
    out_specs = (
        P("section", None, "dp", None),
        P("section", "dp", None),
        P("section", "dp"),
        P("section", "dp"),
    )
    return jax.shard_map(local, mesh=mesh, in_specs=in_specs, out_specs=out_specs, check_vma=False)
```

time: 527 us -> 477 us (0.905); the launches traced: 518 us -> 473 us
  Pallas kernels: 503 us -> 458 us
    pallas_call x4 -> x1, Pallas kernels: 146 us -> 101 us  [both_layers(): pl.pallas_call(both_layers_kernel, out_shape=[jax.ShapeDtypeStruct(flat,...]
where the time goes in v6:
time: 477 us; the launch traced here: 473 us
  Pallas kernels  458 us (96%)
  local copies, waits for them, and re-layouts  11.6 us (2%)
    pallas_call x1, Pallas kernels, enter(): pl.pallas_call(functools.partial(enter_kernel, parts, zn), out_shape=[jax...  183 us
    pallas_call x1, Pallas kernels, rs(): pl.pallas_call(functools.partial(rs_kernel, parts, zn), out_shape=[jax.Sh...  174 us
    pallas_call x1, Pallas kernels, both_layers(): pl.pallas_call(both_layers_kernel, out_shape=[jax.ShapeDtypeStruct(flat,...  101 us

profile of v6, /device:TPU:0, one launch (start us, length us, event | category | flops | bytes accessed | tf_op | source)
XLA Modules:
  0.0 473.3 jit_solution(6096169680688823172)
XLA Ops:
  0.6 0.7 fusion
  1.3 0.2 reduce-window.8
  1.5 0.7 convert_reduce_fusion.1
  2.2 0.1 maximum_convert_fusion
  2.3 0.1 convert_reduce_fusion
  2.4 0.6 broadcast_in_dim.25.refs_4_
  3.0 0.7 convert_element_type.20.deal_ref
  3.7 0.0 copy-start.1
  3.7 0.6 pad.12
  4.3 0.8 broadcast_in_dim.30.refs_3_
  5.1 0.0 copy-done.1
  5.1 182.9 %enter.1 = (bf16[2,16,480,1280]{3,2,1,0:T(8,128)(2,1)}, f32[32,16,128]{2,1,0:T(8,128)}, bf16[384,1280]{1,0:T(8,128)(2,1)}, bf16[384,1280]{1,0:T(8,128)(2,1)}, bf...) custom-call(f32[480,1280]{1,0:T(8,128)} %bitcast.22, f32[16,128]{1,0:T(8,128)} %bitcast.29, f32[2,384]{1,0:T(2,128)} %copy-done.1, ...), custom_call_target="tpu_custom_call" | custom-call | tf_op jit(solution)/shard_map/enter/pallas_call | solution.py:830
  188.0 1.0 reshape.79
  189.0 0.1 reshape.80
  189.1 0.1 reshape.81
  189.2 0.6 pad.13.refs_2_
  189.8 101.4 %both_layers.1 = (bf16[384,1280]{1,0:T(8,128)(2,1)}, bf16[2,7680,1280]{2,1,0:T(8,128)(2,1)}, bf16[384,1280]{1,0:T(8,128)(2,1)}, f32[2,8,1280]{2,1,0:T(8,128)}) custom-call(bf16[2,7680,1280]{2,1,0:T(8,128)(2,1)} %bitcast.20, bf16[384,1280]{1,0:T(8,128)(2,1)} %get-tuple-element.18.refs_1_, f32[2,8,1280]{2,1,0:T(8,128)} %pad.13.refs_2_, ...), custom_call_target="tpu_custom_call" | custom-call | tf_op jit(solution)/shard_map/both_layers/pallas_call | solution.py:378
  291.2 0.9 slice.21
  292.1 0.1 reshape.84
  292.2 0.1 copy.16
  292.3 0.1 reshape.85
  292.4 0.7 copy.17
  293.1 174.1 %shard_map.93 = (f32[480,1280]{1,0:T(8,128)}, f32[8,128]{1,0:T(8,128)}, bf16[2,384,1280]{2,1,0:T(8,128)(2,1)}) custom-call(bf16[2,16,480,1280]{3,2,1,0:T(8,128)(2,1)} %bitcast.21, f32[32,8,128]{2,1,0:T(8,128)} %bitcast.26, bf16[384,1280]{1,0:T(8,128)(2,1)} %get-tuple-element.23.dx_ref, bf16[384,1280]{1,0:T(8,128)(2,1)} %get-tuple-element.24.y_ref, ...), custom_call_target="tpu_custom_call" | custom-call | tf_op jit(solution)/shard_map/pallas_call | solution.py:615
  467.2 0.0 copy-start
  467.2 1.5 fusion.1
  468.7 2.9 copy.20
  471.6 0.0 copy-done
  471.6 1.4 copy.21
  (6 shorter events, 0.0 us)
Async XLA Ops:
  3.7 1.4 copy-start.1
  467.2 4.4 copy-start

commit v7 on v6

--- a/solution.py
+++ b/solution.py
@@ -163,12 +163,12 @@
 
 
 def both_layers_kernel(*refs):
-    mats_ref, x_ref, vec_ref, segc_ref, segr_ref, cot_ref = refs[:6]
-    y_ref, grads_ref, dx_ref, dvec_ref = refs[6:10]
+    mats_ref, x_ref, vec_ref, lens_ref, cot_ref = refs[:5]
+    y_ref, grads_ref, dx_ref, dvec_ref = refs[5:9]
     (
         held, qkvs, probs, atts, mids, us, between, act, low, mask, dqkv, dscore, turned,
     stage, sems, out_sems,
-    ) = refs[10:]
+    ) = refs[9:]
     rows, width = x_ref.shape
     depth = width // HEADS
     scale = depth ** (-0.5)
@@ -201,9 +201,16 @@
         return held.at[slot]
 
     after(-1)
-    qi = lax.broadcasted_iota(jnp.int32, (rows, rows), 0)
-    ki = lax.broadcasted_iota(jnp.int32, (rows, rows), 1)
-    mask[...] = jnp.where((segc_ref[...] == segr_ref[...]) & (ki <= qi), 3e38, NEG)
+    batch = lax.axis_index("section")
+    row = lax.broadcasted_iota(jnp.int32, (rows, 1), 0)
+    col = lax.broadcasted_iota(jnp.int32, (1, rows), 1)
+    end = jnp.int32(0)
+    row_part, col_part = jnp.zeros((rows, 1), jnp.int32), jnp.zeros((1, rows), jnp.int32)
+    for place in range(lens_ref.shape[1]):
+        end = end + lens_ref[batch, place]
+        row_part = row_part + jnp.where(row >= end, 1, 0)
+        col_part = col_part + jnp.where(col >= end, 1, 0)
+    mask[...] = jnp.where((row_part == col_part) & (col <= row), 3e38, NEG)
 
     def forward(layer, source, out_ref):
         qkv, prob, att, mid, u = (ref.at[layer] for ref in (qkvs, probs, atts, mids, us))
@@ -219,7 +226,6 @@
                     part = part * (scale * LOG2E)
                 qkv[index, :, cols] = part.astype(b16)
             after(use + index)
-        att[...] = jnp.zeros_like(att)
 
         def head_group(group, carry):
             blocks = range(rows // QB)
@@ -317,7 +323,6 @@
         for cols in tiles:
             act[:, cols] = nt(low[...], weight[cols, :]).astype(b16)
         after(use + 2)
-        dqkv[...] = jnp.zeros_like(dqkv)
 
         def head_group(group, carry):
             blocks = range(rows // QB)
@@ -368,7 +373,7 @@
         put(*in_slot[slot], slot).wait()
 
 
-def both_layers(mats, x, vec, segc, segr, cot):
+def both_layers(mats, x, vec, lens, cot):
     rows, width = x.shape
     f32, b16 = jnp.float32, jnp.bfloat16
     vm = pl.BlockSpec(memory_space=pltpu.VMEM)
@@ -383,7 +388,7 @@
             jax.ShapeDtypeStruct(flat, b16),
             jax.ShapeDtypeStruct((2, 8, width), f32),
         ],
-        in_specs=[hbm, vm, vm, vm, vm, vm],
+        in_specs=[hbm, vm, vm, pl.BlockSpec(memory_space=pltpu.SMEM), vm],
         out_specs=[vm, hbm, vm, vm],
         scratch_shapes=[
             pltpu.VMEM((SLOTS, width, width), b16),
@@ -407,7 +412,7 @@
             vmem_limit_bytes=63 * 2**20,
         ),
         name="both_layers",
-    )(mats, x, vec, segc, segr, cot)
+    )(mats, x, vec, lens, cot)
 
 
 def give_back(s, d, me, peers, sendbuf, returned, local_sem, send_sem, recv_sem):
@@ -710,9 +715,9 @@
 
 
 def enter_kernel(
-    parts, zn, mats_ref, packet_ref, deal_ref, tokens_ref,
+    parts, zn, mats_ref, deal_in, vecs_ref, tokens_ref,
     w_ref, shared_ref, x_ref, cot_ref, picks_ref, place_ref,
-    own, wide_rows, strips32, sendbuf, landed, order,
+    packet_ref, deal_ref, own, wide_rows, strips32, sendbuf, landed, order,
     own_sem, lsem, ssem, rsem, cs, cr, psend, precv, tsend, trecv,
 ):
     s, d, z, y, c = coords()
@@ -723,7 +728,15 @@
     f32, b16 = jnp.float32, jnp.bfloat16
     cast_in = pltpu.make_async_copy(mats_ref, wide_rows, own_sem)
     cast_in.start()
-    greet(total, me, peers)
+    signal_all(total, me, peers)
+    deal_ref[...] = deal_in[...].astype(f32)
+    lines = rows // 128
+    for batch in range(batches):
+        for line in range(lines):
+            at = batch * lines + line
+            packet_ref[at : at + 1, :] = deal_ref[batch : batch + 1, line * 128 : (line + 1) * 128]
+    packet_ref[batches * lines :, :] = vecs_ref[...]
+    wait_all(total)
     shared_ref[me] = packet_ref[...]
 
     def tell(step, carry):
@@ -818,10 +831,11 @@
     ).wait_send()
 
 
-def enter(mats, packet, deal, tokens, parts, zn):
+def enter(mats, deal, vecs, tokens, parts, zn):
     n = len(parts)
     peers = 4 * zn
     batches, rows, width = tokens.shape
+    packet = (batches * (rows // 128) + vecs.shape[0], 128)
     strip_rows = rows // peers * (width // 128)
     f32, b16 = jnp.float32, jnp.bfloat16
     vm = pl.BlockSpec(memory_space=pltpu.VMEM)
@@ -831,7 +845,7 @@
         functools.partial(enter_kernel, parts, zn),
         out_shape=[
             jax.ShapeDtypeStruct((2, peers) + mats.shape, b16),
-            jax.ShapeDtypeStruct((2 * peers,) + packet.shape, f32),
+            jax.ShapeDtypeStruct((2 * peers,) + packet, f32),
             jax.ShapeDtypeStruct((rows, width), b16),
             jax.ShapeDtypeStruct((rows, width), b16),
             jax.ShapeDtypeStruct((batches, rows, rows), b16),
@@ -840,6 +854,8 @@
         in_specs=[hbm, vm, vm, vm],
         out_specs=[hbm, vm, vm, vm, vm, vm],
         scratch_shapes=[
+            pltpu.VMEM(packet, f32),
+            pltpu.VMEM(deal.shape, f32),
             pltpu.VMEM(mats.shape, b16),
             pltpu.VMEM(mats.shape, f32),
             pltpu.VMEM((peers, strip_rows, 128), f32),
@@ -853,7 +869,7 @@
             collective_id=0, has_side_effects=True, vmem_limit_bytes=VMEM_LIMIT
         ),
         name="enter",
-    )(mats, packet, deal, tokens)
+    )(mats, deal, vecs, tokens)
 
 
 def one_hot(rank):
@@ -918,26 +934,26 @@
     arrival = entering[0]
     batches, rows, width = arrival.shape
     per = 2 * width // peers
+    direct = peers == 16
     vecs = jnp.concatenate([gains[0], biases[0]]).astype(jnp.bfloat16).astype(jnp.float32)
-    packet = jnp.concatenate([deal.reshape(-1).astype(jnp.float32), vecs])
-    packet = padded(packet[None])[0]
-    packet = jnp.pad(packet, ((0, -packet.shape[0] % 8), (0, 0)))
-    args = (mats[0], packet, deal.astype(jnp.float32), arrival)
-    direct = peers == 16
-    entered = enter(*args, GATHER_PARTS, peers // 4) if direct else enter_plain(*args, peers)
+    known = batches * rows
+    if direct:
+        lines = known // 128
+        full = -(-(lines * 128 + vecs.shape[0]) // 1024) * 8 - lines
+        vecs = jnp.pad(vecs, (0, full * 128 - vecs.shape[0])).reshape(full, 128)
+        entered = enter(mats[0], deal, vecs, arrival, GATHER_PARTS, peers // 4)
+    else:
+        packet = jnp.concatenate([deal.reshape(-1).astype(jnp.float32), vecs])
+        packet = padded(packet[None])[0]
+        entered = enter_plain(mats[0], packet, deal, arrival, peers)
     all_mats, shared, tokens, cotangent, picks, place = entered
     shared = shared.reshape(2, peers, -1)
     small = shared[:, :, batches * rows : batches * rows + 2 * per].reshape(2, peers, 2, per)
     small = jnp.swapaxes(small, 1, 2).reshape(2, 4, width)
     small = jnp.pad(small, ((0, 0), (0, 4), (0, 0)))
     all_mats = all_mats.reshape(2, 6 * width, width)
-    lens = jnp.where(section == 0, seq_lens[0, 0], seq_lens[1, 0])
-    ends = jnp.cumsum(lens)
-    positions = jnp.arange(rows, dtype=jnp.int32)
-    segment = jnp.sum((positions[:, None] >= ends[None, :]).astype(jnp.int32), axis=1)
-    segc, segr = segment[:, None], segment[None]
     final, terms, down, vec_grads = both_layers(
-        all_mats, tokens, small, segc, segr, cotangent
+        all_mats, tokens, small, seq_lens[:, 0, :], cotangent
     )
     terms = terms.reshape(2, peers, -1, width)
     vec_terms = vec_grads[:, :4].reshape(2, 2, peers, per)

time: 477 us -> 473 us (level)
  no operation moved by 1% of the time
where the time goes in v7:
time: 473 us; the launch traced here: 470 us
  Pallas kernels  458 us (97%)
  local copies, waits for them, and re-layouts  9.57 us (2%)
    pallas_call x1, Pallas kernels, enter(): pl.pallas_call(functools.partial(enter_kernel, parts, zn), out_shape=[jax...  183 us
    pallas_call x1, Pallas kernels, rs(): pl.pallas_call(functools.partial(rs_kernel, parts, zn), out_shape=[jax.Sh...  174 us
    pallas_call x1, Pallas kernels, both_layers(): pl.pallas_call(both_layers_kernel, out_shape=[jax.ShapeDtypeStruct(flat,...  101 us

profile of v7, /device:TPU:0, one launch (start us, length us, event | category | flops | bytes accessed | tf_op | source)
XLA Modules:
  0.0 469.6 jit_solution(17653837376380665755)
XLA Ops:
  0.6 0.7 convert_reduce_fusion
  1.3 0.7 fusion.4.vecs_ref
  2.0 182.8 %enter.1 = (bf16[2,16,480,1280]{3,2,1,0:T(8,128)(2,1)}, f32[32,16,128]{2,1,0:T(8,128)}, bf16[384,1280]{1,0:T(8,128)(2,1)}, bf16[384,1280]{1,0:T(8,128)(2,1)}, bf...) custom-call(f32[480,1280]{1,0:T(8,128)} %bitcast.24, s32[2,384]{1,0:T(2,128)} %deal_in.1, f32[10,128]{1,0:T(8,128)} %fusion.4.vecs_ref, ...), custom_call_target="tpu_custom_call" | custom-call | tf_op jit(solution)/shard_map/enter/pallas_call | solution.py:844
  184.9 1.0 reshape.43
  185.9 0.1 reshape.44
  186.0 0.1 reshape.45
  186.1 0.6 pad.14.refs_2_
  186.8 100.7 %both_layers.1 = (bf16[384,1280]{1,0:T(8,128)(2,1)}, bf16[2,7680,1280]{2,1,0:T(8,128)(2,1)}, bf16[384,1280]{1,0:T(8,128)(2,1)}, f32[2,8,1280]{2,1,0:T(8,128)}) custom-call(bf16[2,7680,1280]{2,1,0:T(8,128)(2,1)} %bitcast.23, bf16[384,1280]{1,0:T(8,128)(2,1)} %get-tuple-element.18.refs_1_, f32[2,8,1280]{2,1,0:T(8,128)} %pad.14.refs_2_, s32[2,3]{1,0:T(2,128)} %bitcast.31, ...), custom_call_target="tpu_custom_call" | custom-call | tf_op jit(solution)/shard_map/both_layers/pallas_call | solution.py:383
  287.5 0.9 slice.13
  288.4 0.1 reshape.47
  288.5 0.1 copy.12
  288.5 0.1 reshape.48
  288.7 0.7 copy.13
  289.3 174.1 %shard_map.93 = (f32[480,1280]{1,0:T(8,128)}, f32[8,128]{1,0:T(8,128)}, bf16[2,384,1280]{2,1,0:T(8,128)(2,1)}) custom-call(bf16[2,16,480,1280]{3,2,1,0:T(8,128)(2,1)} %bitcast.22, f32[32,8,128]{2,1,0:T(8,128)} %bitcast.28, bf16[384,1280]{1,0:T(8,128)(2,1)} %get-tuple-element.23.dx_ref, bf16[384,1280]{1,0:T(8,128)(2,1)} %get-tuple-element.24.y_ref, ...), custom_call_target="tpu_custom_call" | custom-call | tf_op jit(solution)/shard_map/pallas_call | solution.py:620
  463.5 0.0 copy-start
  463.5 1.5 fusion.5
  465.0 2.9 copy.16
  467.9 0.0 copy-done
  467.9 1.4 copy.17
  (3 shorter events, 0.0 us)
Async XLA Ops:
  463.5 4.4 copy-start

commit v8 on v7

--- a/solution.py
+++ b/solution.py
@@ -580,7 +580,7 @@
                           (jnp.logical_and(jnp.logical_not(a[2]),b[2]),plain+[b])]
             def total(lst):
                 slots=[slot(p,dim,side,dest) for dim,side,_ in lst]
-                CH=16
+                CH=32 if rn%32==0 else 16
                 def body(k,_):
                     ro=pl.multiple_of(k*CH,CH)
                     acc=buf[i%NB,pl.ds(ro,CH),:].astype(jnp.float32)+land[idx,pl.ds(r0+ro,CH),:].astype(jnp.float32)

time: 473 us -> 473 us (level)
  no operation moved by 1% of the time
where the time goes in v8:
time: 473 us; the launch traced here: 470 us
  Pallas kernels  458 us (97%)
  local copies, waits for them, and re-layouts  9.57 us (2%)
    pallas_call x1, Pallas kernels, enter(): pl.pallas_call(functools.partial(enter_kernel, parts, zn), out_shape=[jax...  183 us
    pallas_call x1, Pallas kernels, rs(): pl.pallas_call(functools.partial(rs_kernel, parts, zn), out_shape=[jax.Sh...  174 us
    pallas_call x1, Pallas kernels, both_layers(): pl.pallas_call(both_layers_kernel, out_shape=[jax.ShapeDtypeStruct(flat,...  101 us

profile of v8, /device:TPU:0, one launch (start us, length us, event | category | flops | bytes accessed | tf_op | source)
XLA Modules:
  0.0 469.6 jit_solution(14882348409757508640)
XLA Ops:
  0.6 0.7 convert_reduce_fusion
  1.3 0.7 fusion.4.vecs_ref
  2.0 182.8 %enter.1 = (bf16[2,16,480,1280]{3,2,1,0:T(8,128)(2,1)}, f32[32,16,128]{2,1,0:T(8,128)}, bf16[384,1280]{1,0:T(8,128)(2,1)}, bf16[384,1280]{1,0:T(8,128)(2,1)}, bf...) custom-call(f32[480,1280]{1,0:T(8,128)} %bitcast.24, s32[2,384]{1,0:T(2,128)} %deal_in.1, f32[10,128]{1,0:T(8,128)} %fusion.4.vecs_ref, ...), custom_call_target="tpu_custom_call" | custom-call | tf_op jit(solution)/shard_map/enter/pallas_call | solution.py:844
  184.9 1.0 reshape.43
  185.9 0.1 reshape.44
  186.0 0.1 reshape.45
  186.1 0.6 pad.14.refs_2_
  186.8 100.7 %both_layers.1 = (bf16[384,1280]{1,0:T(8,128)(2,1)}, bf16[2,7680,1280]{2,1,0:T(8,128)(2,1)}, bf16[384,1280]{1,0:T(8,128)(2,1)}, f32[2,8,1280]{2,1,0:T(8,128)}) custom-call(bf16[2,7680,1280]{2,1,0:T(8,128)(2,1)} %bitcast.23, bf16[384,1280]{1,0:T(8,128)(2,1)} %get-tuple-element.18.refs_1_, f32[2,8,1280]{2,1,0:T(8,128)} %pad.14.refs_2_, s32[2,3]{1,0:T(2,128)} %bitcast.31, ...), custom_call_target="tpu_custom_call" | custom-call | tf_op jit(solution)/shard_map/both_layers/pallas_call | solution.py:383
  287.5 0.9 slice.13
  288.4 0.1 reshape.47
  288.5 0.1 copy.12
  288.5 0.1 reshape.48
  288.7 0.7 copy.13
  289.3 174.1 %shard_map.93 = (f32[480,1280]{1,0:T(8,128)}, f32[8,128]{1,0:T(8,128)}, bf16[2,384,1280]{2,1,0:T(8,128)(2,1)}) custom-call(bf16[2,16,480,1280]{3,2,1,0:T(8,128)(2,1)} %bitcast.22, f32[32,8,128]{2,1,0:T(8,128)} %bitcast.28, bf16[384,1280]{1,0:T(8,128)(2,1)} %get-tuple-element.23.dx_ref, bf16[384,1280]{1,0:T(8,128)(2,1)} %get-tuple-element.24.y_ref, ...), custom_call_target="tpu_custom_call" | custom-call | tf_op jit(solution)/shard_map/pallas_call | solution.py:620
  463.5 0.0 copy-start
  463.5 1.5 fusion.5
  464.9 2.9 copy.16
  467.9 0.0 copy-done
  467.9 1.4 copy.17
  (3 shorter events, 0.0 us)
Async XLA Ops:
  463.5 4.4 copy-start
